TPU v7x, 32 devices: a whole 2x2x4 slice. The times are simulated.
32 devices in a mesh: dp: 2 (over core), seq: 2 (over x), vocab: 8 (over z, y).
Axes of the slice: x: 2, y: 2, z: 4, core: 2. Of those that a mesh axis runs over, the one named last changes fastest.
Arguments:
- hidden_states: bfloat16 [6, 256, 4096], P('dp', 'seq', 'vocab'), may hold values from -6 to 6
- head_weight: bfloat16 [4096, 32000], P('seq', 'vocab'), may hold values from -0.09375 to 0.09375
- owner_pos: int32 [6, 32000], P('dp', 'vocab'), may hold values from 0 to 255
- token_ids: int32 [6, 256], P('dp', 'seq'), may hold values from 0 to 31999, as said below
- teacher_margin: float32 [2], P('dp'), may hold values from -150 to 150
Outputs:
- grad_head: float32 [4096, 32000], P('seq', 'vocab')
- grad_hidden: bfloat16 [6, 256, 4096], P('dp', 'seq', 'vocab')
Inputs may be any that keep to these rules, and one draw needn't show every extreme that they name: `owner_pos`: owner positions may fall on padding tokens, which then pool nothing. `token_ids`: 0 marks padding, which fills a tail of one or more positions of every document; a document's first token is 31999.
All inputs are finite; a program needn't handle non-finite values.
Results may differ from a plain program's by a relative error of at most 0.017.
Values may be sent and summed in bfloat16 or wider, within the bound.
No kernel may reach another device: no remote copies, remote signals or barrier semaphores. Data moves between devices by JAX's collectives and lax.ppermute only.
A program may use at most 256 MiB of HBM per device.

v0:
```python
import functools

import jax
import jax.numpy as jnp
from jax import lax
from jax.experimental import pallas as pl
from jax.experimental.pallas import tpu as pltpu
from jax.sharding import PartitionSpec as P

LANES = 128
VMEM_BYTES = 48 * 1024 * 1024


def shift_perm(count, shift):
    return [(i, (i + shift) % count) for i in range(count)]


def waiting(kernel, count):
    return lambda *refs: kernel(refs[0], *refs[1 + count:])


def divisor(terms, limit):
    fits = [b for b in range(16, limit + 1, 16) if terms % b == 0]
    return fits[-1] if fits else terms


def slice_kernel(index_ref, states_ref, out_ref):
    out_ref[...] = states_ref[...]


def pick_kernel(slots, near, outer, index_ref, *refs):
    held = refs[:outer]
    gathered_ref = refs[outer]
    sends = refs[outer + 1:]
    block_z, seq = index_ref[2], index_ref[3]
    for s in range(slots):
        target = gathered_ref.at[0] if s == 0 else sends[s - 1]
        half = lax.rem(seq + slots - s, slots)
        for n in range(near):
            back = lax.rem(block_z + outer - (half * near + n), outer)
            for b in range(outer):

                @pl.when(back == b)
                def _():
                    target[n] = held[b][...]


def logits_kernel(docs, inner, strips, *refs):
    index_ref = refs[0]
    pieces = refs[1:1 + inner]
    heads = refs[1 + inner:1 + inner + strips]
    places_ref = refs[1 + inner + strips]
    logits_ref, rows_ref = refs[-2:]
    slots, near, _, part, width = pieces[0].shape
    length = slots * part

    @pl.when(pl.program_id(0) == 0)
    def _():
        for q in range(inner):
            lane_y = lax.rem(index_ref[0] + q, inner)
            for n in range(near):
                lane = pl.multiple_of((n * inner + lane_y) * width, width)
                for k in range(docs):
                    for s in range(slots):
                        rows_ref[pl.ds(k * length + s * part, part), pl.ds(lane, width)] = pieces[q][s, n, k]

    head = jnp.concatenate([ref[...] for ref in heads], axis=1)
    dense = lax.dot_general(
        rows_ref[...], head, (((1,), (1,)), ((), ())), preferred_element_type=jnp.float32
    )
    token = lax.broadcasted_iota(jnp.int32, (length, head.shape[0]), 0)
    for k in range(docs):
        picked = jnp.where(token == places_ref[pl.ds(k, 1), :], dense[k * length:(k + 1) * length], 0.0)
        logits_ref[pl.ds(k, 1), :] = jnp.sum(picked, axis=0, keepdims=True)


def hidden_kernel(docs, inner, strips, shape, *refs):
    index_ref = refs[0]
    heads = refs[1:1 + strips]
    places_ref, grads_ref = refs[1 + strips:3 + strips]
    outs = refs[3 + strips:3 + strips + inner]
    spread_ref, total_ref = refs[-2:]
    slots, near, _, part, width = shape
    length = slots * part
    step = pl.program_id(0)
    head = jnp.concatenate([ref[...] for ref in heads], axis=1)
    token = lax.broadcasted_iota(jnp.int32, (length, head.shape[0]), 0)
    for k in range(docs):
        spread = jnp.where(token == places_ref[pl.ds(k, 1), :], grads_ref[pl.ds(k, 1), :], 0.0)
        spread_ref[pl.ds(k * length, length), :] = spread.astype(jnp.bfloat16)
    term = jnp.dot(spread_ref[...], head, preferred_element_type=jnp.float32)

    @pl.when(step == 0)
    def _():
        total_ref[...] = term

    @pl.when(step > 0)
    def _():
        total_ref[...] += term

    @pl.when(step == pl.num_programs(0) - 1)
    def _():
        for q in range(inner):
            lane_y = lax.rem(index_ref[0] + q, inner)
            for n in range(near):
                lane = pl.multiple_of((n * inner + lane_y) * width, width)
                for k in range(docs):
                    for s in range(slots):
                        piece = total_ref[pl.ds(k * length + s * part, part), pl.ds(lane, width)]
                        outs[q][s, n, k] = piece.astype(jnp.bfloat16)


def combine_kernel(count, inner, slots, index_ref, *refs):
    outs = refs[count * inner:]
    for i in range(count):
        parts = refs[i * inner:(i + 1) * inner]
        for s in range(slots):
            total = parts[0][s].astype(jnp.float32)
            for other in parts[1:]:
                total = total + other[s].astype(jnp.float32)
            outs[s][i] = total.astype(jnp.bfloat16)


def sort_kernel(slots, near, outer, index_ref, *refs):
    mine, outs = refs[:slots], refs[slots:]
    block_z, seq = index_ref[2], index_ref[3]
    for ahead in range(outer):
        z = lax.rem(block_z + ahead, outer)
        slot = lax.rem(seq + slots - lax.div(z, near), slots)
        for s in range(slots):

            @pl.when(slot == s)
            def _():
                outs[ahead][...] = mine[s][:, lax.rem(z, near)]


def finish_kernel(counts, outer, index_ref, margin_ref, *refs):
    out_ref = refs[-1]
    docs = out_ref.shape[0]
    width = refs[0].shape[-1]
    c = 0
    for group, count in enumerate(counts):
        arrived = refs[group * outer:(group + 1) * outer]
        for i in range(count):
            for k in range(docs):
                total = arrived[0][i, k].astype(jnp.float32)
                for other in arrived[1:]:
                    total = total + other[i, k].astype(jnp.float32)
                out_ref[k, :, c * width:(c + 1) * width] = (total * margin_ref[k // 3]).astype(jnp.bfloat16)
            c += 1


def head_kernel(groups, docs, *refs):
    index_ref, margin_ref = refs[:2]
    rows = refs[2:2 + groups]
    places_ref, grads_ref = refs[2 + groups:4 + groups]
    out_ref, token_ref, spread_ref = refs[-3:]
    chunks, tokens, width = rows[0].shape
    length = tokens // docs

    @pl.when(pl.program_id(1) == 0)
    def _():
        token_ref[...] = jnp.zeros_like(token_ref)
        token = lax.broadcasted_iota(jnp.int32, (out_ref.shape[0], length), 1)
        for k in range(groups * docs):
            grads = grads_ref[:, k:k + 1] * margin_ref[k // 3]
            spread = jnp.where(token == places_ref[:, k:k + 1], grads, 0.0)
            spread_ref[:, k * length:(k + 1) * length] = spread.astype(jnp.bfloat16)

    for first in range(groups):

        @pl.when(index_ref[1] == first)
        def _():
            total = None
            for g in range(groups):
                ref = rows[(g - first) % groups]
                features = jnp.concatenate([ref[c] for c in range(chunks)], axis=1)
                term = jnp.dot(
                    spread_ref[:, g * tokens:(g + 1) * tokens], features, preferred_element_type=jnp.float32
                )
                total = term if total is None else total + term
            out_ref[...] = total


def on_device(axes, hidden_states, head_weight, owner_pos, token_ids, teacher_margin):
    groups, slots, blocks = axes
    docs, part, block_width = hidden_states.shape
    depth, terms = head_weight.shape
    triples = teacher_margin.shape[0]
    inner = 2 if blocks % 2 == 0 else 1
    outer = blocks // inner
    near = outer // slots
    chunks = max(1, block_width // LANES)
    width = block_width // chunks
    length = slots * part
    tokens = docs * length
    columns = divisor(terms, 2048)
    steps = terms // columns
    strips = near * inner

    group = lax.axis_index("dp")
    seq = lax.axis_index("seq")
    block = lax.axis_index("vocab")
    block_y = lax.rem(block, inner)
    block_z = lax.div(block, inner)
    index = jnp.stack([block_y, group, block_z, seq]).astype(jnp.int32)

    def across_y(value, shift):
        perm = [(z * inner + y, z * inner + (y + shift) % inner) for z in range(outer) for y in range(inner)]
        return lax.ppermute(value, "vocab", perm)

    def across_z(value, shift):
        perm = [(z * inner + y, (z + shift) % outer * inner + y) for z in range(outer) for y in range(inner)]
        return lax.ppermute(value, "vocab", perm)

    def other_groups(value):
        return [value] + [lax.ppermute(value, "dp", shift_perm(groups, -g)) for g in range(1, groups)]

    def in_group_order(values):
        doubled = jnp.stack(values + values)
        return lax.dynamic_slice_in_dim(doubled, lax.rem(groups - group, groups), groups, axis=0)

    def by_term(value):
        return value.transpose(1, 3, 0, 2).reshape(terms, groups * docs)

    def blocked(value):
        return value.reshape(docs, steps, columns).transpose(1, 0, 2)

    head_rows = head_weight.T
    strip_specs = lambda c: [
        pl.BlockSpec((columns, width), functools.partial(lambda lane, v: (v, lane), strip * chunks + c))
        for strip in range(strips)
    ]
    row_spec = pl.BlockSpec((pl.squeezed, docs, columns), lambda v: (v, 0, 0))
    piece_shape = (slots, near, docs, part, width)
    piece_spec = pl.BlockSpec(piece_shape, lambda v: (0, 0, 0, 0, 0))
    index_spec = pl.BlockSpec(memory_space=pltpu.SMEM)
    vmem_spec = pl.BlockSpec(memory_space=pltpu.VMEM)
    any_spec = pl.BlockSpec(memory_space=pl.ANY)
    params = pltpu.CompilerParams(vmem_limit_bytes=VMEM_BYTES)

    def cost(flops, transferred):
        return pl.CostEstimate(flops=int(flops), bytes_accessed=int(transferred), transcendentals=0)

    owner_blocks = blocked(owner_pos)
    places = lax.rem(owner_blocks + (length - seq * part), length)
    own_lengths = jnp.sum((token_ids != 0).astype(jnp.int32), axis=1, keepdims=True)
    lengths = own_lengths
    for s in range(1, slots):
        lengths = lengths + lax.ppermute(own_lengths, "seq", shift_perm(slots, s))
    validity = (owner_blocks < lengths[None]).astype(jnp.float32)
    places_all = by_term(in_group_order(other_groups(places)))

    def run(kernel, name, operands, specs, shapes, out_specs=None, waits=(), flops=0, aliases={}, scratch=(), grid=()):
        waits = [value for value in waits if value is not None]
        return pl.pallas_call(
            waiting(kernel, len(waits)),
            grid=grid,
            in_specs=[index_spec] + [any_spec] * len(waits) + specs,
            out_specs=out_specs or [vmem_spec] * len(shapes),
            out_shape=shapes,
            scratch_shapes=list(scratch),
            input_output_aliases={1 + len(waits) + i: o for i, o in aliases.items()},
            compiler_params=params,
            cost_estimate=cost(flops, flops // 64),
            name=name,
        )(index, *waits, *operands)

    bf16 = lambda *shape: jax.ShapeDtypeStruct(shape, jnp.bfloat16)
    moved_shape = bf16(near, docs, part, width)
    gathered_chunks = []
    others = []
    sent = None
    for c in range(chunks):
        (own,) = run(
            slice_kernel,
            "feature_chunk",
            [hidden_states],
            [pl.BlockSpec((docs, part, width), functools.partial(lambda c, i: (0, 0, c), c))],
            [bf16(docs, part, width)],
            out_specs=[pl.BlockSpec((docs, part, width), lambda i: (0, 0, 0))],
            waits=[sent],
            grid=(1,),
        )
        held = [own] + [across_z(own, back) for back in range(1, outer)]
        gathered, *sends = run(
            functools.partial(pick_kernel, slots, near, outer),
            "pick_halves",
            held,
            [vmem_spec] * outer,
            [bf16(*piece_shape)] + [moved_shape] * (slots - 1),
            waits=[gathered_chunks[c - 1] if c > 0 else None, others[c - 2] if c > 1 else None],
        )
        sent = gathered
        if slots > 1:
            arrived = [lax.ppermute(sends[s - 1], "seq", shift_perm(slots, -s)) for s in range(1, slots)]
            gathered = jnp.concatenate([gathered[:1]] + [value[None] for value in arrived])
        gathered_chunks.append(gathered)
        others.append(across_y(gathered, -1) if inner > 1 else None)

    logit_parts = []
    features = None
    for c in range(chunks):
        pieces = [gathered_chunks[c], others[c]][:inner]
        previous = [] if features is None else [features]
        chunk_logits, features = run(
            functools.partial(logits_kernel, docs, inner, strips),
            "pooled_logits",
            [*pieces, *[head_rows] * strips, places, *previous],
            [piece_spec] * inner + strip_specs(c) + [row_spec] + [any_spec] * len(previous),
            [
                jax.ShapeDtypeStruct((steps, docs, columns), jnp.float32),
                bf16(chunks, tokens, strips * width),
            ],
            out_specs=[
                row_spec,
                pl.BlockSpec(
                    (pl.squeezed, tokens, strips * width), functools.partial(lambda c, v: (c, 0, 0), c)
                ),
            ],
            waits=[None if previous else places_all],
            flops=2 * tokens * strips * width * terms,
            aliases={inner + strips + 1: 1} if previous else {},
            grid=(steps,),
        )
        logit_parts.append(chunk_logits)

    logit_part = functools.reduce(jnp.add, logit_parts)
    logits = logit_part
    for s in range(1, slots):
        logits = logits + lax.ppermute(logit_part, "seq", shift_perm(slots, s))
    softened = jax.nn.softplus(logits)
    pooled = validity * jnp.log1p(softened)
    slopes = validity * jax.nn.sigmoid(logits) / (1.0 + softened)
    view = pooled.reshape(steps, triples, 3, columns)
    query, positive, negative = view[:, :, 0], view[:, :, 1], view[:, :, 2]
    unscaled = jnp.stack([positive - negative, query, -query], axis=2).reshape(logits.shape) * slopes
    unscaled = unscaled.astype(jnp.bfloat16)
    scores = jnp.sum(query * positive, axis=(0, 2)) - jnp.sum(query * negative, axis=(0, 2))
    if blocks & (blocks - 1) == 0:
        distance = 1
        while distance < blocks:
            scores = scores + lax.ppermute(scores, "vocab", [(i, i ^ distance) for i in range(blocks)])
            distance *= 2
    else:
        scores = lax.psum(scores, "vocab")
    margin = (scores - teacher_margin) / (triples * groups)
    margin_all = in_group_order(other_groups(margin)).reshape(groups * triples)
    grads_all = by_term(in_group_order(other_groups(unscaled)).astype(jnp.float32))
    unscaled = unscaled.astype(jnp.float32)
    features_all = other_groups(features)

    head_terms = divisor(terms, 400)
    ranges = terms // head_terms
    next_range = 0
    grad_head = token = None

    def run_head(count, *waits):
        nonlocal grad_head, token, next_range
        if count == 0:
            return
        previous = [] if grad_head is None else [grad_head]
        start = next_range
        term_spec = pl.BlockSpec((head_terms, groups * docs), lambda r, d: (start + r, 0))
        grad_head, token = run(
            functools.partial(head_kernel, groups, docs),
            "head_terms",
            [margin_all, *features_all, places_all, grads_all, *previous],
            [index_spec]
            + [pl.BlockSpec((chunks, tokens, width), lambda r, d: (0, 0, d))] * groups
            + [term_spec] * 2
            + [any_spec] * len(previous),
            [jax.ShapeDtypeStruct((terms, depth), jnp.float32), jax.ShapeDtypeStruct((8, LANES), jnp.float32)],
            out_specs=[
                pl.BlockSpec((head_terms, block_width), lambda r, d: (start + r, d)),
                pl.BlockSpec((8, LANES), lambda r, d: (0, 0)),
            ],
            waits=waits,
            flops=count * 2 * groups * tokens * head_terms * depth // 4,
            aliases={3 + groups: 0} if previous else {},
            scratch=[pltpu.VMEM((head_terms, groups * tokens), jnp.bfloat16)],
            grid=(count, strips),
        )
        next_range += count

    parts = []
    for c in range(chunks):
        sums = run(
            functools.partial(hidden_kernel, docs, inner, strips, piece_shape),
            "hidden_terms",
            [head_rows] * strips + [places, unscaled],
            strip_specs(c) + [row_spec, row_spec],
            [bf16(*piece_shape)] * inner,
            out_specs=[piece_spec] * inner,
            waits=[parts[c - 3][-1] if c > 2 else None],
            flops=2 * tokens * strips * width * terms // 4,
            scratch=[
                pltpu.VMEM((tokens, columns), jnp.bfloat16),
                pltpu.VMEM((tokens, strips * width), jnp.float32),
            ],
            grid=(steps,),
        )
        parts.append([sums[0]] + [across_y(sums[q], q) for q in range(1, inner)])

    half = -(-chunks // 2)
    pairs = [pair for pair in (parts[:half], parts[half:]) if pair]
    share = ranges // 10
    mine_all = []
    arrived_all = []

    def add_blocks(pair, *waits):
        mine = run(
            functools.partial(combine_kernel, len(pair), inner, slots),
            "add_blocks",
            [value for each in pair for value in each],
            [vmem_spec] * (len(pair) * inner),
            [bf16(len(pair), near, docs, part, width)] * slots,
            waits=waits,
        )
        mine_all.append([mine[0]] + [lax.ppermute(mine[s], "seq", shift_perm(slots, s)) for s in range(1, slots)])

    def sort_pieces(mine, *waits):
        pieces = run(
            functools.partial(sort_kernel, slots, near, outer),
            "sort_pieces",
            mine,
            [vmem_spec] * slots,
            [bf16(mine[0].shape[0], docs, part, width)] * outer,
            waits=waits,
        )
        arrived_all.append([pieces[0]] + [across_z(pieces[ahead], ahead) for ahead in range(1, outer)])

    add_blocks(pairs[0])
    run_head(2 * share, mine_all[0][0], parts[-1][0])
    sort_pieces(mine_all[0], token)
    if len(pairs) > 1:
        add_blocks(pairs[1], arrived_all[0][0])
        run_head(2 * share, arrived_all[0][0], mine_all[1][0])
        sort_pieces(mine_all[1], token)
        run_head(share, arrived_all[1][0])
    run_head(ranges - next_range, *arrived_all[0][1:])
    (grad_hidden,) = run(
        functools.partial(finish_kernel, [len(pair) for pair in pairs], outer),
        "scale_hidden",
        [margin] + [value for arrived in arrived_all for value in arrived],
        [index_spec] + [vmem_spec] * (len(pairs) * outer),
        [bf16(docs, part, block_width)],
        waits=[token],
    )
    return (grad_head.T, grad_hidden)


def solution(mesh):
    axes = (mesh.shape["dp"], mesh.shape["seq"], mesh.shape["vocab"])
    return jax.shard_map(
        functools.partial(on_device, axes),
        mesh=mesh,
        in_specs=(
            P("dp", "seq", "vocab"),
            P("seq", "vocab"),
            P("dp", "vocab"),
            P("dp", "seq"),
            P("dp"),
        ),
        out_specs=(P("seq", "vocab"), P("dp", "seq", "vocab")),
        check_vma=False,
    )
```

profile of v0, /device:TPU:0, one launch (start us, length us, event | category | flops | bytes accessed | tf_op | source)
XLA Modules:
  0.0 247.0 jit_solution(6530644779055702254)
XLA Ops:
  0.7 1.0 copy-done.6
  2.3 5.1 %collective-permute-start.4 = (bf16[3,128,128]{2,1,0:T(8,128)(2,1)S(1)}, bf16[3,128,128]{2,1,0:T(8,128)(2,1)S(1)}, u32[]{:S(2)}, u32[]{:S(2)}) collective-permute-start(bf16[3,128,128]{2,1,0:T(8,128)(2,1)S(1)} %feature_chunk.4.refs_1_), channel_id=1, source_target_pairs={{0,6},{1,7},{2,0},{3,1},{4,2},{5,3},{6,4},{7,5},{8,14},{9,15},{10,... | collective-permute-start | bytes 294920 | tf_op jit(solution)/shard_map/ppermute | solution.py:214
  7.4 1.0 collective-permute-start.2
  8.4 2.2 collective-permute-done.4.refs_4_
  10.6 5.5 %collective-permute-done.3.refs_3_ = bf16[3,128,128]{2,1,0:T(8,128)(2,1)S(1)} collective-permute-done((bf16[3,128,128]{2,1,0:T(8,128)(2,1)S(1)}, bf16[3,128,128]{2,1,0:T(8,128)(2,1)S(1)}, u32[]{:S(2)}, u32[]{:S(2)}) %collective-permute-start.3) | collective-permute-done | bytes 98336 | tf_op jit(solution)/shard_map/ppermute | solution.py:214
  16.8 1.6 collective-permute-start.5
  18.3 0.9 reshape.78
  19.3 1.0 copy-done.7
  20.9 2.0 collective-permute-start.9
  23.3 1.9 collective-permute-start.7
  25.3 1.6 collective-permute-start.6
  26.9 4.6 %collective-permute-done.8.refs_4_ = bf16[3,128,128]{2,1,0:T(8,128)(2,1)S(1)} collective-permute-done((bf16[3,128,128]{2,1,0:T(8,128)(2,1)S(1)}, bf16[3,128,128]{2,1,0:T(8,128)(2,1)S(1)}, u32[]{:S(2)}, u32[]{:S(2)}) %collective-permute-start.8) | collective-permute-done | bytes 98336 | tf_op jit(solution)/shard_map/ppermute | solution.py:214
  33.4 1.6 collective-permute-start.14
  35.2 2.6 %collective-permute-done.10 = bf16[2,3,128,128]{3,2,1,0:T(8,128)(2,1)S(1)} collective-permute-done((bf16[2,3,128,128]{3,2,1,0:T(8,128)(2,1)S(1)}, bf16[2,3,128,128]{3,2,1,0:T(8,128)(2,1)S(1)}, u32[]{:S(2)}, u32[]{:S(2)}) %collective-permute-start.10) | collective-permute-done | bytes 196640 | tf_op jit(solution)/shard_map/ppermute | solution.py:296
  38.7 1.5 collective-permute-start.11
  40.2 4.8 %collective-permute-done.13.refs_5_ = bf16[3,128,128]{2,1,0:T(8,128)(2,1)S(1)} collective-permute-done((bf16[3,128,128]{2,1,0:T(8,128)(2,1)S(1)}, bf16[3,128,128]{2,1,0:T(8,128)(2,1)S(1)}, u32[]{:S(2)}, u32[]{:S(2)}) %collective-permute-start.13) | collective-permute-done | bytes 98336 | tf_op jit(solution)/shard_map/ppermute | solution.py:214
  45.7 1.6 collective-permute-start.15
  47.6 2.0 copy.18.refs_1_.refs_6_.refs_5_.refs_7_
  50.2 1.3 collective-permute-start.19
  51.5 1.2 collective-permute-start.18
  52.7 1.9 collective-permute-start.17
  55.3 6.4 %collective-permute-done.18.refs_5_ = bf16[3,128,128]{2,1,0:T(8,128)(2,1)S(1)} collective-permute-done((bf16[3,128,128]{2,1,0:T(8,128)(2,1)S(1)}, bf16[3,128,128]{2,1,0:T(8,128)(2,1)S(1)}, u32[]{:S(2)}, u32[]{:S(2)}) %collective-permute-start.18) | collective-permute-done | bytes 98336 | tf_op jit(solution)/shard_map/ppermute | solution.py:214
  61.7 0.8 pick_halves.7
  63.2 1.0 copy-done.14
  64.2 5.5 %pooled_logits.4 = (f32[2,3,2000]{2,1,0:T(4,128)S(1)}, bf16[4,768,512]{2,1,0:T(8,128)(2,1)S(1)}) custom-call(s32[4]{0:T(128)S(1)} %pad_add_fusion.refs_0_, s32[4000,6]{1,0:T(8,128)S(1)} %copy-done.1, bf16[2,2,3,128,128]{4,3,2,1,0:T(8,128)(2,1)S(1)} %copy-done.10, bf16[2,2,3,128,128]{4,3,2,1,0:T(8,128)(2,1)S(1)} %copy-done.14, bf16[4000,2048]{1,0:T(8,128)(2,1)} %bitcast.54, ...), custom_call_target="tpu_custom_call" | custom-call | flops 3145728000 | bytes 49152000 | tf_op jit(solution)/shard_map/pooled_logits/pallas_call | solution.py:256
  69.7 1.6 collective-permute-start.16
  72.0 5.5 %pooled_logits.5 = (f32[2,3,2000]{2,1,0:T(4,128)S(1)}, bf16[4,768,512]{2,1,0:T(8,128)(2,1)S(1)}) custom-call(s32[4]{0:T(128)S(1)} %pad_add_fusion.refs_0_, bf16[2,2,3,128,128]{4,3,2,1,0:T(8,128)(2,1)S(1)} %copy-done.12, bf16[2,2,3,128,128]{4,3,2,1,0:T(8,128)(2,1)S(1)} %copy-done.16, bf16[4000,2048]{1,0:T(8,128)(2,1)} %bitcast.58, ...), custom_call_target="tpu_custom_call", output_to_operand_aliasing={{1}: (8, {})} | custom-call | flops 3145728000 | bytes 49152000 | tf_op jit(solution)/shard_map/pooled_logits/pallas_call | solution.py:256
  77.4 4.4 %collective-permute-done.16.refs_2_ = bf16[2,2,3,128,128]{4,3,2,1,0:T(8,128)(2,1)S(1)} collective-permute-done((bf16[2,2,3,128,128]{4,3,2,1,0:T(8,128)(2,1)S(1)}, bf16[2,2,3,128,128]{4,3,2,1,0:T(8,128)(2,1)S(1)}, u32[]{:S(2)}, u32[]{:S(2)}) %collective-permute-start.16) | collective-permute-done | bytes 393248 | tf_op jit(solution)/shard_map/ppermute | solution.py:210
  81.8 5.5 %pooled_logits.6 = (f32[2,3,2000]{2,1,0:T(4,128)S(1)}, bf16[4,768,512]{2,1,0:T(8,128)(2,1)S(1)}) custom-call(s32[4]{0:T(128)S(1)} %pad_add_fusion.refs_0_, bf16[2,2,3,128,128]{4,3,2,1,0:T(8,128)(2,1)S(1)} %pad_maximum_fusion.2.refs_1_, bf16[2,2,3,128,128]{4,3,2,1,0:T(8,128)(2,1)S(1)} %collective-permute-done.16.refs_2_, ...), custom_call_target="tpu_custom_call", output_to_operand_aliasing={{1}: (8, {})} | custom-call | flops 3145728000 | bytes 49152000 | tf_op jit(solution)/shard_map/pooled_logits/pallas_call | solution.py:256
  87.3 0.8 collective-permute-done.21.refs_2_
  88.2 5.5 %pooled_logits.7 = (f32[2,3,2000]{2,1,0:T(4,128)S(1)}, bf16[4,768,512]{2,1,0:T(8,128)(2,1)S(1)}) custom-call(s32[4]{0:T(128)S(1)} %pad_add_fusion.refs_0_, bf16[2,2,3,128,128]{4,3,2,1,0:T(8,128)(2,1)S(1)} %pad_maximum_fusion.3.refs_1_, bf16[2,2,3,128,128]{4,3,2,1,0:T(8,128)(2,1)S(1)} %collective-permute-done.21.refs_2_, ...), custom_call_target="tpu_custom_call", output_to_operand_aliasing={{1}: (8, {})} | custom-call | flops 3145728000 | bytes 49152000 | tf_op jit(solution)/shard_map/pooled_logits/pallas_call | solution.py:256
  93.9 1.5 collective-permute-start
  96.1 1.4 collective-permute-done
  97.5 2.3 collective-permute-done.22
  100.7 0.8 fusion.15
  101.5 6.4 %hidden_terms.4 = (bf16[2,2,3,128,128]{4,3,2,1,0:T(8,128)(2,1)S(1)}, bf16[2,2,3,128,128]{4,3,2,1,0:T(8,128)(2,1)}) custom-call(s32[4]{0:T(128)S(1)} %pad_add_fusion.refs_0_, bf16[4000,2048]{1,0:T(8,128)(2,1)} %bitcast.70, bf16[4000,2048]{1,0:T(8,128)(2,1)} %bitcast.71, bf16[4000,2048]{1,0:T(8,128)(2,1)} %bitcast.72, bf16[4000,2048]{1,0:T(8,128)(2,1)} %bitcast.73, ...), custom_call_target="tpu_custom_call" | custom-call | flops 786432000 | bytes 12288000 | tf_op jit(solution)/shard_map/hidden_terms/pallas_call | solution.py:256
  108.6 1.5 collective-permute-start.23
  110.1 6.4 %hidden_terms.5 = (bf16[2,2,3,128,128]{4,3,2,1,0:T(8,128)(2,1)S(1)}, bf16[2,2,3,128,128]{4,3,2,1,0:T(8,128)(2,1)}) custom-call(s32[4]{0:T(128)S(1)} %pad_add_fusion.refs_0_, bf16[4000,2048]{1,0:T(8,128)(2,1)} %bitcast.74, bf16[4000,2048]{1,0:T(8,128)(2,1)} %bitcast.75, bf16[4000,2048]{1,0:T(8,128)(2,1)} %bitcast.76, bf16[4000,2048]{1,0:T(8,128)(2,1)} %bitcast.77, ...), custom_call_target="tpu_custom_call" | custom-call | flops 786432000 | bytes 12288000 | tf_op jit(solution)/shard_map/hidden_terms/pallas_call | solution.py:256
  119.7 6.7 %collective-permute-start.25 = (f32[1]{0:T(128)}, f32[1]{0:T(128)}, u32[]{:S(2)}, u32[]{:S(2)}) collective-permute-start(f32[1]{0:T(128)} %bitcast.18), channel_id=1, source_target_pairs={{0,1},{1,0},{2,3},{3,2},{4,5},{5,4},{6,7},{7,6},{8,9},{9,8},{10,11... | collective-permute-start | bytes 20 | tf_op jit(solution)/shard_map/ppermute | solution.py:343
  126.5 6.4 %hidden_terms.7 = (bf16[2,2,3,128,128]{4,3,2,1,0:T(8,128)(2,1)S(1)}, bf16[2,2,3,128,128]{4,3,2,1,0:T(8,128)(2,1)}) custom-call(s32[4]{0:T(128)S(1)} %pad_add_fusion.refs_0_, bf16[4000,2048]{1,0:T(8,128)(2,1)} %bitcast.78, bf16[4000,2048]{1,0:T(8,128)(2,1)} %bitcast.79, bf16[4000,2048]{1,0:T(8,128)(2,1)} %bitcast.80, bf16[4000,2048]{1,0:T(8,128)(2,1)} %bitcast.81, ...), custom_call_target="tpu_custom_call" | custom-call | flops 786432000 | bytes 12288000 | tf_op jit(solution)/shard_map/hidden_terms/pallas_call | solution.py:256
  134.2 1.9 collective-permute-start.26
  136.2 1.6 collective-permute-done.26
  138.4 3.8 %collective-permute-start.27 = (f32[1]{0:T(128)}, f32[1]{0:T(128)}, u32[]{:S(2)}, u32[]{:S(2)}) collective-permute-start(f32[1]{0:T(128)} %add.61), channel_id=1, source_target_pairs={{0,4},{1,5},{2,6},{3,7},{4,0},{5,1},{6,2},{7,3},{8,12},{9,13},{10,... | collective-permute-start | bytes 20 | tf_op jit(solution)/shard_map/ppermute | solution.py:343
  143.5 0.9 collective-permute-start.28
  145.9 6.5 %hidden_terms.6 = (bf16[2,2,3,128,128]{4,3,2,1,0:T(8,128)(2,1)S(1)}, bf16[2,2,3,128,128]{4,3,2,1,0:T(8,128)(2,1)}) custom-call(s32[4]{0:T(128)S(1)} %pad_add_fusion.refs_0_, bf16[2,2,3,128,128]{4,3,2,1,0:T(8,128)(2,1)} %collective-permute-done.23.refs_2_.refs_1_, bf16[4000,2048]{1,0:T(8,128)(2,1)} %bitcast.82, bf16[4000,2048]{1,0:T(8,128)(2,1)} %bitcast.83, ...), custom_call_target="tpu_custom_call" | custom-call | flops 786432000 | bytes 12288000 | tf_op jit(solution)/shard_map/hidden_terms/pallas_call | solution.py:256
  153.1 1.5 collective-permute-start.36
  154.6 2.0 add_blocks.2
  157.2 1.0 convert_bitcast_fusion
  158.9 1.7 reshape.86
  160.6 2.8 %copy.21.refs_7_.refs_6_.refs_8_ = f32[4000,6]{1,0:T(8,128)} copy(f32[4000,6]{0,1:T(8,128)} %reshape.86) | data formatting | bytes 192000 | tf_op jit(solution)/shard_map/reshape | solution.py:224
  163.5 1.6 copy-done.2
  165.1 1.6 copy-done.4
  166.6 1.0 copy-done.18
  167.6 13.1 %head_terms.4 = (f32[4000,2048]{1,0:T(8,128)}, f32[8,128]{1,0:T(8,128)S(1)}) custom-call(s32[4]{0:T(128)S(1)} %pad_add_fusion.refs_0_, bf16[2,2,3,128,128]{4,3,2,1,0:T(8,128)(2,1)S(1)} %get-tuple-element.64.refs_1_.refs_2_, bf16[2,2,3,128,128]{4,3,2,1,0:T(8,128)(2,1)S(1)} %copy-done.18, f32[2]{0:T(128)S(1)} %fusion.13.refs_3_.refs_2_.refs_4_, ...), custom_call_target="tpu_custom_call" | custom-call | flops 1258291200 | bytes 19660800 | tf_op jit(solution)/shard_map/head_terms/pallas_call | solution.py:256
  180.8 1.3 sort_pieces.2
  182.1 1.3 add_blocks.3
  183.4 1.5 collective-permute-start.37
  185.6 1.9 collective-permute-start.33
  187.5 2.9 %collective-permute-start.34 = (bf16[2,3,128,128]{3,2,1,0:T(8,128)(2,1)S(1)}, bf16[2,3,128,128]{3,2,1,0:T(8,128)(2,1)S(1)}, u32[]{:S(2)}, u32[]{:S(2)}) collective-permute-start(bf16[2,3,128,128]{3,2,1,0:T(8,128)(2,1)S(1)} %get-tuple-element.71), channel_id=1, source_target_pairs={{0,6},{1,7},{2,0},{3,1},{4,2},{5,3},{6,4},{7,5},{8,14},{9,15},{10,... | collective-permute-start | bytes 589832 | tf_op jit(solution)/shard_map/ppermute | solution.py:214
  190.4 13.0 %head_terms.5 = (f32[4000,2048]{1,0:T(8,128)}, f32[8,128]{1,0:T(8,128)S(1)}) custom-call(s32[4]{0:T(128)S(1)} %pad_add_fusion.refs_0_, bf16[2,3,128,128]{3,2,1,0:T(8,128)(2,1)S(1)} %get-tuple-element.72.refs_1_.refs_3_, bf16[2,2,3,128,128]{4,3,2,1,0:T(8,128)(2,1)S(1)} %get-tuple-element.76.refs_2_, ...), custom_call_target="tpu_custom_call", output_to_operand_aliasing={{0}: (8, {})} | custom-call | flops 1258291200 | bytes 19660800 | tf_op jit(solution)/shard_map/head_terms/pallas_call | solution.py:256
  204.7 7.2 %head_terms.6 = (f32[4000,2048]{1,0:T(8,128)}, f32[8,128]{1,0:T(8,128)}) custom-call(s32[4]{0:T(128)S(1)} %pad_add_fusion.refs_0_, bf16[2,3,128,128]{3,2,1,0:T(8,128)(2,1)S(1)} %get-tuple-element.80.refs_1_.refs_7_, f32[2]{0:T(128)S(1)} %fusion.13.refs_3_.refs_2_.refs_4_, bf16[4,768,512]{2,1,0:T(8,128)(2,1)} %copy-done, ...), custom_call_target="tpu_custom_call", output_to_operand_aliasing={{0}: (7, {})} | custom-call | flops 629145600 | bytes 9830400 | tf_op jit(solution)/shard_map/head_terms/pallas_call | solution.py:256
  211.9 3.3 %collective-permute-start.40 = (bf16[2,3,128,128]{3,2,1,0:T(8,128)(2,1)S(1)}, bf16[2,3,128,128]{3,2,1,0:T(8,128)(2,1)S(1)}, u32[]{:S(2)}, u32[]{:S(2)}) collective-permute-start(bf16[2,3,128,128]{3,2,1,0:T(8,128)(2,1)S(1)} %get-tuple-element.87), channel_id=1, source_target_pairs={{0,6},{1,7},{2,0},{3,1},{4,2},{5,3},{6,4},{7,5},{8,14},{9,15},{10,... | collective-permute-start | bytes 589832 | tf_op jit(solution)/shard_map/ppermute | solution.py:214
  215.2 30.2 %head_terms.7 = (f32[4000,2048]{1,0:T(8,128)}, f32[8,128]{1,0:T(8,128)S(1)}) custom-call(s32[4]{0:T(128)S(1)} %pad_add_fusion.refs_0_, bf16[2,3,128,128]{3,2,1,0:T(8,128)(2,1)S(1)} %collective-permute-done.32.refs_1_.refs_4_, bf16[2,3,128,128]{3,2,1,0:T(8,128)(2,1)S(1)} %collective-permute-done.33.refs_2_.refs_5_, ...), custom_call_target="tpu_custom_call", output_to_operand_aliasing={{0}: (9, {})} | custom-call | flops 3145728000 | bytes 49152000 | tf_op jit(solution)/shard_map/head_terms/pallas_call | solution.py:256
  245.4 1.5 scale_hidden.1
  (128 shorter events, 19.3 us)
Async XLA Ops:
  0.7 1.0 copy-start.6
  1.7 31.1 %copy-start.8 = (bf16[3,128,512]{2,1,0:T(8,128)(2,1)S(1)}, bf16[3,128,512]{2,1,0:T(8,128)(2,1)}, u32[]{:S(2)}) copy-start(bf16[3,128,512]{2,1,0:T(8,128)(2,1)} %refs_2_.5) | copy-start | bytes 1179652
  2.3 8.3 %collective-permute-start.4 = (bf16[3,128,128]{2,1,0:T(8,128)(2,1)S(1)}, bf16[3,128,128]{2,1,0:T(8,128)(2,1)S(1)}, u32[]{:S(2)}, u32[]{:S(2)}) collective-permute-start(bf16[3,128,128]{2,1,0:T(8,128)(2,1)S(1)} %feature_chunk.4.refs_1_), channel_id=1, source_target_pairs={{0,6},{1,7},{2,0},{3,1},{4,2},{5,3},{6,4},{7,5},{8,14},{9,15},{10,... | collective-permute-start | bytes 294920 | tf_op jit(solution)/shard_map/ppermute | solution.py:214
  7.4 8.7 %collective-permute-start.3 = (bf16[3,128,128]{2,1,0:T(8,128)(2,1)S(1)}, bf16[3,128,128]{2,1,0:T(8,128)(2,1)S(1)}, u32[]{:S(2)}, u32[]{:S(2)}) collective-permute-start(bf16[3,128,128]{2,1,0:T(8,128)(2,1)S(1)} %feature_chunk.4.refs_1_), channel_id=1, source_target_pairs={{0,4},{1,5},{2,6},{3,7},{4,0},{5,1},{6,2},{7,3},{8,12},{9,13},{10,... | collective-permute-start | bytes 294920 | tf_op jit(solution)/shard_map/ppermute | solution.py:214
  7.4 8.7 %collective-permute-start.2 = (bf16[3,128,128]{2,1,0:T(8,128)(2,1)S(1)}, bf16[3,128,128]{2,1,0:T(8,128)(2,1)S(1)}, u32[]{:S(2)}, u32[]{:S(2)}) collective-permute-start(bf16[3,128,128]{2,1,0:T(8,128)(2,1)S(1)} %feature_chunk.4.refs_1_), channel_id=1, source_target_pairs={{0,2},{1,3},{2,4},{3,5},{4,6},{5,7},{6,0},{7,1},{8,10},{9,11},{10,... | collective-permute-start | bytes 294920 | tf_op jit(solution)/shard_map/ppermute | solution.py:214
  16.8 8.5 %collective-permute-start.5 = (bf16[2,3,128,128]{3,2,1,0:T(8,128)(2,1)S(1)}, bf16[2,3,128,128]{3,2,1,0:T(8,128)(2,1)S(1)}, u32[]{:S(2)}, u32[]{:S(2)}) collective-permute-start(bf16[2,3,128,128]{3,2,1,0:T(8,128)(2,1)S(1)} %get-tuple-element.46), channel_id=1, source_target_pairs={{0,8},{8,0},{1,9},{9,1},{2,10},{10,2},{3,11},{11,3},{4,12},{12,4},... | collective-permute-start | bytes 589832 | tf_op jit(solution)/shard_map/ppermute | solution.py:296
  19.3 18.6 %copy-start.26 = (s32[3,2,2000]{2,1,0:T(2,128)}, s32[3,2,2000]{2,1,0:T(2,128)S(1)}, u32[]{:S(2)}) copy-start(s32[3,2,2000]{2,1,0:T(2,128)S(1)} %reshape.78) | copy-start | bytes 144004
  19.3 1.0 copy-start.7
  20.9 6.0 %collective-permute-start.9 = (bf16[3,128,128]{2,1,0:T(8,128)(2,1)S(1)}, bf16[3,128,128]{2,1,0:T(8,128)(2,1)S(1)}, u32[]{:S(2)}, u32[]{:S(2)}) collective-permute-start(bf16[3,128,128]{2,1,0:T(8,128)(2,1)S(1)} %feature_chunk.5.refs_2_), channel_id=1, source_target_pairs={{0,6},{1,7},{2,0},{3,1},{4,2},{5,3},{6,4},{7,5},{8,14},{9,15},{10,... | collective-permute-start | bytes 294920 | tf_op jit(solution)/shard_map/ppermute | solution.py:214
  22.9 8.6 %collective-permute-start.8 = (bf16[3,128,128]{2,1,0:T(8,128)(2,1)S(1)}, bf16[3,128,128]{2,1,0:T(8,128)(2,1)S(1)}, u32[]{:S(2)}, u32[]{:S(2)}) collective-permute-start(bf16[3,128,128]{2,1,0:T(8,128)(2,1)S(1)} %feature_chunk.5.refs_2_), channel_id=1, source_target_pairs={{0,4},{1,5},{2,6},{3,7},{4,0},{5,1},{6,2},{7,3},{8,12},{9,13},{10,... | collective-permute-start | bytes 294920 | tf_op jit(solution)/shard_map/ppermute | solution.py:214
  23.3 8.2 %collective-permute-start.7 = (bf16[3,128,128]{2,1,0:T(8,128)(2,1)S(1)}, bf16[3,128,128]{2,1,0:T(8,128)(2,1)S(1)}, u32[]{:S(2)}, u32[]{:S(2)}) collective-permute-start(bf16[3,128,128]{2,1,0:T(8,128)(2,1)S(1)} %feature_chunk.5.refs_2_), channel_id=1, source_target_pairs={{0,2},{1,3},{2,4},{3,5},{4,6},{5,7},{6,0},{7,1},{8,10},{9,11},{10,... | collective-permute-start | bytes 294920 | tf_op jit(solution)/shard_map/ppermute | solution.py:214
  25.3 24.3 %copy-start.9 = (bf16[2,2,3,128,128]{4,3,2,1,0:T(8,128)(2,1)}, bf16[2,2,3,128,128]{4,3,2,1,0:T(8,128)(2,1)S(1)}, u32[]{:S(2)}) copy-start(bf16[2,2,3,128,128]{4,3,2,1,0:T(8,128)(2,1)S(1)} %pad_maximum_fusion.refs_2_.refs_1_) | copy-start | bytes 1179652
  25.3 19.7 %collective-permute-start.6 = (bf16[2,2,3,128,128]{4,3,2,1,0:T(8,128)(2,1)S(1)}, bf16[2,2,3,128,128]{4,3,2,1,0:T(8,128)(2,1)S(1)}, u32[]{:S(2)}, u32[]{:S(2)}) collective-permute-start(bf16[2,2,3,128,128]{4,3,2,1,0:T(8,128)(2,1)S(1)} %pad_maximum_fusion.refs_2_.refs_1_), channel_id=1, source_target_pairs={{0,1},{1,0},{2,3},{3,2},{4,5},{5,4},{6,7},{7,6},{8,9},{9,8},{10,11... | collective-permute-start | bytes 1179656 | tf_op jit(solution)/shard_map/ppermute | solution.py:210
  32.1 5.7 %collective-permute-start.10 = (bf16[2,3,128,128]{3,2,1,0:T(8,128)(2,1)S(1)}, bf16[2,3,128,128]{3,2,1,0:T(8,128)(2,1)S(1)}, u32[]{:S(2)}, u32[]{:S(2)}) collective-permute-start(bf16[2,3,128,128]{3,2,1,0:T(8,128)(2,1)S(1)} %get-tuple-element.49), channel_id=1, source_target_pairs={{0,8},{8,0},{1,9},{9,1},{2,10},{10,2},{3,11},{11,3},{4,12},{12,4},... | collective-permute-start | bytes 589832 | tf_op jit(solution)/shard_map/ppermute | solution.py:296
  32.8 14.5 %collective-permute-start.1 = (s32[2,3,2000]{2,1,0:T(4,128)S(1)}, s32[2,3,2000]{2,1,0:T(4,128)S(1)}, u32[]{:S(2)}, u32[]{:S(2)}) collective-permute-start(s32[2,3,2000]{2,1,0:T(4,128)S(1)} %get-tuple-element.96.refs_8_.refs_7_.refs_5_.refs_6_), channel_id=1, source_target_pairs={{0,16},{16,0},{1,17},{17,1},{2,18},{18,2},{3,19},{19,3},{4,20},{20... | collective-permute-start | bytes 144008 | tf_op jit(solution)/shard_map/ppermute | solution.py:217
  33.4 5.2 %collective-permute-start.14 = (bf16[3,128,128]{2,1,0:T(8,128)(2,1)S(1)}, bf16[3,128,128]{2,1,0:T(8,128)(2,1)S(1)}, u32[]{:S(2)}, u32[]{:S(2)}) collective-permute-start(bf16[3,128,128]{2,1,0:T(8,128)(2,1)S(1)} %feature_chunk.6.refs_3_), channel_id=1, source_target_pairs={{0,6},{1,7},{2,0},{3,1},{4,2},{5,3},{6,4},{7,5},{8,14},{9,15},{10,... | collective-permute-start | bytes 294920 | tf_op jit(solution)/shard_map/ppermute | solution.py:214
  35.0 10.0 %collective-permute-start.13 = (bf16[3,128,128]{2,1,0:T(8,128)(2,1)S(1)}, bf16[3,128,128]{2,1,0:T(8,128)(2,1)S(1)}, u32[]{:S(2)}, u32[]{:S(2)}) collective-permute-start(bf16[3,128,128]{2,1,0:T(8,128)(2,1)S(1)} %feature_chunk.6.refs_3_), channel_id=1, source_target_pairs={{0,4},{1,5},{2,6},{3,7},{4,0},{5,1},{6,2},{7,3},{8,12},{9,13},{10,... | collective-permute-start | bytes 294920 | tf_op jit(solution)/shard_map/ppermute | solution.py:214
  37.9 7.2 %collective-permute-start.12 = (bf16[3,128,128]{2,1,0:T(8,128)(2,1)S(1)}, bf16[3,128,128]{2,1,0:T(8,128)(2,1)S(1)}, u32[]{:S(2)}, u32[]{:S(2)}) collective-permute-start(bf16[3,128,128]{2,1,0:T(8,128)(2,1)S(1)} %feature_chunk.6.refs_3_), channel_id=1, source_target_pairs={{0,2},{1,3},{2,4},{3,5},{4,6},{5,7},{6,0},{7,1},{8,10},{9,11},{10,... | collective-permute-start | bytes 294920 | tf_op jit(solution)/shard_map/ppermute | solution.py:214
  37.9 24.6 %copy-start.11 = (bf16[2,2,3,128,128]{4,3,2,1,0:T(8,128)(2,1)}, bf16[2,2,3,128,128]{4,3,2,1,0:T(8,128)(2,1)S(1)}, u32[]{:S(2)}) copy-start(bf16[2,2,3,128,128]{4,3,2,1,0:T(8,128)(2,1)S(1)} %pad_maximum_fusion.1.refs_1_) | copy-start | bytes 1179652
  38.7 23.0 %collective-permute-start.11 = (bf16[2,2,3,128,128]{4,3,2,1,0:T(8,128)(2,1)S(1)}, bf16[2,2,3,128,128]{4,3,2,1,0:T(8,128)(2,1)S(1)}, u32[]{:S(2)}, u32[]{:S(2)}) collective-permute-start(bf16[2,2,3,128,128]{4,3,2,1,0:T(8,128)(2,1)S(1)} %pad_maximum_fusion.1.refs_1_), channel_id=1, source_target_pairs={{0,1},{1,0},{2,3},{3,2},{4,5},{5,4},{6,7},{7,6},{8,9},{9,8},{10,11... | collective-permute-start | bytes 1179656 | tf_op jit(solution)/shard_map/ppermute | solution.py:210
  45.0 17.5 %copy-start.13 = (bf16[2,2,3,128,128]{4,3,2,1,0:T(8,128)(2,1)}, bf16[2,2,3,128,128]{4,3,2,1,0:T(8,128)(2,1)S(1)}, u32[]{:S(2)}) copy-start(bf16[2,2,3,128,128]{4,3,2,1,0:T(8,128)(2,1)S(1)} %collective-permute-done.6.refs_3_.refs_2_) | copy-start | bytes 1179652
  45.7 9.0 %collective-permute-start.15 = (bf16[2,3,128,128]{3,2,1,0:T(8,128)(2,1)S(1)}, bf16[2,3,128,128]{3,2,1,0:T(8,128)(2,1)S(1)}, u32[]{:S(2)}, u32[]{:S(2)}) collective-permute-start(bf16[2,3,128,128]{3,2,1,0:T(8,128)(2,1)S(1)} %get-tuple-element.53), channel_id=1, source_target_pairs={{0,8},{8,0},{1,9},{9,1},{2,10},{10,2},{3,11},{11,3},{4,12},{12,4},... | collective-permute-start | bytes 589832 | tf_op jit(solution)/shard_map/ppermute | solution.py:296
  49.6 13.5 %copy-start.1 = (s32[4000,6]{1,0:T(8,128)S(1)}, s32[4000,6]{1,0:T(8,128)}, u32[]{:S(2)}) copy-start(s32[4000,6]{1,0:T(8,128)} %copy.18.refs_1_.refs_6_.refs_5_.refs_7_) | copy-start | bytes 288004
  49.6 13.5 %copy-start.10 = (bf16[2,2,3,128,128]{4,3,2,1,0:T(8,128)(2,1)S(1)}, bf16[2,2,3,128,128]{4,3,2,1,0:T(8,128)(2,1)}, u32[]{:S(2)}) copy-start(bf16[2,2,3,128,128]{4,3,2,1,0:T(8,128)(2,1)} %copy-done.9) | copy-start | bytes 1179652
  50.2 5.1 %collective-permute-start.19 = (bf16[3,128,128]{2,1,0:T(8,128)(2,1)S(1)}, bf16[3,128,128]{2,1,0:T(8,128)(2,1)S(1)}, u32[]{:S(2)}, u32[]{:S(2)}) collective-permute-start(bf16[3,128,128]{2,1,0:T(8,128)(2,1)S(1)} %feature_chunk.7.refs_3_), channel_id=1, source_target_pairs={{0,6},{1,7},{2,0},{3,1},{4,2},{5,3},{6,4},{7,5},{8,14},{9,15},{10,... | collective-permute-start | bytes 294920 | tf_op jit(solution)/shard_map/ppermute | solution.py:214
  51.5 10.2 %collective-permute-start.18 = (bf16[3,128,128]{2,1,0:T(8,128)(2,1)S(1)}, bf16[3,128,128]{2,1,0:T(8,128)(2,1)S(1)}, u32[]{:S(2)}, u32[]{:S(2)}) collective-permute-start(bf16[3,128,128]{2,1,0:T(8,128)(2,1)S(1)} %feature_chunk.7.refs_3_), channel_id=1, source_target_pairs={{0,4},{1,5},{2,6},{3,7},{4,0},{5,1},{6,2},{7,3},{8,12},{9,13},{10,... | collective-permute-start | bytes 294920 | tf_op jit(solution)/shard_map/ppermute | solution.py:214
  52.7 9.0 %collective-permute-start.17 = (bf16[3,128,128]{2,1,0:T(8,128)(2,1)S(1)}, bf16[3,128,128]{2,1,0:T(8,128)(2,1)S(1)}, u32[]{:S(2)}, u32[]{:S(2)}) collective-permute-start(bf16[3,128,128]{2,1,0:T(8,128)(2,1)S(1)} %feature_chunk.7.refs_3_), channel_id=1, source_target_pairs={{0,2},{1,3},{2,4},{3,5},{4,6},{5,7},{6,0},{7,1},{8,10},{9,11},{10,... | collective-permute-start | bytes 294920 | tf_op jit(solution)/shard_map/ppermute | solution.py:214
  61.7 1.5 copy-start.15
  62.6 8.8 %collective-permute-start.20 = (bf16[2,3,128,128]{3,2,1,0:T(8,128)(2,1)S(1)}, bf16[2,3,128,128]{3,2,1,0:T(8,128)(2,1)S(1)}, u32[]{:S(2)}, u32[]{:S(2)}) collective-permute-start(bf16[2,3,128,128]{3,2,1,0:T(8,128)(2,1)S(1)} %get-tuple-element.57), channel_id=1, source_target_pairs={{0,8},{8,0},{1,9},{9,1},{2,10},{10,2},{3,11},{11,3},{4,12},{12,4},... | collective-permute-start | bytes 589832 | tf_op jit(solution)/shard_map/ppermute | solution.py:296
  64.2 7.8 %copy-start.12 = (bf16[2,2,3,128,128]{4,3,2,1,0:T(8,128)(2,1)S(1)}, bf16[2,2,3,128,128]{4,3,2,1,0:T(8,128)(2,1)}, u32[]{:S(2)}) copy-start(bf16[2,2,3,128,128]{4,3,2,1,0:T(8,128)(2,1)} %copy-done.11) | copy-start | bytes 1179652
  64.2 7.8 %copy-start.16 = (bf16[2,2,3,128,128]{4,3,2,1,0:T(8,128)(2,1)S(1)}, bf16[2,2,3,128,128]{4,3,2,1,0:T(8,128)(2,1)}, u32[]{:S(2)}) copy-start(bf16[2,2,3,128,128]{4,3,2,1,0:T(8,128)(2,1)} %copy-done.15) | copy-start | bytes 1179652
  69.7 12.1 %collective-permute-start.16 = (bf16[2,2,3,128,128]{4,3,2,1,0:T(8,128)(2,1)S(1)}, bf16[2,2,3,128,128]{4,3,2,1,0:T(8,128)(2,1)S(1)}, u32[]{:S(2)}, u32[]{:S(2)}) collective-permute-start(bf16[2,2,3,128,128]{4,3,2,1,0:T(8,128)(2,1)S(1)} %pad_maximum_fusion.2.refs_1_), channel_id=1, source_target_pairs={{0,1},{1,0},{2,3},{3,2},{4,5},{5,4},{6,7},{7,6},{8,9},{9,8},{10,11... | collective-permute-start | bytes 1179656 | tf_op jit(solution)/shard_map/ppermute | solution.py:210
  71.4 16.8 %collective-permute-start.21 = (bf16[2,2,3,128,128]{4,3,2,1,0:T(8,128)(2,1)S(1)}, bf16[2,2,3,128,128]{4,3,2,1,0:T(8,128)(2,1)S(1)}, u32[]{:S(2)}, u32[]{:S(2)}) collective-permute-start(bf16[2,2,3,128,128]{4,3,2,1,0:T(8,128)(2,1)S(1)} %pad_maximum_fusion.3.refs_1_), channel_id=1, source_target_pairs={{0,1},{1,0},{2,3},{3,2},{4,5},{5,4},{6,7},{7,6},{8,9},{9,8},{10,11... | collective-permute-start | bytes 1179656 | tf_op jit(solution)/shard_map/ppermute | solution.py:210
  88.2 5.6 %copy-start.28 = (s32[3,128]{1,0:T(4,128)S(1)}, s32[3,128]{1,0:T(4,128)}, u32[]{:S(2)}) copy-start(s32[3,128]{1,0:T(4,128)} %param.8) | copy-start | bytes 4612
  88.2 11.6 %copy-start.27 = (s32[3,2,2000]{2,1,0:T(2,128)S(1)}, s32[3,2,2000]{2,1,0:T(2,128)}, u32[]{:S(2)}) copy-start(s32[3,2,2000]{2,1,0:T(2,128)} %copy-done.26) | copy-start | bytes 144004
  93.7 14.2 %copy-start = (bf16[4,768,512]{2,1,0:T(8,128)(2,1)}, bf16[4,768,512]{2,1,0:T(8,128)(2,1)S(1)}, u32[]{:S(2)}) copy-start(bf16[4,768,512]{2,1,0:T(8,128)(2,1)S(1)} %get-tuple-element.66.refs_4_.refs_3_.refs_5_) | copy-start | bytes 9437188
  93.7 69.8 %collective-permute-start.29 = (bf16[4,768,512]{2,1,0:T(8,128)(2,1)S(1)}, bf16[4,768,512]{2,1,0:T(8,128)(2,1)}, u32[]{:S(2)}, u32[]{:S(2)}) collective-permute-start(bf16[4,768,512]{2,1,0:T(8,128)(2,1)S(1)} %get-tuple-element.66.refs_4_.refs_3_.refs_5_), channel_id=1, source_target_pairs={{0,16},{16,0},{1,17},{17,1},{2,18},{18,2},{3,19},{19,3},{4,20},{20... | collective-permute-start | bytes 9437192 | tf_op jit(solution)/shard_map/ppermute | solution.py:217
  93.9 3.6 %collective-permute-start = (s32[3,1]{0,1:T(1,128)S(1)}, s32[3,1]{0,1:T(1,128)S(1)}, u32[]{:S(2)}, u32[]{:S(2)}) collective-permute-start(s32[3,1]{0,1:T(1,128)S(1)} %bitcast.93), channel_id=1, source_target_pairs={{0,8},{8,0},{1,9},{9,1},{2,10},{10,2},{3,11},{11,3},{4,12},{12,4},... | collective-permute-start | bytes 44 | tf_op jit(solution)/shard_map/ppermute | solution.py:250
  95.5 4.3 %collective-permute-start.22 = (f32[2,3,2000]{2,1,0:T(4,128)S(1)}, f32[2,3,2000]{2,1,0:T(4,128)S(1)}, u32[]{:S(2)}, u32[]{:S(2)}) collective-permute-start(f32[2,3,2000]{2,1,0:T(4,128)S(1)} %add_add_fusion), channel_id=1, source_target_pairs={{0,8},{8,0},{1,9},{9,1},{2,10},{10,2},{3,11},{11,3},{4,12},{12,4},... | collective-permute-start | bytes 144008 | tf_op jit(solution)/shard_map/ppermute | solution.py:331
  108.6 37.3 %collective-permute-start.23 = (bf16[2,2,3,128,128]{4,3,2,1,0:T(8,128)(2,1)}, bf16[2,2,3,128,128]{4,3,2,1,0:T(8,128)(2,1)}, u32[]{:S(2)}, u32[]{:S(2)}) collective-permute-start(bf16[2,2,3,128,128]{4,3,2,1,0:T(8,128)(2,1)} %get-tuple-element.61), channel_id=1, source_target_pairs={{0,1},{1,0},{2,3},{3,2},{4,5},{5,4},{6,7},{7,6},{8,9},{9,8},{10,11... | collective-permute-start | bytes 1179656 | tf_op jit(solution)/shard_map/ppermute | solution.py:210
  117.3 37.4 %collective-permute-start.24 = (bf16[2,2,3,128,128]{4,3,2,1,0:T(8,128)(2,1)}, bf16[2,2,3,128,128]{4,3,2,1,0:T(8,128)(2,1)}, u32[]{:S(2)}, u32[]{:S(2)}) collective-permute-start(bf16[2,2,3,128,128]{4,3,2,1,0:T(8,128)(2,1)} %get-tuple-element.63), channel_id=1, source_target_pairs={{0,1},{1,0},{2,3},{3,2},{4,5},{5,4},{6,7},{7,6},{8,9},{9,8},{10,11... | collective-permute-start | bytes 1179656 | tf_op jit(solution)/shard_map/ppermute | solution.py:210
  119.7 13.9 %collective-permute-start.25 = (f32[1]{0:T(128)}, f32[1]{0:T(128)}, u32[]{:S(2)}, u32[]{:S(2)}) collective-permute-start(f32[1]{0:T(128)} %bitcast.18), channel_id=1, source_target_pairs={{0,1},{1,0},{2,3},{3,2},{4,5},{5,4},{6,7},{7,6},{8,9},{9,8},{10,11... | collective-permute-start | bytes 20 | tf_op jit(solution)/shard_map/ppermute | solution.py:343
  126.5 30.8 %collective-permute-start.30 = (bf16[2,3,2000]{2,1,0:T(4,128)(2,1)}, bf16[2,3,2000]{2,1,0:T(4,128)(2,1)S(1)}, u32[]{:S(2)}, u32[]{:S(2)}) collective-permute-start(bf16[2,3,2000]{2,1,0:T(4,128)(2,1)} %get-tuple-element.91), channel_id=1, source_target_pairs={{0,16},{16,0},{1,17},{17,1},{2,18},{18,2},{3,19},{19,3},{4,20},{20... | collective-permute-start | bytes 72008 | tf_op jit(solution)/shard_map/ppermute | solution.py:217
  134.2 3.6 %collective-permute-start.26 = (f32[1]{0:T(128)}, f32[1]{0:T(128)}, u32[]{:S(2)}, u32[]{:S(2)}) collective-permute-start(f32[1]{0:T(128)} %add.60), channel_id=1, source_target_pairs={{0,2},{1,3},{2,0},{3,1},{4,6},{5,7},{6,4},{7,5},{8,10},{9,11},{10,... | collective-permute-start | bytes 20 | tf_op jit(solution)/shard_map/ppermute | solution.py:343
  138.4 4.5 %collective-permute-start.27 = (f32[1]{0:T(128)}, f32[1]{0:T(128)}, u32[]{:S(2)}, u32[]{:S(2)}) collective-permute-start(f32[1]{0:T(128)} %add.61), channel_id=1, source_target_pairs={{0,4},{1,5},{2,6},{3,7},{4,0},{5,1},{6,2},{7,3},{8,12},{9,13},{10,... | collective-permute-start | bytes 20 | tf_op jit(solution)/shard_map/ppermute | solution.py:343
  143.5 1.2 collective-permute-start.28
  144.7 37.4 %collective-permute-start.35 = (bf16[2,2,3,128,128]{4,3,2,1,0:T(8,128)(2,1)}, bf16[2,2,3,128,128]{4,3,2,1,0:T(8,128)(2,1)}, u32[]{:S(2)}, u32[]{:S(2)}) collective-permute-start(bf16[2,2,3,128,128]{4,3,2,1,0:T(8,128)(2,1)} %get-tuple-element.74), channel_id=1, source_target_pairs={{0,1},{1,0},{2,3},{3,2},{4,5},{5,4},{6,7},{7,6},{8,9},{9,8},{10,11... | collective-permute-start | bytes 1179656 | tf_op jit(solution)/shard_map/ppermute | solution.py:210
  145.9 8.7 %copy-start.21 = (bf16[2,2,3,128,128]{4,3,2,1,0:T(8,128)(2,1)S(1)}, bf16[2,2,3,128,128]{4,3,2,1,0:T(8,128)(2,1)}, u32[]{:S(2)}) copy-start(bf16[2,2,3,128,128]{4,3,2,1,0:T(8,128)(2,1)} %copy-done.20) | copy-start | bytes 1179652
  145.9 8.7 %copy-start.23 = (bf16[2,2,3,128,128]{4,3,2,1,0:T(8,128)(2,1)S(1)}, bf16[2,2,3,128,128]{4,3,2,1,0:T(8,128)(2,1)}, u32[]{:S(2)}) copy-start(bf16[2,2,3,128,128]{4,3,2,1,0:T(8,128)(2,1)} %copy-done.22) | copy-start | bytes 1179652
  153.1 29.0 %collective-permute-start.36 = (bf16[2,2,3,128,128]{4,3,2,1,0:T(8,128)(2,1)}, bf16[2,2,3,128,128]{4,3,2,1,0:T(8,128)(2,1)}, u32[]{:S(2)}, u32[]{:S(2)}) collective-permute-start(bf16[2,2,3,128,128]{4,3,2,1,0:T(8,128)(2,1)} %get-tuple-element.75), channel_id=1, source_target_pairs={{0,1},{1,0},{2,3},{3,2},{4,5},{5,4},{6,7},{7,6},{8,9},{9,8},{10,11... | collective-permute-start | bytes 1179656 | tf_op jit(solution)/shard_map/ppermute | solution.py:210
  156.6 24.2 %collective-permute-start.31 = (bf16[2,2,3,128,128]{4,3,2,1,0:T(8,128)(2,1)}, bf16[2,2,3,128,128]{4,3,2,1,0:T(8,128)(2,1)}, u32[]{:S(2)}, u32[]{:S(2)}) collective-permute-start(bf16[2,2,3,128,128]{4,3,2,1,0:T(8,128)(2,1)} %get-tuple-element.68), channel_id=1, source_target_pairs={{0,8},{8,0},{1,9},{9,1},{2,10},{10,2},{3,11},{11,3},{4,12},{12,4},... | collective-permute-start | bytes 1179656 | tf_op jit(solution)/shard_map/ppermute | solution.py:420
  163.5 1.6 copy-start.2
  165.0 1.6 copy-start.4
  167.6 14.5 %copy-start.19 = (bf16[2,2,3,128,128]{4,3,2,1,0:T(8,128)(2,1)S(1)}, bf16[2,2,3,128,128]{4,3,2,1,0:T(8,128)(2,1)}, u32[]{:S(2)}) copy-start(bf16[2,2,3,128,128]{4,3,2,1,0:T(8,128)(2,1)} %copy-done.17) | copy-start | bytes 1179652
  167.6 14.5 %copy-start.25 = (bf16[2,2,3,128,128]{4,3,2,1,0:T(8,128)(2,1)S(1)}, bf16[2,2,3,128,128]{4,3,2,1,0:T(8,128)(2,1)}, u32[]{:S(2)}) copy-start(bf16[2,2,3,128,128]{4,3,2,1,0:T(8,128)(2,1)} %copy-done.24) | copy-start | bytes 1179652
  167.6 22.8 %copy-start.5 = (f32[4000,6]{1,0:T(8,128)S(1)}, f32[4000,6]{1,0:T(8,128)}, u32[]{:S(2)}) copy-start(f32[4000,6]{1,0:T(8,128)} %copy.21.refs_7_.refs_6_.refs_8_) | copy-start | bytes 288004
  180.8 9.6 %copy-start.3 = (s32[4000,6]{1,0:T(8,128)S(1)}, s32[4000,6]{1,0:T(8,128)}, u32[]{:S(2)}) copy-start(s32[4000,6]{1,0:T(8,128)} %copy.18.refs_1_.refs_6_.refs_5_.refs_7_) | copy-start | bytes 288004
  183.4 19.9 %collective-permute-start.37 = (bf16[2,2,3,128,128]{4,3,2,1,0:T(8,128)(2,1)S(1)}, bf16[2,2,3,128,128]{4,3,2,1,0:T(8,128)(2,1)S(1)}, u32[]{:S(2)}, u32[]{:S(2)}) collective-permute-start(bf16[2,2,3,128,128]{4,3,2,1,0:T(8,128)(2,1)S(1)} %get-tuple-element.79), channel_id=1, source_target_pairs={{0,8},{8,0},{1,9},{9,1},{2,10},{10,2},{3,11},{11,3},{4,12},{12,4},... | collective-permute-start | bytes 1179656 | tf_op jit(solution)/shard_map/ppermute | solution.py:420
  185.0 26.9 %collective-permute-start.32 = (bf16[2,3,128,128]{3,2,1,0:T(8,128)(2,1)S(1)}, bf16[2,3,128,128]{3,2,1,0:T(8,128)(2,1)S(1)}, u32[]{:S(2)}, u32[]{:S(2)}) collective-permute-start(bf16[2,3,128,128]{3,2,1,0:T(8,128)(2,1)S(1)} %get-tuple-element.69), channel_id=1, source_target_pairs={{0,2},{1,3},{2,4},{3,5},{4,6},{5,7},{6,0},{7,1},{8,10},{9,11},{10,... | collective-permute-start | bytes 589832 | tf_op jit(solution)/shard_map/ppermute | solution.py:214
  185.6 29.7 %collective-permute-start.33 = (bf16[2,3,128,128]{3,2,1,0:T(8,128)(2,1)S(1)}, bf16[2,3,128,128]{3,2,1,0:T(8,128)(2,1)S(1)}, u32[]{:S(2)}, u32[]{:S(2)}) collective-permute-start(bf16[2,3,128,128]{3,2,1,0:T(8,128)(2,1)S(1)} %get-tuple-element.70), channel_id=1, source_target_pairs={{0,4},{1,5},{2,6},{3,7},{4,0},{5,1},{6,2},{7,3},{8,12},{9,13},{10,... | collective-permute-start | bytes 589832 | tf_op jit(solution)/shard_map/ppermute | solution.py:214
  187.5 27.8 %collective-permute-start.34 = (bf16[2,3,128,128]{3,2,1,0:T(8,128)(2,1)S(1)}, bf16[2,3,128,128]{3,2,1,0:T(8,128)(2,1)S(1)}, u32[]{:S(2)}, u32[]{:S(2)}) collective-permute-start(bf16[2,3,128,128]{3,2,1,0:T(8,128)(2,1)S(1)} %get-tuple-element.71), channel_id=1, source_target_pairs={{0,6},{1,7},{2,0},{3,1},{4,2},{5,3},{6,4},{7,5},{8,14},{9,15},{10,... | collective-permute-start | bytes 589832 | tf_op jit(solution)/shard_map/ppermute | solution.py:214
  204.1 41.3 %collective-permute-start.38 = (bf16[2,3,128,128]{3,2,1,0:T(8,128)(2,1)S(1)}, bf16[2,3,128,128]{3,2,1,0:T(8,128)(2,1)S(1)}, u32[]{:S(2)}, u32[]{:S(2)}) collective-permute-start(bf16[2,3,128,128]{3,2,1,0:T(8,128)(2,1)S(1)} %get-tuple-element.85), channel_id=1, source_target_pairs={{0,2},{1,3},{2,4},{3,5},{4,6},{5,7},{6,0},{7,1},{8,10},{9,11},{10,... | collective-permute-start | bytes 589832 | tf_op jit(solution)/shard_map/ppermute | solution.py:214
  204.1 41.3 %collective-permute-start.39 = (bf16[2,3,128,128]{3,2,1,0:T(8,128)(2,1)S(1)}, bf16[2,3,128,128]{3,2,1,0:T(8,128)(2,1)S(1)}, u32[]{:S(2)}, u32[]{:S(2)}) collective-permute-start(bf16[2,3,128,128]{3,2,1,0:T(8,128)(2,1)S(1)} %get-tuple-element.86), channel_id=1, source_target_pairs={{0,4},{1,5},{2,6},{3,7},{4,0},{5,1},{6,2},{7,3},{8,12},{9,13},{10,... | collective-permute-start | bytes 589832 | tf_op jit(solution)/shard_map/ppermute | solution.py:214
  211.9 33.5 %collective-permute-start.40 = (bf16[2,3,128,128]{3,2,1,0:T(8,128)(2,1)S(1)}, bf16[2,3,128,128]{3,2,1,0:T(8,128)(2,1)S(1)}, u32[]{:S(2)}, u32[]{:S(2)}) collective-permute-start(bf16[2,3,128,128]{3,2,1,0:T(8,128)(2,1)S(1)} %get-tuple-element.87), channel_id=1, source_target_pairs={{0,6},{1,7},{2,0},{3,1},{4,2},{5,3},{6,4},{7,5},{8,14},{9,15},{10,... | collective-permute-start | bytes 589832 | tf_op jit(solution)/shard_map/ppermute | solution.py:214
  (6 other events, 5.0 us)
where the time goes:
time: 248 us; the launch traced here: 247 us
  Pallas kernels  123 us (50%)
  starting transfers between devices  57.4 us (23%)
  waiting for transfers between devices  39 us (16%)
  local copies, waits for them, and re-layouts  18.8 us (8%)
  between operations  4.93 us (2%)
  other arithmetic  3.88 us (2%)
    pallas_call x25, Pallas kernels, run(): pl.pallas_call(waiting(kernel, len(waits)), grid=grid, in_specs=[index_sp...  123 us
    ppermute x18, starting transfers between devices, across_z(): return lax.ppermute(value, 'vocab', perm)  26 us
    ppermute x18, waiting for transfers between devices, across_z(): return lax.ppermute(value, 'vocab', perm)  24.9 us
    ppermute x3, starting transfers between devices, on_device(): lax.ppermute(scores, 'vocab', [(i, i ^ distance) for i in range(blocks)])  12.5 us
    unnamed x58, local copies, waits for them, and re-layouts  10.2 us
    ppermute x8, starting transfers between devices, across_y(): return lax.ppermute(value, 'vocab', perm)  9.31 us
    reshape x5, local copies, waits for them, and re-layouts, by_term(): return value.transpose(1, 3, 0, 2).reshape(terms, groups * docs)  7.45 us
    ppermute x8, waiting for transfers between devices, across_y(): return lax.ppermute(value, 'vocab', perm)  5.26 us
  transfers between devices with their start and end apart: 41, of which 15 were waited for; matrix products, arithmetic and copies ran while one was open for 5% of the time, Pallas kernels for 46%

commit v1 on v0

--- a/solution.py
+++ b/solution.py
@@ -24,25 +24,31 @@
     return fits[-1] if fits else terms
 
 
+def ring_place(z, count):
+    return jnp.where(lax.rem(z, 2) == 1, lax.div(z + 1, 2), jnp.where(z == 0, 0, count - lax.div(z, 2)))
+
+
 def slice_kernel(index_ref, states_ref, out_ref):
     out_ref[...] = states_ref[...]
 
 
 def pick_kernel(slots, near, outer, index_ref, *refs):
-    held = refs[:outer]
-    gathered_ref = refs[outer]
-    sends = refs[outer + 1:]
+    held, outs = refs[:outer], refs[outer:]
     block_z, seq = index_ref[2], index_ref[3]
     for s in range(slots):
-        target = gathered_ref.at[0] if s == 0 else sends[s - 1]
         half = lax.rem(seq + slots - s, slots)
         for n in range(near):
-            back = lax.rem(block_z + outer - (half * near + n), outer)
+            back = lax.rem(ring_place(block_z, outer) + outer - ring_place(half * near + n, outer), outer)
             for b in range(outer):
 
                 @pl.when(back == b)
                 def _():
-                    target[n] = held[b][...]
+                    outs[s][n] = held[b][...]
+
+
+def join_kernel(index_ref, *refs):
+    for s in range(len(refs) - 1):
+        refs[-1][s] = refs[s][...]
 
 
 def logits_kernel(docs, inner, strips, *refs):
@@ -80,7 +86,7 @@
     places_ref, grads_ref = refs[1 + strips:3 + strips]
     outs = refs[3 + strips:3 + strips + inner]
     spread_ref, total_ref = refs[-2:]
-    slots, near, _, part, width = shape
+    count, slots, near, _, part, width = shape
     length = slots * part
     step = pl.program_id(0)
     head = jnp.concatenate([ref[...] for ref in heads], axis=1)
@@ -102,23 +108,41 @@
     def _():
         for q in range(inner):
             lane_y = lax.rem(index_ref[0] + q, inner)
-            for n in range(near):
-                lane = pl.multiple_of((n * inner + lane_y) * width, width)
-                for k in range(docs):
-                    for s in range(slots):
-                        piece = total_ref[pl.ds(k * length + s * part, part), pl.ds(lane, width)]
-                        outs[q][s, n, k] = piece.astype(jnp.bfloat16)
-
-
-def combine_kernel(count, inner, slots, index_ref, *refs):
-    outs = refs[count * inner:]
-    for i in range(count):
-        parts = refs[i * inner:(i + 1) * inner]
+            for i in range(count):
+                for n in range(near):
+                    lane = pl.multiple_of(((i * near + n) * inner + lane_y) * width, width)
+                    for k in range(docs):
+                        for s in range(slots):
+                            piece = total_ref[pl.ds(k * length + s * part, part), pl.ds(lane, width)]
+                            outs[q][i, s, n, k] = piece.astype(jnp.bfloat16)
+
+
+def combine_kernel(inner, slots, index_ref, *refs):
+    parts, outs = refs[:inner], refs[inner:]
+    for i in range(parts[0].shape[0]):
         for s in range(slots):
-            total = parts[0][s].astype(jnp.float32)
+            total = parts[0][i, s].astype(jnp.float32)
             for other in parts[1:]:
-                total = total + other[s].astype(jnp.float32)
+                total = total + other[i, s].astype(jnp.float32)
             outs[s][i] = total.astype(jnp.bfloat16)
+
+
+def columns_kernel(groups, index_ref, *refs):
+    rows = refs[:groups]
+    out_ref, turned_ref = refs[groups:]
+    steps, docs, columns = rows[0].shape
+    turned_ref[...] = jnp.zeros_like(turned_ref)
+    for step in range(steps):
+        for first in range(groups):
+
+            @pl.when(index_ref[1] == first)
+            def _():
+                for g in range(groups):
+                    place = (first + g) % groups * docs
+                    turned_ref[place:place + docs, :columns] = rows[g][step]
+
+        turned = turned_ref[...].T
+        out_ref[step * columns:(step + 1) * columns, :] = turned[:columns, :groups * docs]
 
 
 def sort_kernel(slots, near, outer, index_ref, *refs):
@@ -209,6 +233,9 @@
         perm = [(z * inner + y, z * inner + (y + shift) % inner) for z in range(outer) for y in range(inner)]
         return lax.ppermute(value, "vocab", perm)
 
+    order = [0] + list(range(1, outer, 2)) + [z for z in range(outer - 1, 0, -1) if z % 2 == 0]
+    ring = [(order[p] * inner + y, order[(p + 1) % outer] * inner + y) for p in range(outer) for y in range(inner)]
+
     def across_z(value, shift):
         perm = [(z * inner + y, (z + shift) % outer * inner + y) for z in range(outer) for y in range(inner)]
         return lax.ppermute(value, "vocab", perm)
@@ -270,7 +297,7 @@
     moved_shape = bf16(near, docs, part, width)
     gathered_chunks = []
     others = []
-    sent = None
+    first_step = None
     for c in range(chunks):
         (own,) = run(
             slice_kernel,
@@ -279,22 +306,30 @@
             [pl.BlockSpec((docs, part, width), functools.partial(lambda c, i: (0, 0, c), c))],
             [bf16(docs, part, width)],
             out_specs=[pl.BlockSpec((docs, part, width), lambda i: (0, 0, 0))],
-            waits=[sent],
+            waits=[first_step],
             grid=(1,),
         )
-        held = [own] + [across_z(own, back) for back in range(1, outer)]
-        gathered, *sends = run(
+        held = [own]
+        for _ in range(outer - 1):
+            held.append(lax.ppermute(held[-1], "vocab", ring))
+        first_step = held[min(1, outer - 1)]
+        mine, *sends = run(
             functools.partial(pick_kernel, slots, near, outer),
             "pick_halves",
             held,
             [vmem_spec] * outer,
-            [bf16(*piece_shape)] + [moved_shape] * (slots - 1),
-            waits=[gathered_chunks[c - 1] if c > 0 else None, others[c - 2] if c > 1 else None],
-        )
-        sent = gathered
-        if slots > 1:
-            arrived = [lax.ppermute(sends[s - 1], "seq", shift_perm(slots, -s)) for s in range(1, slots)]
-            gathered = jnp.concatenate([gathered[:1]] + [value[None] for value in arrived])
+            [moved_shape] * slots,
+            waits=[gathered_chunks[c - 2] if c > 1 else None],
+        )
+        arrived = [lax.ppermute(sends[s - 1], "seq", shift_perm(slots, -s)) for s in range(1, slots)]
+        (gathered,) = run(
+            join_kernel,
+            "join_tokens",
+            [mine, *arrived],
+            [vmem_spec] * slots,
+            [bf16(*piece_shape)],
+            waits=[others[c - 2] if c > 1 else None],
+        )
         gathered_chunks.append(gathered)
         others.append(across_y(gathered, -1) if inner > 1 else None)
 
@@ -318,7 +353,7 @@
                     (pl.squeezed, tokens, strips * width), functools.partial(lambda c, v: (c, 0, 0), c)
                 ),
             ],
-            waits=[None if previous else places_all],
+            waits=[places_all, gathered_chunks[-1]] if c == 0 else [validity, others[-2]] if c == 1 else [],
             flops=2 * tokens * strips * width * terms,
             aliases={inner + strips + 1: 1} if previous else {},
             grid=(steps,),
@@ -336,7 +371,12 @@
     query, positive, negative = view[:, :, 0], view[:, :, 1], view[:, :, 2]
     unscaled = jnp.stack([positive - negative, query, -query], axis=2).reshape(logits.shape) * slopes
     unscaled = unscaled.astype(jnp.bfloat16)
+    unscaled = unscaled.astype(jnp.float32)
     scores = jnp.sum(query * positive, axis=(0, 2)) - jnp.sum(query * negative, axis=(0, 2))
+    score_row = jnp.pad(scores, (0, columns - triples)).reshape(1, 1, columns)
+    packed = jnp.concatenate([unscaled, jnp.broadcast_to(score_row, (steps, 1, columns))], axis=1)
+    packed_all = other_groups(packed)
+    scores = in_group_order([scores] + [value[0, docs, :triples] for value in packed_all[1:]])
     if blocks & (blocks - 1) == 0:
         distance = 1
         while distance < blocks:
@@ -344,13 +384,19 @@
             distance *= 2
     else:
         scores = lax.psum(scores, "vocab")
-    margin = (scores - teacher_margin) / (triples * groups)
-    margin_all = in_group_order(other_groups(margin)).reshape(groups * triples)
-    grads_all = by_term(in_group_order(other_groups(unscaled)).astype(jnp.float32))
-    unscaled = unscaled.astype(jnp.float32)
+    margin_all = ((scores - in_group_order(other_groups(teacher_margin))) / (triples * groups)).reshape(-1)
+    margin = lax.dynamic_slice(margin_all, (group * triples,), (triples,))
+    (grads_all,) = run(
+        functools.partial(columns_kernel, groups),
+        "turn_gradients",
+        [unscaled] + [value[:, :docs] for value in packed_all[1:]],
+        [vmem_spec] * groups,
+        [jax.ShapeDtypeStruct((terms, groups * docs), jnp.float32)],
+        scratch=[pltpu.VMEM((-(-groups * docs // 8) * 8, -(-columns // LANES) * LANES), jnp.float32)],
+    )
     features_all = other_groups(features)
 
-    head_terms = divisor(terms, 400)
+    head_terms = divisor(terms, 800)
     ranges = terms // head_terms
     next_range = 0
     grad_head = token = None
@@ -383,38 +429,37 @@
         )
         next_range += count
 
-    parts = []
-    for c in range(chunks):
+    half = -(-chunks // 2)
+    chunk_groups = [members for members in (range(half), range(half, chunks)) if members]
+    pairs = []
+    for members in chunk_groups:
+        pair_shape = (len(members), *piece_shape)
+        lanes = len(members) * strips * width
         sums = run(
-            functools.partial(hidden_kernel, docs, inner, strips, piece_shape),
+            functools.partial(hidden_kernel, docs, inner, len(members) * strips, pair_shape),
             "hidden_terms",
-            [head_rows] * strips + [places, unscaled],
-            strip_specs(c) + [row_spec, row_spec],
-            [bf16(*piece_shape)] * inner,
-            out_specs=[piece_spec] * inner,
-            waits=[parts[c - 3][-1] if c > 2 else None],
-            flops=2 * tokens * strips * width * terms // 4,
-            scratch=[
-                pltpu.VMEM((tokens, columns), jnp.bfloat16),
-                pltpu.VMEM((tokens, strips * width), jnp.float32),
-            ],
+            [head_rows] * (len(members) * strips) + [places, unscaled],
+            [spec for c in members for spec in strip_specs(c)] + [row_spec, row_spec],
+            [bf16(*pair_shape)] * inner,
+            out_specs=[pl.BlockSpec(pair_shape, lambda v: (0,) * 6)] * inner,
+            flops=2 * tokens * lanes * terms // 4,
+            scratch=[pltpu.VMEM((tokens, columns), jnp.bfloat16), pltpu.VMEM((tokens, lanes), jnp.float32)],
             grid=(steps,),
         )
-        parts.append([sums[0]] + [across_y(sums[q], q) for q in range(1, inner)])
-
-    half = -(-chunks // 2)
-    pairs = [pair for pair in (parts[:half], parts[half:]) if pair]
-    share = ranges // 10
+        pairs.append([sums[0]] + [across_y(sums[q], q) for q in range(1, inner)])
+
+    share = ranges // 5
     mine_all = []
     arrived_all = []
 
     def add_blocks(pair, *waits):
+        count = pair[0].shape[0]
         mine = run(
-            functools.partial(combine_kernel, len(pair), inner, slots),
+            functools.partial(combine_kernel, inner, slots),
             "add_blocks",
-            [value for each in pair for value in each],
-            [vmem_spec] * (len(pair) * inner),
-            [bf16(len(pair), near, docs, part, width)] * slots,
+            pair,
+            [vmem_spec] * inner,
+            [bf16(count, near, docs, part, width)] * slots,
             waits=waits,
         )
         mine_all.append([mine[0]] + [lax.ppermute(mine[s], "seq", shift_perm(slots, s)) for s in range(1, slots)])
@@ -431,16 +476,15 @@
         arrived_all.append([pieces[0]] + [across_z(pieces[ahead], ahead) for ahead in range(1, outer)])
 
     add_blocks(pairs[0])
-    run_head(2 * share, mine_all[0][0], parts[-1][0])
+    run_head(2 * share, mine_all[0][0], pairs[-1][0])
     sort_pieces(mine_all[0], token)
     if len(pairs) > 1:
         add_blocks(pairs[1], arrived_all[0][0])
-        run_head(2 * share, arrived_all[0][0], mine_all[1][0])
+        run_head(share, arrived_all[0][0], mine_all[1][0])
         sort_pieces(mine_all[1], token)
-        run_head(share, arrived_all[1][0])
-    run_head(ranges - next_range, *arrived_all[0][1:])
+    run_head(ranges - next_range, arrived_all[-1][0])
     (grad_hidden,) = run(
-        functools.partial(finish_kernel, [len(pair) for pair in pairs], outer),
+        functools.partial(finish_kernel, [len(members) for members in chunk_groups], outer),
         "scale_hidden",
         [margin] + [value for arrived in arrived_all for value in arrived],
         [index_spec] + [vmem_spec] * (len(pairs) * outer),

time: 248 us -> 221 us (0.89)
  Pallas kernels: 123 us -> 111 us
  local copies, waits for them, and re-layouts: 18.8 us -> 10.1 us
  starting transfers between devices: 57.4 us -> 52 us
    ppermute x18 -> x6, waiting for transfers between devices: 24.9 us -> 0.02 us  [across_z(): return lax.ppermute(value, 'vocab', perm)]
    ppermute x3, waiting for transfers between devices: 2.26 us -> 23 us  [on_device(): lax.ppermute(scores, 'vocab', [(i, i ^ distance) for i in range(blocks)])]
    ppermute x0 -> x12, starting transfers between devices: none -> 20.5 us  [on_device(): held.append(lax.ppermute(held[-1], 'vocab', ring))]
    ppermute x18 -> x6, starting transfers between devices: 26 us -> 8.83 us  [across_z(): return lax.ppermute(value, 'vocab', perm)]
    pallas_call x25 -> x27, Pallas kernels: 123 us -> 111 us  [run(): pl.pallas_call(waiting(kernel, len(waits)), grid=grid, in_specs=[index_sp...]
    ppermute x0 -> x12, waiting for transfers between devices: none -> 10.9 us  [on_device(): held.append(lax.ppermute(held[-1], 'vocab', ring))]
    ppermute x3, starting transfers between devices: 12.5 us -> 3.93 us  [on_device(): lax.ppermute(scores, 'vocab', [(i, i ^ distance) for i in range(blocks)])]
    reshape x5 -> x2, local copies, waits for them, and re-layouts: 7.45 us -> 0.8 us  [by_term(): return value.transpose(1, 3, 0, 2).reshape(terms, groups * docs)]
  transfers between devices with their start and end apart: 41 -> 39, of which waited for: 15 -> 12; matrix products, arithmetic and copies ran while one was open for 5% -> 3% of each run, Pallas kernels for 46% -> 46%
where the time goes in v1:
time: 221 us; the launch traced here: 220 us
  Pallas kernels  111 us (50%)
  starting transfers between devices  52 us (24%)
  waiting for transfers between devices  40.4 us (18%)
  local copies, waits for them, and re-layouts  10.1 us (5%)
  other arithmetic  3.54 us (2%)
  between operations  2.82 us (1%)
    pallas_call x27, Pallas kernels, run(): pl.pallas_call(waiting(kernel, len(waits)), grid=grid, in_specs=[index_sp...  111 us
    ppermute x3, waiting for transfers between devices, on_device(): lax.ppermute(scores, 'vocab', [(i, i ^ distance) for i in range(blocks)])  23 us
    ppermute x12, starting transfers between devices, on_device(): held.append(lax.ppermute(held[-1], 'vocab', ring))  20.5 us
    ppermute x12, waiting for transfers between devices, on_device(): held.append(lax.ppermute(held[-1], 'vocab', ring))  10.9 us
    ppermute x6, starting transfers between devices, across_z(): return lax.ppermute(value, 'vocab', perm)  8.83 us
    ppermute x6, starting transfers between devices, across_y(): return lax.ppermute(value, 'vocab', perm)  8.35 us
    unnamed x24, local copies, waits for them, and re-layouts  7.08 us
  transfers between devices with their start and end apart: 39, of which 12 were waited for; matrix products, arithmetic and copies ran while one was open for 3% of the time, Pallas kernels for 46%

profile of v1, /device:TPU:0, one launch (start us, length us, event | category | flops | bytes accessed | tf_op | source)
XLA Modules:
  0.0 219.7 jit_solution(2996175186568367847)
XLA Ops:
  0.7 1.0 copy-done.3
  2.3 3.1 %collective-permute-start.2 = (bf16[3,128,128]{2,1,0:T(8,128)(2,1)S(1)}, bf16[3,128,128]{2,1,0:T(8,128)(2,1)S(1)}, u32[]{:S(2)}, u32[]{:S(2)}) collective-permute-start(bf16[3,128,128]{2,1,0:T(8,128)(2,1)S(1)} %feature_chunk.4.refs_1_), channel_id=1, source_target_pairs={{0,2},{1,3},{2,6},{3,7},{6,4},{7,5},{4,0},{5,1},{8,10},{9,11},{10,... | collective-permute-start | bytes 294920 | tf_op jit(solution)/shard_map/ppermute | solution.py:314
  5.3 3.8 %collective-permute-done.2.refs_1_.refs_2_ = bf16[3,128,128]{2,1,0:T(8,128)(2,1)S(1)} collective-permute-done((bf16[3,128,128]{2,1,0:T(8,128)(2,1)S(1)}, bf16[3,128,128]{2,1,0:T(8,128)(2,1)S(1)}, u32[]{:S(2)}, u32[]{:S(2)}) %collective-permute-start.2) | collective-permute-done | bytes 98336 | tf_op jit(solution)/shard_map/ppermute | solution.py:314
  9.7 1.0 collective-permute-start.3
  10.8 3.3 %collective-permute-start.13 = (bf16[3,128,128]{2,1,0:T(8,128)(2,1)S(1)}, bf16[3,128,128]{2,1,0:T(8,128)(2,1)S(1)}, u32[]{:S(2)}, u32[]{:S(2)}) collective-permute-start(bf16[3,128,128]{2,1,0:T(8,128)(2,1)S(1)} %collective-permute-done.2.refs_1_.refs_2_), channel_id=1, source_target_pairs={{0,2},{1,3},{2,6},{3,7},{6,4},{7,5},{4,0},{5,1},{8,10},{9,11},{10,... | collective-permute-start | bytes 294920 | tf_op jit(solution)/shard_map/ppermute | solution.py:314
  14.1 1.6 collective-permute-done.3.refs_2_.refs_1_
  16.9 3.3 %collective-permute-start.4 = (bf16[3,128,128]{2,1,0:T(8,128)(2,1)S(1)}, bf16[3,128,128]{2,1,0:T(8,128)(2,1)S(1)}, u32[]{:S(2)}, u32[]{:S(2)}) collective-permute-start(bf16[3,128,128]{2,1,0:T(8,128)(2,1)S(1)} %collective-permute-done.3.refs_2_.refs_1_), channel_id=1, source_target_pairs={{0,2},{1,3},{2,6},{3,7},{6,4},{7,5},{4,0},{5,1},{8,10},{9,11},{10,... | collective-permute-start | bytes 294920 | tf_op jit(solution)/shard_map/ppermute | solution.py:314
  20.2 0.8 convert_reduce_fusion
  21.0 1.5 collective-permute-start
  22.5 0.9 reshape.79
  23.6 1.0 copy-done.4
  25.2 0.8 collective-permute-start.9
  25.9 2.3 %collective-permute-start.17 = (bf16[3,128,128]{2,1,0:T(8,128)(2,1)S(1)}, bf16[3,128,128]{2,1,0:T(8,128)(2,1)S(1)}, u32[]{:S(2)}, u32[]{:S(2)}) collective-permute-start(bf16[3,128,128]{2,1,0:T(8,128)(2,1)S(1)} %collective-permute-done.8.refs_1_.refs_3_), channel_id=1, source_target_pairs={{0,2},{1,3},{2,6},{3,7},{6,4},{7,5},{4,0},{5,1},{8,10},{9,11},{10,... | collective-permute-start | bytes 294920 | tf_op jit(solution)/shard_map/ppermute | solution.py:314
  28.2 1.9 collective-permute-start.5
  30.9 2.8 %collective-permute-done.5.refs_4_ = bf16[3,128,128]{2,1,0:T(8,128)(2,1)S(1)} collective-permute-done((bf16[3,128,128]{2,1,0:T(8,128)(2,1)S(1)}, bf16[3,128,128]{2,1,0:T(8,128)(2,1)S(1)}, u32[]{:S(2)}, u32[]{:S(2)}) %collective-permute-start.5) | collective-permute-done | bytes 98336 | tf_op jit(solution)/shard_map/ppermute | solution.py:314
  33.7 1.0 collective-permute-start.15
  35.4 1.1 collective-permute-start.6
  36.5 1.0 collective-permute-start.10
  37.5 2.0 collective-permute-start.18
  39.5 0.9 collective-permute-done.15.refs_2_
  41.0 1.6 collective-permute-start.16
  43.8 1.1 collective-permute-start.19
  44.9 1.1 collective-permute-start.11
  46.6 1.6 collective-permute-start.7
  48.2 2.1 collective-permute-done.11.refs_5_
  50.4 1.5 pick_halves.5
  52.6 1.0 collective-permute-start.12
  53.6 1.3 join_tokens.7.refs_1_
  54.9 1.5 collective-permute-start.20
  57.5 1.1 collective-permute-done.12.refs_3_
  58.6 1.6 collective-permute-done.7.refs_1_.refs_4_
  60.2 0.9 copy-done.10
  61.1 1.0 join_tokens.5.refs_2_.refs_1_
  62.1 1.6 collective-permute-start.21
  63.7 1.0 copy-done.6
  64.7 5.9 %pooled_logits.4 = (f32[2,3,2000]{2,1,0:T(4,128)S(1)}, bf16[4,768,512]{2,1,0:T(8,128)(2,1)}) custom-call(s32[4]{0:T(128)S(1)} %pad_add_fusion.refs_0_, s32[4000,6]{1,0:T(8,128)S(1)} %copy.23.refs_1_.refs_6_.refs_5_, bf16[2,2,3,128,128]{4,3,2,1,0:T(8,128)(2,1)S(1)} %join_tokens.5.refs_2_.refs_1_, bf16[2,2,3,128,128]{4,3,2,1,0:T(8,128)(2,1)S(1)} %join_tokens.6.refs_3_.refs_1_, ...), custom_call_target="tpu_custom_call" | custom-call | flops 3145728000 | bytes 49152000 | tf_op jit(solution)/shard_map/pooled_logits/pallas_call | solution.py:283
  70.6 6.4 %pooled_logits.5 = (f32[2,3,2000]{2,1,0:T(4,128)S(1)}, bf16[4,768,512]{2,1,0:T(8,128)(2,1)}) custom-call(s32[4]{0:T(128)S(1)} %pad_add_fusion.refs_0_, f32[2,3,2000]{2,1,0:T(4,128)S(1)} %get-tuple-element.80.refs_1_, bf16[2,2,3,128,128]{4,3,2,1,0:T(8,128)(2,1)S(1)} %collective-permute-done.20.refs_2_, ...), custom_call_target="tpu_custom_call", output_to_operand_aliasing={{1}: (10, {})} | custom-call | flops 3145728000 | bytes 49152000 | tf_op jit(solution)/shard_map/pooled_logits/pallas_call | solution.py:283
  77.0 6.4 %pooled_logits.6 = (f32[2,3,2000]{2,1,0:T(4,128)S(1)}, bf16[4,768,512]{2,1,0:T(8,128)(2,1)}) custom-call(s32[4]{0:T(128)S(1)} %pad_add_fusion.refs_0_, bf16[2,2,3,128,128]{4,3,2,1,0:T(8,128)(2,1)} %join_tokens.7.refs_1_, bf16[2,2,3,128,128]{4,3,2,1,0:T(8,128)(2,1)S(1)} %collective-permute-done.20.refs_2_, ...), custom_call_target="tpu_custom_call", output_to_operand_aliasing={{1}: (8, {})} | custom-call | flops 3145728000 | bytes 49152000 | tf_op jit(solution)/shard_map/pooled_logits/pallas_call | solution.py:283
  83.4 5.9 %pooled_logits.7 = (f32[2,3,2000]{2,1,0:T(4,128)S(1)}, bf16[4,768,512]{2,1,0:T(8,128)(2,1)}) custom-call(s32[4]{0:T(128)S(1)} %pad_add_fusion.refs_0_, bf16[2,2,3,128,128]{4,3,2,1,0:T(8,128)(2,1)S(1)} %join_tokens.5.refs_2_.refs_1_, bf16[2,2,3,128,128]{4,3,2,1,0:T(8,128)(2,1)S(1)} %collective-permute-done.21.refs_2_, ...), custom_call_target="tpu_custom_call", output_to_operand_aliasing={{1}: (8, {})} | custom-call | flops 3145728000 | bytes 49152000 | tf_op jit(solution)/shard_map/pooled_logits/pallas_call | solution.py:283
  90.5 2.0 collective-permute-start.22
  92.5 2.8 %collective-permute-done.28 = f32[1]{0:T(128)} collective-permute-done((f32[1]{0:T(128)}, f32[1]{0:T(128)}, u32[]{:S(2)}, u32[]{:S(2)}) %collective-permute-start.28) | collective-permute-done | bytes 36 | tf_op jit(solution)/shard_map/ppermute | solution.py:244
  96.9 11.0 %hidden_terms.2 = (bf16[2,2,2,3,128,128]{5,4,3,2,1,0:T(8,128)(2,1)S(1)}, bf16[2,2,2,3,128,128]{5,4,3,2,1,0:T(8,128)(2,1)}) custom-call(s32[4]{0:T(128)S(1)} %pad_add_fusion.refs_0_, bf16[4000,2048]{1,0:T(8,128)(2,1)} %bitcast.67, bf16[4000,2048]{1,0:T(8,128)(2,1)} %bitcast.68, bf16[4000,2048]{1,0:T(8,128)(2,1)} %bitcast.69, bf16[4000,2048]{1,0:T(8,128)(2,1)} %bitcast.70, ...), custom_call_target="tpu_custom_call" | custom-call | flops 1572864000 | bytes 24576000 | tf_op jit(solution)/shard_map/hidden_terms/pallas_call | solution.py:283
  107.9 0.9 copy-done.7
  110.7 10.4 %hidden_terms.3 = (bf16[2,2,2,3,128,128]{5,4,3,2,1,0:T(8,128)(2,1)S(1)}, bf16[2,2,2,3,128,128]{5,4,3,2,1,0:T(8,128)(2,1)S(1)}) custom-call(s32[4]{0:T(128)S(1)} %pad_add_fusion.refs_0_, bf16[4000,2048]{1,0:T(8,128)(2,1)} %bitcast.75, bf16[4000,2048]{1,0:T(8,128)(2,1)} %bitcast.76, bf16[4000,2048]{1,0:T(8,128)(2,1)} %bitcast.77, bf16[4000,2048]{1,0:T(8,128)(2,1)} %bitcast.78, ...), custom_call_target="tpu_custom_call" | custom-call | flops 1572864000 | bytes 24576000 | tf_op jit(solution)/shard_map/hidden_terms/pallas_call | solution.py:283
  121.1 1.6 collective-permute-start.31
  124.4 1.2 turn_gradients.1.refs_7_.refs_6_
  125.6 19.9 %collective-permute-done.25 = f32[2,1]{0,1:T(1,128)S(1)} collective-permute-done((f32[2,1]{0,1:T(1,128)S(1)}, f32[2,1]{0,1:T(1,128)S(1)}, u32[]{:S(2)}, u32[]{:S(2)}) %collective-permute-start.25) | collective-permute-done | bytes 40 | tf_op jit(solution)/shard_map/ppermute | solution.py:383
  145.6 1.2 collective-permute-start.26
  146.9 2.3 %collective-permute-done.26 = f32[2,1]{0,1:T(1,128)S(1)} collective-permute-done((f32[2,1]{0,1:T(1,128)S(1)}, f32[2,1]{0,1:T(1,128)S(1)}, u32[]{:S(2)}, u32[]{:S(2)}) %collective-permute-start.26) | collective-permute-done | bytes 40 | tf_op jit(solution)/shard_map/ppermute | solution.py:383
  149.2 2.2 collective-permute-start.27
  151.3 1.4 add_blocks.2
  152.8 0.8 collective-permute-done.27
  153.7 18.4 %head_terms.3 = (f32[4000,2048]{1,0:T(8,128)}, f32[8,128]{1,0:T(8,128)S(1)}) custom-call(s32[4]{0:T(128)S(1)} %pad_add_fusion.refs_0_, bf16[2,2,3,128,128]{4,3,2,1,0:T(8,128)(2,1)S(1)} %get-tuple-element.57.refs_1_.refs_2_, bf16[2,2,2,3,128,128]{5,4,3,2,1,0:T(8,128)(2,1)S(1)} %get-tuple-element.58.refs_2_, f32[2]{0:T(128)S(1)} %bitcast.48, ...), custom_call_target="tpu_custom_call" | custom-call | flops 2516582400 | bytes 39321600 | tf_op jit(solution)/shard_map/head_terms/pallas_call | solution.py:283
  172.1 1.3 sort_pieces.2
  173.5 1.4 add_blocks.3
  174.9 1.9 collective-permute-start.32
  177.8 1.1 collective-permute-start.34
  178.9 2.4 %collective-permute-start.35 = (bf16[2,3,128,128]{3,2,1,0:T(8,128)(2,1)S(1)}, bf16[2,3,128,128]{3,2,1,0:T(8,128)(2,1)S(1)}, u32[]{:S(2)}, u32[]{:S(2)}) collective-permute-start(bf16[2,3,128,128]{3,2,1,0:T(8,128)(2,1)S(1)} %get-tuple-element.74), channel_id=1, source_target_pairs={{0,6},{1,7},{2,0},{3,1},{4,2},{5,3},{6,4},{7,5},{8,14},{9,15},{10,... | collective-permute-start | bytes 589832 | tf_op jit(solution)/shard_map/ppermute | solution.py:241
  181.3 1.6 copy-done.1
  182.9 10.4 %head_terms.4 = (f32[4000,2048]{1,0:T(8,128)}, f32[8,128]{1,0:T(8,128)S(1)}) custom-call(s32[4]{0:T(128)S(1)} %pad_add_fusion.refs_0_, bf16[2,3,128,128]{3,2,1,0:T(8,128)(2,1)S(1)} %get-tuple-element.62.refs_1_.refs_3_, bf16[2,2,3,128,128]{4,3,2,1,0:T(8,128)(2,1)S(1)} %get-tuple-element.64.refs_2_, f32[2]{0:T(128)S(1)} %bitcast.49, ...), custom_call_target="tpu_custom_call", output_to_operand_aliasing={{0}: (8, {})} | custom-call | flops 1258291200 | bytes 19660800 | tf_op jit(solution)/shard_map/head_terms/pallas_call | solution.py:283
  194.6 1.5 collective-permute-start.37
  196.1 2.8 %collective-permute-start.38 = (bf16[2,3,128,128]{3,2,1,0:T(8,128)(2,1)S(1)}, bf16[2,3,128,128]{3,2,1,0:T(8,128)(2,1)S(1)}, u32[]{:S(2)}, u32[]{:S(2)}) collective-permute-start(bf16[2,3,128,128]{3,2,1,0:T(8,128)(2,1)S(1)} %get-tuple-element.77), channel_id=1, source_target_pairs={{0,6},{1,7},{2,0},{3,1},{4,2},{5,3},{6,4},{7,5},{8,14},{9,15},{10,... | collective-permute-start | bytes 589832 | tf_op jit(solution)/shard_map/ppermute | solution.py:241
  199.0 18.4 %head_terms.5 = (f32[4000,2048]{1,0:T(8,128)}, f32[8,128]{1,0:T(8,128)S(1)}) custom-call(s32[4]{0:T(128)S(1)} %pad_add_fusion.refs_0_, bf16[2,3,128,128]{3,2,1,0:T(8,128)(2,1)S(1)} %get-tuple-element.68.refs_1_.refs_7_, f32[2]{0:T(128)S(1)} %bitcast.50, bf16[4,768,512]{2,1,0:T(8,128)(2,1)} %get-tuple-element.59.refs_4_.refs_3_, ...), custom_call_target="tpu_custom_call", output_to_operand_aliasing={{0}: (7, {})} | custom-call | flops 2516582400 | bytes 39321600 | tf_op jit(solution)/shard_map/head_terms/pallas_call | solution.py:283
  217.4 2.2 %scale_hidden.1 = bf16[3,128,512]{2,1,0:T(8,128)(2,1)} custom-call(s32[4]{0:T(128)S(1)} %pad_add_fusion.refs_0_, f32[8,128]{1,0:T(8,128)S(1)} %get-tuple-element.71.refs_1_, f32[1]{0:T(128)} %bitcast.22.refs_2_, bf16[2,3,128,128]{3,2,1,0:T(8,128)(2,1)S(1)} %get-tuple-element.62.refs_1_.refs_3_, bf16[2,3,128,128]{3,2,1,0:T(8,128)(2,1)S(1)} %collective-permute-done.33.refs_4_, ...), custom_call_target="tpu_custom_call" | custom-call | tf_op jit(solution)/shard_map/scale_hidden/pallas_call | solution.py:283
  (90 shorter events, 15.6 us)
Async XLA Ops:
  0.7 1.0 copy-start.3
  2.3 6.9 %collective-permute-start.2 = (bf16[3,128,128]{2,1,0:T(8,128)(2,1)S(1)}, bf16[3,128,128]{2,1,0:T(8,128)(2,1)S(1)}, u32[]{:S(2)}, u32[]{:S(2)}) collective-permute-start(bf16[3,128,128]{2,1,0:T(8,128)(2,1)S(1)} %feature_chunk.4.refs_1_), channel_id=1, source_target_pairs={{0,2},{1,3},{2,6},{3,7},{6,4},{7,5},{4,0},{5,1},{8,10},{9,11},{10,... | collective-permute-start | bytes 294920 | tf_op jit(solution)/shard_map/ppermute | solution.py:314
  9.7 6.0 %collective-permute-start.3 = (bf16[3,128,128]{2,1,0:T(8,128)(2,1)S(1)}, bf16[3,128,128]{2,1,0:T(8,128)(2,1)S(1)}, u32[]{:S(2)}, u32[]{:S(2)}) collective-permute-start(bf16[3,128,128]{2,1,0:T(8,128)(2,1)S(1)} %feature_chunk.5.refs_1_), channel_id=1, source_target_pairs={{0,2},{1,3},{2,6},{3,7},{6,4},{7,5},{4,0},{5,1},{8,10},{9,11},{10,... | collective-permute-start | bytes 294920 | tf_op jit(solution)/shard_map/ppermute | solution.py:314
  10.8 12.7 %collective-permute-start.13 = (bf16[3,128,128]{2,1,0:T(8,128)(2,1)S(1)}, bf16[3,128,128]{2,1,0:T(8,128)(2,1)S(1)}, u32[]{:S(2)}, u32[]{:S(2)}) collective-permute-start(bf16[3,128,128]{2,1,0:T(8,128)(2,1)S(1)} %collective-permute-done.2.refs_1_.refs_2_), channel_id=1, source_target_pairs={{0,2},{1,3},{2,6},{3,7},{6,4},{7,5},{4,0},{5,1},{8,10},{9,11},{10,... | collective-permute-start | bytes 294920 | tf_op jit(solution)/shard_map/ppermute | solution.py:314
  16.3 7.4 %collective-permute-start.8 = (bf16[3,128,128]{2,1,0:T(8,128)(2,1)S(1)}, bf16[3,128,128]{2,1,0:T(8,128)(2,1)S(1)}, u32[]{:S(2)}, u32[]{:S(2)}) collective-permute-start(bf16[3,128,128]{2,1,0:T(8,128)(2,1)S(1)} %feature_chunk.6.refs_2_), channel_id=1, source_target_pairs={{0,2},{1,3},{2,6},{3,7},{6,4},{7,5},{4,0},{5,1},{8,10},{9,11},{10,... | collective-permute-start | bytes 294920 | tf_op jit(solution)/shard_map/ppermute | solution.py:314
  16.9 11.3 %collective-permute-start.4 = (bf16[3,128,128]{2,1,0:T(8,128)(2,1)S(1)}, bf16[3,128,128]{2,1,0:T(8,128)(2,1)S(1)}, u32[]{:S(2)}, u32[]{:S(2)}) collective-permute-start(bf16[3,128,128]{2,1,0:T(8,128)(2,1)S(1)} %collective-permute-done.3.refs_2_.refs_1_), channel_id=1, source_target_pairs={{0,2},{1,3},{2,6},{3,7},{6,4},{7,5},{4,0},{5,1},{8,10},{9,11},{10,... | collective-permute-start | bytes 294920 | tf_op jit(solution)/shard_map/ppermute | solution.py:314
  21.0 14.5 %collective-permute-start = (s32[3,1]{0,1:T(1,128)S(1)}, s32[3,1]{0,1:T(1,128)S(1)}, u32[]{:S(2)}, u32[]{:S(2)}) collective-permute-start(s32[3,1]{0,1:T(1,128)S(1)} %bitcast.85), channel_id=1, source_target_pairs={{0,8},{8,0},{1,9},{9,1},{2,10},{10,2},{3,11},{11,3},{4,12},{12,4},... | collective-permute-start | bytes 44 | tf_op jit(solution)/shard_map/ppermute | solution.py:277
  23.5 6.7 %collective-permute-start.14 = (bf16[3,128,128]{2,1,0:T(8,128)(2,1)S(1)}, bf16[3,128,128]{2,1,0:T(8,128)(2,1)S(1)}, u32[]{:S(2)}, u32[]{:S(2)}) collective-permute-start(bf16[3,128,128]{2,1,0:T(8,128)(2,1)S(1)} %collective-permute-done.13.refs_3_), channel_id=1, source_target_pairs={{0,2},{1,3},{2,6},{3,7},{6,4},{7,5},{4,0},{5,1},{8,10},{9,11},{10,... | collective-permute-start | bytes 294920 | tf_op jit(solution)/shard_map/ppermute | solution.py:314
  23.6 1.0 copy-start.4
  25.2 11.4 %collective-permute-start.9 = (bf16[3,128,128]{2,1,0:T(8,128)(2,1)S(1)}, bf16[3,128,128]{2,1,0:T(8,128)(2,1)S(1)}, u32[]{:S(2)}, u32[]{:S(2)}) collective-permute-start(bf16[3,128,128]{2,1,0:T(8,128)(2,1)S(1)} %feature_chunk.7.refs_2_), channel_id=1, source_target_pairs={{0,2},{1,3},{2,6},{3,7},{6,4},{7,5},{4,0},{5,1},{8,10},{9,11},{10,... | collective-permute-start | bytes 294920 | tf_op jit(solution)/shard_map/ppermute | solution.py:314
  25.9 11.6 %collective-permute-start.17 = (bf16[3,128,128]{2,1,0:T(8,128)(2,1)S(1)}, bf16[3,128,128]{2,1,0:T(8,128)(2,1)S(1)}, u32[]{:S(2)}, u32[]{:S(2)}) collective-permute-start(bf16[3,128,128]{2,1,0:T(8,128)(2,1)S(1)} %collective-permute-done.8.refs_1_.refs_3_), channel_id=1, source_target_pairs={{0,2},{1,3},{2,6},{3,7},{6,4},{7,5},{4,0},{5,1},{8,10},{9,11},{10,... | collective-permute-start | bytes 294920 | tf_op jit(solution)/shard_map/ppermute | solution.py:314
  28.2 5.5 %collective-permute-start.5 = (bf16[3,128,128]{2,1,0:T(8,128)(2,1)S(1)}, bf16[3,128,128]{2,1,0:T(8,128)(2,1)S(1)}, u32[]{:S(2)}, u32[]{:S(2)}) collective-permute-start(bf16[3,128,128]{2,1,0:T(8,128)(2,1)S(1)} %collective-permute-done.4.refs_3_), channel_id=1, source_target_pairs={{0,2},{1,3},{2,6},{3,7},{6,4},{7,5},{4,0},{5,1},{8,10},{9,11},{10,... | collective-permute-start | bytes 294920 | tf_op jit(solution)/shard_map/ppermute | solution.py:314
  30.2 26.3 %collective-permute-start.1 = (s32[2,3,2000]{2,1,0:T(4,128)S(1)}, s32[2,3,2000]{2,1,0:T(4,128)S(1)}, u32[]{:S(2)}, u32[]{:S(2)}) collective-permute-start(s32[2,3,2000]{2,1,0:T(4,128)S(1)} %get-tuple-element.86.refs_9_.refs_7_), channel_id=1, source_target_pairs={{0,16},{16,0},{1,17},{17,1},{2,18},{18,2},{3,19},{19,3},{4,20},{20... | collective-permute-start | bytes 144008 | tf_op jit(solution)/shard_map/ppermute | solution.py:244
  33.7 6.7 %collective-permute-start.15 = (bf16[2,3,128,128]{3,2,1,0:T(8,128)(2,1)S(1)}, bf16[2,3,128,128]{3,2,1,0:T(8,128)(2,1)S(1)}, u32[]{:S(2)}, u32[]{:S(2)}) collective-permute-start(bf16[2,3,128,128]{3,2,1,0:T(8,128)(2,1)S(1)} %get-tuple-element.45), channel_id=1, source_target_pairs={{0,8},{8,0},{1,9},{9,1},{2,10},{10,2},{3,11},{11,3},{4,12},{12,4},... | collective-permute-start | bytes 589832 | tf_op jit(solution)/shard_map/ppermute | solution.py:324
  35.4 10.5 %collective-permute-start.6 = (bf16[2,3,128,128]{3,2,1,0:T(8,128)(2,1)S(1)}, bf16[2,3,128,128]{3,2,1,0:T(8,128)(2,1)S(1)}, u32[]{:S(2)}, u32[]{:S(2)}) collective-permute-start(bf16[2,3,128,128]{3,2,1,0:T(8,128)(2,1)S(1)} %get-tuple-element.41), channel_id=1, source_target_pairs={{0,8},{8,0},{1,9},{9,1},{2,10},{10,2},{3,11},{11,3},{4,12},{12,4},... | collective-permute-start | bytes 589832 | tf_op jit(solution)/shard_map/ppermute | solution.py:324
  36.5 8.3 %collective-permute-start.10 = (bf16[3,128,128]{2,1,0:T(8,128)(2,1)S(1)}, bf16[3,128,128]{2,1,0:T(8,128)(2,1)S(1)}, u32[]{:S(2)}, u32[]{:S(2)}) collective-permute-start(bf16[3,128,128]{2,1,0:T(8,128)(2,1)S(1)} %collective-permute-done.9.refs_3_), channel_id=1, source_target_pairs={{0,2},{1,3},{2,6},{3,7},{6,4},{7,5},{4,0},{5,1},{8,10},{9,11},{10,... | collective-permute-start | bytes 294920 | tf_op jit(solution)/shard_map/ppermute | solution.py:314
  37.5 5.6 %collective-permute-start.18 = (bf16[3,128,128]{2,1,0:T(8,128)(2,1)S(1)}, bf16[3,128,128]{2,1,0:T(8,128)(2,1)S(1)}, u32[]{:S(2)}, u32[]{:S(2)}) collective-permute-start(bf16[3,128,128]{2,1,0:T(8,128)(2,1)S(1)} %collective-permute-done.17.refs_4_), channel_id=1, source_target_pairs={{0,2},{1,3},{2,6},{3,7},{6,4},{7,5},{4,0},{5,1},{8,10},{9,11},{10,... | collective-permute-start | bytes 294920 | tf_op jit(solution)/shard_map/ppermute | solution.py:314
  41.0 12.6 %collective-permute-start.16 = (bf16[2,2,3,128,128]{4,3,2,1,0:T(8,128)(2,1)S(1)}, bf16[2,2,3,128,128]{4,3,2,1,0:T(8,128)(2,1)S(1)}, u32[]{:S(2)}, u32[]{:S(2)}) collective-permute-start(bf16[2,2,3,128,128]{4,3,2,1,0:T(8,128)(2,1)S(1)} %join_tokens.6.refs_3_.refs_1_), channel_id=1, source_target_pairs={{0,1},{1,0},{2,3},{3,2},{4,5},{5,4},{6,7},{7,6},{8,9},{9,8},{10,11... | collective-permute-start | bytes 1179656 | tf_op jit(solution)/shard_map/ppermute | solution.py:234
  43.8 9.8 %collective-permute-start.19 = (bf16[2,3,128,128]{3,2,1,0:T(8,128)(2,1)S(1)}, bf16[2,3,128,128]{3,2,1,0:T(8,128)(2,1)S(1)}, u32[]{:S(2)}, u32[]{:S(2)}) collective-permute-start(bf16[2,3,128,128]{3,2,1,0:T(8,128)(2,1)S(1)} %get-tuple-element.48), channel_id=1, source_target_pairs={{0,8},{8,0},{1,9},{9,1},{2,10},{10,2},{3,11},{11,3},{4,12},{12,4},... | collective-permute-start | bytes 589832 | tf_op jit(solution)/shard_map/ppermute | solution.py:324
  44.9 5.5 %collective-permute-start.11 = (bf16[3,128,128]{2,1,0:T(8,128)(2,1)S(1)}, bf16[3,128,128]{2,1,0:T(8,128)(2,1)S(1)}, u32[]{:S(2)}, u32[]{:S(2)}) collective-permute-start(bf16[3,128,128]{2,1,0:T(8,128)(2,1)S(1)} %collective-permute-done.10.refs_4_), channel_id=1, source_target_pairs={{0,2},{1,3},{2,6},{3,7},{6,4},{7,5},{4,0},{5,1},{8,10},{9,11},{10,... | collective-permute-start | bytes 294920 | tf_op jit(solution)/shard_map/ppermute | solution.py:314
  46.6 13.6 %collective-permute-start.7 = (bf16[2,2,3,128,128]{4,3,2,1,0:T(8,128)(2,1)S(1)}, bf16[2,2,3,128,128]{4,3,2,1,0:T(8,128)(2,1)}, u32[]{:S(2)}, u32[]{:S(2)}) collective-permute-start(bf16[2,2,3,128,128]{4,3,2,1,0:T(8,128)(2,1)S(1)} %join_tokens.4.refs_1_.refs_3_), channel_id=1, source_target_pairs={{0,1},{1,0},{2,3},{3,2},{4,5},{5,4},{6,7},{7,6},{8,9},{9,8},{10,11... | collective-permute-start | bytes 1179656 | tf_op jit(solution)/shard_map/ppermute | solution.py:234
  51.9 0.7 copy-start.9
  52.6 6.0 %collective-permute-start.12 = (bf16[2,3,128,128]{3,2,1,0:T(8,128)(2,1)}, bf16[2,3,128,128]{3,2,1,0:T(8,128)(2,1)}, u32[]{:S(2)}, u32[]{:S(2)}) collective-permute-start(bf16[2,3,128,128]{3,2,1,0:T(8,128)(2,1)} %get-tuple-element.43), channel_id=1, source_target_pairs={{0,8},{8,0},{1,9},{9,1},{2,10},{10,2},{3,11},{11,3},{4,12},{12,4},... | collective-permute-start | bytes 589832 | tf_op jit(solution)/shard_map/ppermute | solution.py:324
  53.6 2.8 %copy-start.5 = (bf16[2,2,3,128,128]{4,3,2,1,0:T(8,128)(2,1)}, bf16[2,2,3,128,128]{4,3,2,1,0:T(8,128)(2,1)S(1)}, u32[]{:S(2)}) copy-start(bf16[2,2,3,128,128]{4,3,2,1,0:T(8,128)(2,1)S(1)} %collective-permute-done.16.refs_4_.refs_1_) | copy-start | bytes 1179652
  54.9 15.6 %collective-permute-start.20 = (bf16[2,2,3,128,128]{4,3,2,1,0:T(8,128)(2,1)}, bf16[2,2,3,128,128]{4,3,2,1,0:T(8,128)(2,1)S(1)}, u32[]{:S(2)}, u32[]{:S(2)}) collective-permute-start(bf16[2,2,3,128,128]{4,3,2,1,0:T(8,128)(2,1)} %join_tokens.7.refs_1_), channel_id=1, source_target_pairs={{0,1},{1,0},{2,3},{3,2},{4,5},{5,4},{6,7},{7,6},{8,9},{9,8},{10,11... | collective-permute-start | bytes 1179656 | tf_op jit(solution)/shard_map/ppermute | solution.py:234
  60.2 0.9 copy-start.10
  62.1 21.3 %collective-permute-start.21 = (bf16[2,2,3,128,128]{4,3,2,1,0:T(8,128)(2,1)S(1)}, bf16[2,2,3,128,128]{4,3,2,1,0:T(8,128)(2,1)S(1)}, u32[]{:S(2)}, u32[]{:S(2)}) collective-permute-start(bf16[2,2,3,128,128]{4,3,2,1,0:T(8,128)(2,1)S(1)} %join_tokens.5.refs_2_.refs_1_), channel_id=1, source_target_pairs={{0,1},{1,0},{2,3},{3,2},{4,5},{5,4},{6,7},{7,6},{8,9},{9,8},{10,11... | collective-permute-start | bytes 1179656 | tf_op jit(solution)/shard_map/ppermute | solution.py:234
  63.7 1.0 copy-start.6
  89.3 64.4 %collective-permute-start.29 = (bf16[4,768,512]{2,1,0:T(8,128)(2,1)}, bf16[4,768,512]{2,1,0:T(8,128)(2,1)}, u32[]{:S(2)}, u32[]{:S(2)}) collective-permute-start(bf16[4,768,512]{2,1,0:T(8,128)(2,1)} %get-tuple-element.59.refs_4_.refs_3_), channel_id=1, source_target_pairs={{0,16},{16,0},{1,17},{17,1},{2,18},{18,2},{3,19},{19,3},{4,20},{20... | collective-permute-start | bytes 9437192 | tf_op jit(solution)/shard_map/ppermute | solution.py:244
  89.3 6.0 %collective-permute-start.28 = (f32[1]{0:T(128)}, f32[1]{0:T(128)}, u32[]{:S(2)}, u32[]{:S(2)}) collective-permute-start(f32[1]{0:T(128)} %param.9), channel_id=1, source_target_pairs={{0,16},{16,0},{1,17},{17,1},{2,18},{18,2},{3,19},{19,3},{4,20},{20... | collective-permute-start | bytes 20 | tf_op jit(solution)/shard_map/ppermute | solution.py:244
  90.5 5.4 %collective-permute-start.22 = (f32[2,3,2000]{2,1,0:T(4,128)S(1)}, f32[2,3,2000]{2,1,0:T(4,128)S(1)}, u32[]{:S(2)}, u32[]{:S(2)}) collective-permute-start(f32[2,3,2000]{2,1,0:T(4,128)S(1)} %add_add_fusion), channel_id=1, source_target_pairs={{0,8},{8,0},{1,9},{9,1},{2,10},{10,2},{3,11},{11,3},{4,12},{12,4},... | collective-permute-start | bytes 144008 | tf_op jit(solution)/shard_map/ppermute | solution.py:366
  107.9 0.9 copy-start.7
  108.8 42.5 %collective-permute-start.23 = (bf16[2,2,2,3,128,128]{5,4,3,2,1,0:T(8,128)(2,1)}, bf16[2,2,2,3,128,128]{5,4,3,2,1,0:T(8,128)(2,1)}, u32[]{:S(2)}, u32[]{:S(2)}) collective-permute-start(bf16[2,2,2,3,128,128]{5,4,3,2,1,0:T(8,128)(2,1)} %get-tuple-element.56), channel_id=1, source_target_pairs={{0,1},{1,0},{2,3},{3,2},{4,5},{5,4},{6,7},{7,6},{8,9},{9,8},{10,11... | collective-permute-start | bytes 2359304 | tf_op jit(solution)/shard_map/ppermute | solution.py:234
  110.6 40.7 %copy-start.8 = (bf16[2,2,2,3,128,128]{5,4,3,2,1,0:T(8,128)(2,1)S(1)}, bf16[2,2,2,3,128,128]{5,4,3,2,1,0:T(8,128)(2,1)}, u32[]{:S(2)}) copy-start(bf16[2,2,2,3,128,128]{5,4,3,2,1,0:T(8,128)(2,1)} %copy-done.7) | copy-start | bytes 2359300
  110.6 12.1 %collective-permute-start.24 = (f32[2,4,2000]{2,1,0:T(4,128)S(1)}, f32[2,4,2000]{2,1,0:T(4,128)S(1)}, u32[]{:S(2)}, u32[]{:S(2)}) collective-permute-start(f32[2,4,2000]{2,1,0:T(4,128)S(1)} %pad_maximum_fusion), channel_id=1, source_target_pairs={{0,16},{16,0},{1,17},{17,1},{2,18},{18,2},{3,19},{19,3},{4,20},{20... | collective-permute-start | bytes 192008 | tf_op jit(solution)/shard_map/ppermute | solution.py:244
  121.1 52.4 %collective-permute-start.31 = (bf16[2,2,2,3,128,128]{5,4,3,2,1,0:T(8,128)(2,1)S(1)}, bf16[2,2,2,3,128,128]{5,4,3,2,1,0:T(8,128)(2,1)S(1)}, u32[]{:S(2)}, u32[]{:S(2)}) collective-permute-start(bf16[2,2,2,3,128,128]{5,4,3,2,1,0:T(8,128)(2,1)S(1)} %get-tuple-element.63), channel_id=1, source_target_pairs={{0,1},{1,0},{2,3},{3,2},{4,5},{5,4},{6,7},{7,6},{8,9},{9,8},{10,11... | collective-permute-start | bytes 2359304 | tf_op jit(solution)/shard_map/ppermute | solution.py:234
  123.9 21.7 %collective-permute-start.25 = (f32[2,1]{0,1:T(1,128)S(1)}, f32[2,1]{0,1:T(1,128)S(1)}, u32[]{:S(2)}, u32[]{:S(2)}) collective-permute-start(f32[2,1]{0,1:T(1,128)S(1)} %constant_dynamic-slice_fusion.2), channel_id=1, source_target_pairs={{0,1},{1,0},{2,3},{3,2},{4,5},{5,4},{6,7},{7,6},{8,9},{9,8},{10,11... | collective-permute-start | bytes 32 | tf_op jit(solution)/shard_map/ppermute | solution.py:383
  125.6 46.5 %copy-start = (f32[4000,6]{1,0:T(8,128)}, f32[4000,6]{1,0:T(8,128)S(1)}, u32[]{:S(2)}) copy-start(f32[4000,6]{1,0:T(8,128)S(1)} %turn_gradients.1.refs_7_.refs_6_) | copy-start | bytes 288004
  145.6 3.5 %collective-permute-start.26 = (f32[2,1]{0,1:T(1,128)S(1)}, f32[2,1]{0,1:T(1,128)S(1)}, u32[]{:S(2)}, u32[]{:S(2)}) collective-permute-start(f32[2,1]{0,1:T(1,128)S(1)} %fusion.16), channel_id=1, source_target_pairs={{0,2},{1,3},{2,0},{3,1},{4,6},{5,7},{6,4},{7,5},{8,10},{9,11},{10,... | collective-permute-start | bytes 32 | tf_op jit(solution)/shard_map/ppermute | solution.py:383
  149.2 4.4 %collective-permute-start.27 = (f32[2,1]{0,1:T(1,128)S(1)}, f32[2,1]{0,1:T(1,128)S(1)}, u32[]{:S(2)}, u32[]{:S(2)}) collective-permute-start(f32[2,1]{0,1:T(1,128)S(1)} %add.66), channel_id=1, source_target_pairs={{0,4},{1,5},{2,6},{3,7},{4,0},{5,1},{6,2},{7,3},{8,12},{9,13},{10,... | collective-permute-start | bytes 32 | tf_op jit(solution)/shard_map/ppermute | solution.py:383
  152.7 19.4 %collective-permute-start.30 = (bf16[2,2,3,128,128]{4,3,2,1,0:T(8,128)(2,1)S(1)}, bf16[2,2,3,128,128]{4,3,2,1,0:T(8,128)(2,1)S(1)}, u32[]{:S(2)}, u32[]{:S(2)}) collective-permute-start(bf16[2,2,3,128,128]{4,3,2,1,0:T(8,128)(2,1)S(1)} %get-tuple-element.61), channel_id=1, source_target_pairs={{0,8},{8,0},{1,9},{9,1},{2,10},{10,2},{3,11},{11,3},{4,12},{12,4},... | collective-permute-start | bytes 1179656 | tf_op jit(solution)/shard_map/ppermute | solution.py:465
  173.5 3.3 %copy-start.11 = (bf16[2,3,128,128]{3,2,1,0:T(8,128)(2,1)}, bf16[2,3,128,128]{3,2,1,0:T(8,128)(2,1)S(1)}, u32[]{:S(2)}) copy-start(bf16[2,3,128,128]{3,2,1,0:T(8,128)(2,1)S(1)} %get-tuple-element.73) | copy-start | bytes 589828
  174.9 18.4 %collective-permute-start.32 = (bf16[2,2,3,128,128]{4,3,2,1,0:T(8,128)(2,1)}, bf16[2,2,3,128,128]{4,3,2,1,0:T(8,128)(2,1)S(1)}, u32[]{:S(2)}, u32[]{:S(2)}) collective-permute-start(bf16[2,2,3,128,128]{4,3,2,1,0:T(8,128)(2,1)} %get-tuple-element.67), channel_id=1, source_target_pairs={{0,8},{8,0},{1,9},{9,1},{2,10},{10,2},{3,11},{11,3},{4,12},{12,4},... | collective-permute-start | bytes 1179656 | tf_op jit(solution)/shard_map/ppermute | solution.py:465
  176.8 19.3 %collective-permute-start.33 = (bf16[2,3,128,128]{3,2,1,0:T(8,128)(2,1)}, bf16[2,3,128,128]{3,2,1,0:T(8,128)(2,1)S(1)}, u32[]{:S(2)}, u32[]{:S(2)}) collective-permute-start(bf16[2,3,128,128]{3,2,1,0:T(8,128)(2,1)} %get-tuple-element.72), channel_id=1, source_target_pairs={{0,2},{1,3},{2,4},{3,5},{4,6},{5,7},{6,0},{7,1},{8,10},{9,11},{10,... | collective-permute-start | bytes 589832 | tf_op jit(solution)/shard_map/ppermute | solution.py:241
  177.8 39.6 %collective-permute-start.34 = (bf16[2,3,128,128]{3,2,1,0:T(8,128)(2,1)}, bf16[2,3,128,128]{3,2,1,0:T(8,128)(2,1)S(1)}, u32[]{:S(2)}, u32[]{:S(2)}) collective-permute-start(bf16[2,3,128,128]{3,2,1,0:T(8,128)(2,1)} %copy-done.11), channel_id=1, source_target_pairs={{0,4},{1,5},{2,6},{3,7},{4,0},{5,1},{6,2},{7,3},{8,12},{9,13},{10,... | collective-permute-start | bytes 589832 | tf_op jit(solution)/shard_map/ppermute | solution.py:241
  178.9 38.5 %collective-permute-start.35 = (bf16[2,3,128,128]{3,2,1,0:T(8,128)(2,1)S(1)}, bf16[2,3,128,128]{3,2,1,0:T(8,128)(2,1)S(1)}, u32[]{:S(2)}, u32[]{:S(2)}) collective-permute-start(bf16[2,3,128,128]{3,2,1,0:T(8,128)(2,1)S(1)} %get-tuple-element.74), channel_id=1, source_target_pairs={{0,6},{1,7},{2,0},{3,1},{4,2},{5,3},{6,4},{7,5},{8,14},{9,15},{10,... | collective-permute-start | bytes 589832 | tf_op jit(solution)/shard_map/ppermute | solution.py:241
  181.3 1.6 copy-start.1
  182.9 16.1 %copy-start.2 = (f32[4000,6]{1,0:T(8,128)S(1)}, f32[4000,6]{1,0:T(8,128)}, u32[]{:S(2)}) copy-start(f32[4000,6]{1,0:T(8,128)} %copy-done) | copy-start | bytes 288004
  194.0 23.5 %collective-permute-start.36 = (bf16[2,3,128,128]{3,2,1,0:T(8,128)(2,1)S(1)}, bf16[2,3,128,128]{3,2,1,0:T(8,128)(2,1)S(1)}, u32[]{:S(2)}, u32[]{:S(2)}) collective-permute-start(bf16[2,3,128,128]{3,2,1,0:T(8,128)(2,1)S(1)} %get-tuple-element.75), channel_id=1, source_target_pairs={{0,2},{1,3},{2,4},{3,5},{4,6},{5,7},{6,0},{7,1},{8,10},{9,11},{10,... | collective-permute-start | bytes 589832 | tf_op jit(solution)/shard_map/ppermute | solution.py:241
  194.6 22.8 %collective-permute-start.37 = (bf16[2,3,128,128]{3,2,1,0:T(8,128)(2,1)S(1)}, bf16[2,3,128,128]{3,2,1,0:T(8,128)(2,1)S(1)}, u32[]{:S(2)}, u32[]{:S(2)}) collective-permute-start(bf16[2,3,128,128]{3,2,1,0:T(8,128)(2,1)S(1)} %get-tuple-element.76), channel_id=1, source_target_pairs={{0,4},{1,5},{2,6},{3,7},{4,0},{5,1},{6,2},{7,3},{8,12},{9,13},{10,... | collective-permute-start | bytes 589832 | tf_op jit(solution)/shard_map/ppermute | solution.py:241
  196.1 21.3 %collective-permute-start.38 = (bf16[2,3,128,128]{3,2,1,0:T(8,128)(2,1)S(1)}, bf16[2,3,128,128]{3,2,1,0:T(8,128)(2,1)S(1)}, u32[]{:S(2)}, u32[]{:S(2)}) collective-permute-start(bf16[2,3,128,128]{3,2,1,0:T(8,128)(2,1)S(1)} %get-tuple-element.77), channel_id=1, source_target_pairs={{0,6},{1,7},{2,0},{3,1},{4,2},{5,3},{6,4},{7,5},{8,14},{9,15},{10,... | collective-permute-start | bytes 589832 | tf_op jit(solution)/shard_map/ppermute | solution.py:241

commit v2 on v1

--- a/solution.py
+++ b/solution.py
@@ -28,7 +28,7 @@
     return jnp.where(lax.rem(z, 2) == 1, lax.div(z + 1, 2), jnp.where(z == 0, 0, count - lax.div(z, 2)))
 
 
-def slice_kernel(index_ref, states_ref, out_ref):
+def copy_kernel(index_ref, states_ref, out_ref):
     out_ref[...] = states_ref[...]
 
 
@@ -127,10 +127,11 @@
             outs[s][i] = total.astype(jnp.bfloat16)
 
 
-def columns_kernel(groups, index_ref, *refs):
-    rows = refs[:groups]
+def columns_kernel(groups, docs, index_ref, *refs):
+    packed = refs[:groups]
     out_ref, turned_ref = refs[groups:]
-    steps, docs, columns = rows[0].shape
+    steps, _, columns = packed[0].shape
+    count = groups * docs
     turned_ref[...] = jnp.zeros_like(turned_ref)
     for step in range(steps):
         for first in range(groups):
@@ -139,10 +140,11 @@
             def _():
                 for g in range(groups):
                     place = (first + g) % groups * docs
-                    turned_ref[place:place + docs, :columns] = rows[g][step]
+                    turned_ref[place:place + docs, :columns] = packed[g][step, :docs]
+                    turned_ref[count + place:count + place + docs, :columns] = packed[g][step, docs:2 * docs]
 
         turned = turned_ref[...].T
-        out_ref[step * columns:(step + 1) * columns, :] = turned[:columns, :groups * docs]
+        out_ref[step * columns:(step + 1) * columns, :] = turned[:columns, :2 * count]
 
 
 def sort_kernel(slots, near, outer, index_ref, *refs):
@@ -177,18 +179,19 @@
 def head_kernel(groups, docs, *refs):
     index_ref, margin_ref = refs[:2]
     rows = refs[2:2 + groups]
-    places_ref, grads_ref = refs[2 + groups:4 + groups]
+    columns_ref = refs[2 + groups]
     out_ref, token_ref, spread_ref = refs[-3:]
     chunks, tokens, width = rows[0].shape
     length = tokens // docs
+    count = groups * docs
 
     @pl.when(pl.program_id(1) == 0)
     def _():
         token_ref[...] = jnp.zeros_like(token_ref)
-        token = lax.broadcasted_iota(jnp.int32, (out_ref.shape[0], length), 1)
-        for k in range(groups * docs):
-            grads = grads_ref[:, k:k + 1] * margin_ref[k // 3]
-            spread = jnp.where(token == places_ref[:, k:k + 1], grads, 0.0)
+        token = lax.broadcasted_iota(jnp.int32, (out_ref.shape[0], length), 1).astype(jnp.float32)
+        for k in range(count):
+            grads = columns_ref[:, k:k + 1] * margin_ref[k // 3]
+            spread = jnp.where(token == columns_ref[:, count + k:count + k + 1], grads, 0.0)
             spread_ref[:, k * length:(k + 1) * length] = spread.astype(jnp.bfloat16)
 
     for first in range(groups):
@@ -234,7 +237,14 @@
         return lax.ppermute(value, "vocab", perm)
 
     order = [0] + list(range(1, outer, 2)) + [z for z in range(outer - 1, 0, -1) if z % 2 == 0]
-    ring = [(order[p] * inner + y, order[(p + 1) % outer] * inner + y) for p in range(outer) for y in range(inner)]
+
+    def around_ring(value, steps_on):
+        perm = [
+            (order[p] * inner + y, order[(p + steps_on) % outer] * inner + y)
+            for p in range(outer)
+            for y in range(inner)
+        ]
+        return lax.ppermute(value, "vocab", perm)
 
     def across_z(value, shift):
         perm = [(z * inner + y, (z + shift) % outer * inner + y) for z in range(outer) for y in range(inner)]
@@ -246,9 +256,6 @@
     def in_group_order(values):
         doubled = jnp.stack(values + values)
         return lax.dynamic_slice_in_dim(doubled, lax.rem(groups - group, groups), groups, axis=0)
-
-    def by_term(value):
-        return value.transpose(1, 3, 0, 2).reshape(terms, groups * docs)
 
     def blocked(value):
         return value.reshape(docs, steps, columns).transpose(1, 0, 2)
@@ -276,7 +283,6 @@
     for s in range(1, slots):
         lengths = lengths + lax.ppermute(own_lengths, "seq", shift_perm(slots, s))
     validity = (owner_blocks < lengths[None]).astype(jnp.float32)
-    places_all = by_term(in_group_order(other_groups(places)))
 
     def run(kernel, name, operands, specs, shapes, out_specs=None, waits=(), flops=0, aliases={}, scratch=(), grid=()):
         waits = [value for value in waits if value is not None]
@@ -295,53 +301,20 @@
 
     bf16 = lambda *shape: jax.ShapeDtypeStruct(shape, jnp.bfloat16)
     moved_shape = bf16(near, docs, part, width)
+    sliced = [hidden_states[:, :, c * width:(c + 1) * width] for c in range(chunks)]
+    last = chunks - 1
     gathered_chunks = []
     others = []
-    first_step = None
-    for c in range(chunks):
-        (own,) = run(
-            slice_kernel,
-            "feature_chunk",
-            [hidden_states],
-            [pl.BlockSpec((docs, part, width), functools.partial(lambda c, i: (0, 0, c), c))],
-            [bf16(docs, part, width)],
-            out_specs=[pl.BlockSpec((docs, part, width), lambda i: (0, 0, 0))],
-            waits=[first_step],
-            grid=(1,),
-        )
-        held = [own]
-        for _ in range(outer - 1):
-            held.append(lax.ppermute(held[-1], "vocab", ring))
-        first_step = held[min(1, outer - 1)]
-        mine, *sends = run(
-            functools.partial(pick_kernel, slots, near, outer),
-            "pick_halves",
-            held,
-            [vmem_spec] * outer,
-            [moved_shape] * slots,
-            waits=[gathered_chunks[c - 2] if c > 1 else None],
-        )
-        arrived = [lax.ppermute(sends[s - 1], "seq", shift_perm(slots, -s)) for s in range(1, slots)]
-        (gathered,) = run(
-            join_kernel,
-            "join_tokens",
-            [mine, *arrived],
-            [vmem_spec] * slots,
-            [bf16(*piece_shape)],
-            waits=[others[c - 2] if c > 1 else None],
-        )
-        gathered_chunks.append(gathered)
-        others.append(across_y(gathered, -1) if inner > 1 else None)
-
     logit_parts = []
     features = None
-    for c in range(chunks):
-        pieces = [gathered_chunks[c], others[c]][:inner]
+
+    def add_logits(c, waits):
+        nonlocal features
         previous = [] if features is None else [features]
         chunk_logits, features = run(
             functools.partial(logits_kernel, docs, inner, strips),
             "pooled_logits",
-            [*pieces, *[head_rows] * strips, places, *previous],
+            [gathered_chunks[c], others[c]][:inner] + [head_rows] * strips + [places, *previous],
             [piece_spec] * inner + strip_specs(c) + [row_spec] + [any_spec] * len(previous),
             [
                 jax.ShapeDtypeStruct((steps, docs, columns), jnp.float32),
@@ -353,12 +326,47 @@
                     (pl.squeezed, tokens, strips * width), functools.partial(lambda c, v: (c, 0, 0), c)
                 ),
             ],
-            waits=[places_all, gathered_chunks[-1]] if c == 0 else [validity, others[-2]] if c == 1 else [],
+            waits=waits,
             flops=2 * tokens * strips * width * terms,
             aliases={inner + strips + 1: 1} if previous else {},
             grid=(steps,),
         )
         logit_parts.append(chunk_logits)
+
+    first_step = None
+    for c in range(chunks):
+        own = sliced[c]
+        if c > 0:
+            (own,) = run(
+                copy_kernel, "feature_chunk", [own], [vmem_spec], [bf16(docs, part, width)], waits=[first_step]
+            )
+        held = [own]
+        for back in range(1, outer):
+            held.append(around_ring(own, back) if c == 0 else around_ring(held[-1], 1))
+        first_step = held[min(1, outer - 1)]
+        mine, *sends = run(
+            functools.partial(pick_kernel, slots, near, outer),
+            "pick_halves",
+            held,
+            [vmem_spec] * outer,
+            [moved_shape] * slots,
+            waits=[gathered_chunks[c - 1] if c > 0 else None],
+        )
+        arrived = [lax.ppermute(sends[s - 1], "seq", shift_perm(slots, -s)) for s in range(1, slots)]
+        if c == last and c > 1:
+            add_logits(0, [mine])
+        (gathered,) = run(
+            join_kernel,
+            "join_tokens",
+            [mine, *arrived],
+            [vmem_spec] * slots,
+            [bf16(*piece_shape)],
+            waits=[others[c - 2] if c > 1 else None, logit_parts[0] if logit_parts else None],
+        )
+        gathered_chunks.append(gathered)
+        others.append(across_y(gathered, -1) if inner > 1 else None)
+    for c in range(len(logit_parts), chunks):
+        add_logits(c, [validity, others[-2]] if c == 1 else [])
 
     logit_part = functools.reduce(jnp.add, logit_parts)
     logits = logit_part
@@ -373,26 +381,37 @@
     unscaled = unscaled.astype(jnp.bfloat16)
     unscaled = unscaled.astype(jnp.float32)
     scores = jnp.sum(query * positive, axis=(0, 2)) - jnp.sum(query * negative, axis=(0, 2))
-    score_row = jnp.pad(scores, (0, columns - triples)).reshape(1, 1, columns)
-    packed = jnp.concatenate([unscaled, jnp.broadcast_to(score_row, (steps, 1, columns))], axis=1)
+    paired = blocks & (blocks - 1) == 0
+    distance = 1
+
+    def add_distance(value, distance):
+        return value + lax.ppermute(value, "vocab", [(i, i ^ distance) for i in range(blocks)])
+
+    if paired and blocks > 1:
+        scores = add_distance(scores, distance)
+        distance *= 2
+    score_row = jnp.pad(jnp.concatenate([scores, teacher_margin]), (0, columns - 2 * triples))
+    packed = jnp.concatenate(
+        [unscaled, places.astype(jnp.float32), jnp.broadcast_to(score_row, (steps, 1, columns))], axis=1
+    )
     packed_all = other_groups(packed)
-    scores = in_group_order([scores] + [value[0, docs, :triples] for value in packed_all[1:]])
-    if blocks & (blocks - 1) == 0:
-        distance = 1
+    scores = in_group_order([scores] + [value[0, 2 * docs, :triples] for value in packed_all[1:]])
+    teacher = in_group_order([teacher_margin] + [value[0, 2 * docs, triples:2 * triples] for value in packed_all[1:]])
+    if paired:
         while distance < blocks:
-            scores = scores + lax.ppermute(scores, "vocab", [(i, i ^ distance) for i in range(blocks)])
+            scores = add_distance(scores, distance)
             distance *= 2
     else:
         scores = lax.psum(scores, "vocab")
-    margin_all = ((scores - in_group_order(other_groups(teacher_margin))) / (triples * groups)).reshape(-1)
+    margin_all = ((scores - teacher) / (triples * groups)).reshape(-1)
     margin = lax.dynamic_slice(margin_all, (group * triples,), (triples,))
-    (grads_all,) = run(
-        functools.partial(columns_kernel, groups),
+    (head_columns,) = run(
+        functools.partial(columns_kernel, groups, docs),
         "turn_gradients",
-        [unscaled] + [value[:, :docs] for value in packed_all[1:]],
+        packed_all,
         [vmem_spec] * groups,
-        [jax.ShapeDtypeStruct((terms, groups * docs), jnp.float32)],
-        scratch=[pltpu.VMEM((-(-groups * docs // 8) * 8, -(-columns // LANES) * LANES), jnp.float32)],
+        [jax.ShapeDtypeStruct((terms, 2 * groups * docs), jnp.float32)],
+        scratch=[pltpu.VMEM((-(-2 * groups * docs // 8) * 8, -(-columns // LANES) * LANES), jnp.float32)],
     )
     features_all = other_groups(features)
 
@@ -407,14 +426,14 @@
             return
         previous = [] if grad_head is None else [grad_head]
         start = next_range
-        term_spec = pl.BlockSpec((head_terms, groups * docs), lambda r, d: (start + r, 0))
+        term_spec = pl.BlockSpec((head_terms, 2 * groups * docs), lambda r, d: (start + r, 0))
         grad_head, token = run(
             functools.partial(head_kernel, groups, docs),
             "head_terms",
-            [margin_all, *features_all, places_all, grads_all, *previous],
+            [margin_all, *features_all, head_columns, *previous],
             [index_spec]
             + [pl.BlockSpec((chunks, tokens, width), lambda r, d: (0, 0, d))] * groups
-            + [term_spec] * 2
+            + [term_spec]
             + [any_spec] * len(previous),
             [jax.ShapeDtypeStruct((terms, depth), jnp.float32), jax.ShapeDtypeStruct((8, LANES), jnp.float32)],
             out_specs=[
@@ -423,7 +442,7 @@
             ],
             waits=waits,
             flops=count * 2 * groups * tokens * head_terms * depth // 4,
-            aliases={3 + groups: 0} if previous else {},
+            aliases={2 + groups: 0} if previous else {},
             scratch=[pltpu.VMEM((head_terms, groups * tokens), jnp.bfloat16)],
             grid=(count, strips),
         )
@@ -442,6 +461,7 @@
             [spec for c in members for spec in strip_specs(c)] + [row_spec, row_spec],
             [bf16(*pair_shape)] * inner,
             out_specs=[pl.BlockSpec(pair_shape, lambda v: (0,) * 6)] * inner,
+            waits=[packed] if pairs else [],
             flops=2 * tokens * lanes * terms // 4,
             scratch=[pltpu.VMEM((tokens, columns), jnp.bfloat16), pltpu.VMEM((tokens, lanes), jnp.float32)],
             grid=(steps,),

time: 221 us -> 191 us (0.86)
  waiting for transfers between devices: 40.4 us -> 21.7 us
  Pallas kernels: 111 us -> 103 us
  local copies, waits for them, and re-layouts: 10.1 us -> 6.67 us
    ppermute x15, waiting for transfers between devices: 33.9 us -> 6.71 us  [the longest x12 4.15 us: around_ring(): return lax.ppermute(value, 'vocab', perm)]
    pallas_call x27 -> x26, Pallas kernels: 111 us -> 103 us  [run(): pl.pallas_call(waiting(kernel, len(waits)), grid=grid, in_specs=[index_sp...]
    ppermute x4, waiting for transfers between devices: 2.05 us -> 7.46 us  [on_device(): lax.ppermute(sends[s - 1], 'seq', shift_perm(slots, -s))]
    ppermute x15, starting transfers between devices: 24.4 us -> 28.6 us  [the longest x12 24.9 us: around_ring(): return lax.ppermute(value, 'vocab', perm)]
    unnamed x24 -> x18, local copies, waits for them, and re-layouts: 7.08 us -> 3.37 us
    ppermute x1, waiting for transfers between devices: 0.01 us -> 3.2 us  [on_device(): logits = logits + lax.ppermute(logit_part, 'seq', shift_perm(slots, s))]
    ppermute x4 -> x2, waiting for transfers between devices: 2.81 us -> 0.01 us  [other_groups(): lax.ppermute(value, 'dp', shift_perm(groups, -g))]
    ppermute x6, waiting for transfers between devices: 1.61 us -> 4.34 us  [across_y(): return lax.ppermute(value, 'vocab', perm)]
  transfers between devices with their start and end apart: 39 -> 37, of which waited for: 12 -> 10; matrix products, arithmetic and copies ran while one was open for 3% -> 3% of each run, Pallas kernels for 46% -> 49%
where the time goes in v2:
time: 191 us; the launch traced here: 190 us
  Pallas kernels  103 us (54%)
  starting transfers between devices  51.6 us (27%)
  waiting for transfers between devices  21.7 us (11%)
  local copies, waits for them, and re-layouts  6.67 us (3%)
  other arithmetic  3.67 us (2%)
  between operations  3.57 us (2%)
    pallas_call x26, Pallas kernels, run(): pl.pallas_call(waiting(kernel, len(waits)), grid=grid, in_specs=[index_sp...  103 us
    ppermute x12, starting transfers between devices, around_ring(): return lax.ppermute(value, 'vocab', perm)  24.9 us
    ppermute x6, starting transfers between devices, across_z(): return lax.ppermute(value, 'vocab', perm)  8.83 us
    ppermute x4, waiting for transfers between devices, on_device(): lax.ppermute(sends[s - 1], 'seq', shift_perm(slots, -s))  7.46 us
    ppermute x6, starting transfers between devices, across_y(): return lax.ppermute(value, 'vocab', perm)  6.78 us
    ppermute x6, waiting for transfers between devices, across_y(): return lax.ppermute(value, 'vocab', perm)  4.34 us
    ppermute x4, starting transfers between devices, on_device(): lax.ppermute(sends[s - 1], 'seq', shift_perm(slots, -s))  4.3 us
    ppermute x12, waiting for transfers between devices, around_ring(): return lax.ppermute(value, 'vocab', perm)  4.15 us
  transfers between devices with their start and end apart: 37, of which 10 were waited for; matrix products, arithmetic and copies ran while one was open for 3% of the time, Pallas kernels for 49%

profile of v2, /device:TPU:0, one launch (start us, length us, event | category | flops | bytes accessed | tf_op | source)
XLA Modules:
  0.0 190.5 jit_solution(4914155676848159024)
XLA Ops:
  0.6 1.1 fusion.12
  1.7 3.1 %collective-permute-start.1 = (bf16[3,128,128]{2,1,0:T(8,128)(2,1)S(1)}, bf16[3,128,128]{2,1,0:T(8,128)(2,1)S(1)}, u32[]{:S(2)}, u32[]{:S(2)}) collective-permute-start(bf16[3,128,128]{2,1,0:T(8,128)(2,1)S(1)} %get-tuple-element.84.refs_1_), channel_id=1, source_target_pairs={{0,2},{1,3},{2,6},{3,7},{6,4},{7,5},{4,0},{5,1},{8,10},{9,11},{10,... | collective-permute-start | bytes 294920 | tf_op jit(solution)/shard_map/ppermute | solution.py:247
  4.9 3.7 %collective-permute-done.1.refs_2_.refs_1_ = bf16[3,128,128]{2,1,0:T(8,128)(2,1)S(1)} collective-permute-done((bf16[3,128,128]{2,1,0:T(8,128)(2,1)S(1)}, bf16[3,128,128]{2,1,0:T(8,128)(2,1)S(1)}, u32[]{:S(2)}, u32[]{:S(2)}) %collective-permute-start.1) | collective-permute-done | bytes 98336 | tf_op jit(solution)/shard_map/ppermute | solution.py:247
  9.1 1.0 collective-permute-start.6
  10.2 1.9 %collective-permute-start.3 = (bf16[3,128,128]{2,1,0:T(8,128)(2,1)S(1)}, bf16[3,128,128]{2,1,0:T(8,128)(2,1)S(1)}, u32[]{:S(2)}, u32[]{:S(2)}) collective-permute-start(bf16[3,128,128]{2,1,0:T(8,128)(2,1)S(1)} %get-tuple-element.84.refs_1_), channel_id=1, source_target_pairs={{0,4},{1,5},{2,0},{3,1},{6,2},{7,3},{4,6},{5,7},{8,12},{9,13},{10,... | collective-permute-start | bytes 294920 | tf_op jit(solution)/shard_map/ppermute | solution.py:247
  12.1 3.7 %collective-permute-start.2 = (bf16[3,128,128]{2,1,0:T(8,128)(2,1)S(1)}, bf16[3,128,128]{2,1,0:T(8,128)(2,1)S(1)}, u32[]{:S(2)}, u32[]{:S(2)}) collective-permute-start(bf16[3,128,128]{2,1,0:T(8,128)(2,1)S(1)} %get-tuple-element.84.refs_1_), channel_id=1, source_target_pairs={{0,6},{1,7},{2,4},{3,5},{6,0},{7,1},{4,2},{5,3},{8,14},{9,15},{10,... | collective-permute-start | bytes 294920 | tf_op jit(solution)/shard_map/ppermute | solution.py:247
  16.8 3.5 %collective-permute-start.10 = (bf16[3,128,128]{2,1,0:T(8,128)(2,1)S(1)}, bf16[3,128,128]{2,1,0:T(8,128)(2,1)S(1)}, u32[]{:S(2)}, u32[]{:S(2)}) collective-permute-start(bf16[3,128,128]{2,1,0:T(8,128)(2,1)S(1)} %feature_chunk.4.refs_2_), channel_id=1, source_target_pairs={{0,2},{1,3},{2,6},{3,7},{6,4},{7,5},{4,0},{5,1},{8,10},{9,11},{10,... | collective-permute-start | bytes 294920 | tf_op jit(solution)/shard_map/ppermute | solution.py:247
  20.3 3.7 %collective-permute-start.7 = (bf16[3,128,128]{2,1,0:T(8,128)(2,1)S(1)}, bf16[3,128,128]{2,1,0:T(8,128)(2,1)S(1)}, u32[]{:S(2)}, u32[]{:S(2)}) collective-permute-start(bf16[3,128,128]{2,1,0:T(8,128)(2,1)S(1)} %collective-permute-done.6.refs_3_.refs_1_), channel_id=1, source_target_pairs={{0,2},{1,3},{2,6},{3,7},{6,4},{7,5},{4,0},{5,1},{8,10},{9,11},{10,... | collective-permute-start | bytes 294920 | tf_op jit(solution)/shard_map/ppermute | solution.py:247
  24.0 0.7 pick_halves.4
  24.7 1.3 collective-permute-start.4
  26.0 1.2 collective-permute-start.11
  27.2 3.4 %collective-permute-start.8 = (bf16[3,128,128]{2,1,0:T(8,128)(2,1)S(1)}, bf16[3,128,128]{2,1,0:T(8,128)(2,1)S(1)}, u32[]{:S(2)}, u32[]{:S(2)}) collective-permute-start(bf16[3,128,128]{2,1,0:T(8,128)(2,1)S(1)} %collective-permute-done.7.refs_4_), channel_id=1, source_target_pairs={{0,2},{1,3},{2,6},{3,7},{6,4},{7,5},{4,0},{5,1},{8,10},{9,11},{10,... | collective-permute-start | bytes 294920 | tf_op jit(solution)/shard_map/ppermute | solution.py:247
  30.6 0.8 convert_reduce_fusion
  31.4 1.2 collective-permute-start
  32.5 0.9 reshape.71
  34.0 2.2 %collective-permute-start.14 = (bf16[3,128,128]{2,1,0:T(8,128)(2,1)S(1)}, bf16[3,128,128]{2,1,0:T(8,128)(2,1)S(1)}, u32[]{:S(2)}, u32[]{:S(2)}) collective-permute-start(bf16[3,128,128]{2,1,0:T(8,128)(2,1)S(1)} %feature_chunk.5.refs_2_), channel_id=1, source_target_pairs={{0,2},{1,3},{2,6},{3,7},{6,4},{7,5},{4,0},{5,1},{8,10},{9,11},{10,... | collective-permute-start | bytes 294920 | tf_op jit(solution)/shard_map/ppermute | solution.py:247
  36.8 1.6 collective-permute-start.5
  38.4 0.7 pick_halves.5
  39.7 1.1 collective-permute-start.15
  40.8 4.0 %collective-permute-done.9.refs_2_ = bf16[2,3,128,128]{3,2,1,0:T(8,128)(2,1)S(1)} collective-permute-done((bf16[2,3,128,128]{3,2,1,0:T(8,128)(2,1)S(1)}, bf16[2,3,128,128]{3,2,1,0:T(8,128)(2,1)S(1)}, u32[]{:S(2)}, u32[]{:S(2)}) %collective-permute-start.9) | collective-permute-done | bytes 196640 | tf_op jit(solution)/shard_map/ppermute | solution.py:355
  45.4 0.7 pick_halves.6
  46.0 1.4 collective-permute-start.13
  47.5 0.6 collective-permute-start.18
  48.3 3.5 %collective-permute-done.13.refs_3_ = bf16[2,3,128,128]{3,2,1,0:T(8,128)(2,1)S(1)} collective-permute-done((bf16[2,3,128,128]{3,2,1,0:T(8,128)(2,1)S(1)}, bf16[2,3,128,128]{3,2,1,0:T(8,128)(2,1)S(1)}, u32[]{:S(2)}, u32[]{:S(2)}) %collective-permute-start.13) | collective-permute-done | bytes 196640 | tf_op jit(solution)/shard_map/ppermute | solution.py:355
  52.4 0.9 collective-permute-start.17
  53.3 0.9 pick_halves.7
  54.2 1.1 collective-permute-start.19
  55.3 5.5 %pooled_logits.4 = (f32[2,3,2000]{2,1,0:T(4,128)S(1)}, bf16[4,768,512]{2,1,0:T(8,128)(2,1)S(1)}) custom-call(s32[4]{0:T(128)S(1)} %pad_add_fusion.refs_0_, bf16[2,3,128,128]{3,2,1,0:T(8,128)(2,1)S(1)} %get-tuple-element.46.refs_1_.refs_3_, bf16[2,2,3,128,128]{4,3,2,1,0:T(8,128)(2,1)S(1)} %join_tokens.4.refs_1_.refs_2_, ...), custom_call_target="tpu_custom_call" | custom-call | flops 3145728000 | bytes 49152000 | tf_op jit(solution)/shard_map/pooled_logits/pallas_call | solution.py:289
  61.3 1.6 collective-permute-start.20
  62.9 2.8 %collective-permute-done.17.refs_2_ = bf16[2,2,3,128,128]{4,3,2,1,0:T(8,128)(2,1)S(1)} collective-permute-done((bf16[2,2,3,128,128]{4,3,2,1,0:T(8,128)(2,1)S(1)}, bf16[2,2,3,128,128]{4,3,2,1,0:T(8,128)(2,1)S(1)}, u32[]{:S(2)}, u32[]{:S(2)}) %collective-permute-start.17) | collective-permute-done | bytes 393248 | tf_op jit(solution)/shard_map/ppermute | solution.py:237
  65.7 5.5 %pooled_logits.5 = (f32[2,3,2000]{2,1,0:T(4,128)S(1)}, bf16[4,768,512]{2,1,0:T(8,128)(2,1)S(1)}) custom-call(s32[4]{0:T(128)S(1)} %pad_add_fusion.refs_0_, f32[2,3,2000]{2,1,0:T(4,128)S(1)} %get-tuple-element.80.refs_1_, bf16[2,2,3,128,128]{4,3,2,1,0:T(8,128)(2,1)S(1)} %collective-permute-done.17.refs_2_, ...), custom_call_target="tpu_custom_call", output_to_operand_aliasing={{1}: (10, {})} | custom-call | flops 3145728000 | bytes 49152000 | tf_op jit(solution)/shard_map/pooled_logits/pallas_call | solution.py:289
  71.1 5.5 %pooled_logits.6 = (f32[2,3,2000]{2,1,0:T(4,128)S(1)}, bf16[4,768,512]{2,1,0:T(8,128)(2,1)S(1)}) custom-call(s32[4]{0:T(128)S(1)} %pad_add_fusion.refs_0_, bf16[2,2,3,128,128]{4,3,2,1,0:T(8,128)(2,1)S(1)} %join_tokens.6.refs_1_, bf16[2,2,3,128,128]{4,3,2,1,0:T(8,128)(2,1)S(1)} %collective-permute-done.17.refs_2_, ...), custom_call_target="tpu_custom_call", output_to_operand_aliasing={{1}: (8, {})} | custom-call | flops 3145728000 | bytes 49152000 | tf_op jit(solution)/shard_map/pooled_logits/pallas_call | solution.py:289
  76.6 5.5 %pooled_logits.7 = (f32[2,3,2000]{2,1,0:T(4,128)S(1)}, bf16[4,768,512]{2,1,0:T(8,128)(2,1)S(1)}) custom-call(s32[4]{0:T(128)S(1)} %pad_add_fusion.refs_0_, bf16[2,2,3,128,128]{4,3,2,1,0:T(8,128)(2,1)S(1)} %join_tokens.7.refs_1_, bf16[2,2,3,128,128]{4,3,2,1,0:T(8,128)(2,1)S(1)} %collective-permute-done.20.refs_2_, ...), custom_call_target="tpu_custom_call", output_to_operand_aliasing={{1}: (8, {})} | custom-call | flops 3145728000 | bytes 49152000 | tf_op jit(solution)/shard_map/pooled_logits/pallas_call | solution.py:289
  82.3 0.7 collective-permute-start.21
  83.6 3.2 %collective-permute-done.21 = f32[2,3,2000]{2,1,0:T(4,128)S(1)} collective-permute-done((f32[2,3,2000]{2,1,0:T(4,128)S(1)}, f32[2,3,2000]{2,1,0:T(4,128)S(1)}, u32[]{:S(2)}, u32[]{:S(2)}) %collective-permute-start.21) | collective-permute-done | bytes 48032 | tf_op jit(solution)/shard_map/ppermute | solution.py:374
  87.0 0.7 multiply_reduce_fusion
  88.9 2.9 %collective-permute-start.23 = (f32[1]{0:T(128)}, f32[1]{0:T(128)}, u32[]{:S(2)}, u32[]{:S(2)}) collective-permute-start(f32[1]{0:T(128)} %bitcast.11), channel_id=1, source_target_pairs={{0,1},{1,0},{2,3},{3,2},{4,5},{5,4},{6,7},{7,6},{8,9},{9,8},{10,11... | collective-permute-start | bytes 20 | tf_op jit(solution)/shard_map/ppermute | solution.py:388
  92.0 10.2 %hidden_terms.2 = (bf16[2,2,2,3,128,128]{5,4,3,2,1,0:T(8,128)(2,1)S(1)}, bf16[2,2,2,3,128,128]{5,4,3,2,1,0:T(8,128)(2,1)S(1)}) custom-call(s32[4]{0:T(128)S(1)} %pad_add_fusion.refs_0_, bf16[4000,2048]{1,0:T(8,128)(2,1)} %bitcast.60, bf16[4000,2048]{1,0:T(8,128)(2,1)} %bitcast.61, bf16[4000,2048]{1,0:T(8,128)(2,1)} %bitcast.62, bf16[4000,2048]{1,0:T(8,128)(2,1)} %bitcast.63, ...), custom_call_target="tpu_custom_call" | custom-call | flops 1572864000 | bytes 24576000 | tf_op jit(solution)/shard_map/hidden_terms/pallas_call | solution.py:289
  103.6 10.4 %hidden_terms.3 = (bf16[2,2,2,3,128,128]{5,4,3,2,1,0:T(8,128)(2,1)S(1)}, bf16[2,2,2,3,128,128]{5,4,3,2,1,0:T(8,128)(2,1)S(1)}) custom-call(s32[4]{0:T(128)S(1)} %pad_add_fusion.refs_0_, f32[2,7,2000]{2,1,0:T(8,128)S(1)} %pad_maximum_fusion.refs_1_, bf16[4000,2048]{1,0:T(8,128)(2,1)} %bitcast.68, bf16[4000,2048]{1,0:T(8,128)(2,1)} %bitcast.69, ...), custom_call_target="tpu_custom_call" | custom-call | flops 1572864000 | bytes 24576000 | tf_op jit(solution)/shard_map/hidden_terms/pallas_call | solution.py:289
  114.0 1.6 collective-permute-start.29
  116.2 0.7 pad_maximum_fusion.1
  117.0 1.3 turn_gradients.1.refs_6_.refs_5_
  118.3 0.6 pad_maximum_fusion.2
  118.9 1.6 collective-permute-done.25
  120.6 0.8 collective-permute-start.26
  121.4 1.4 collective-permute-done.22.refs_2_
  122.7 0.7 add_blocks.2
  124.0 1.0 collective-permute-done.26
  125.1 18.4 %head_terms.3 = (f32[4000,2048]{1,0:T(8,128)}, f32[8,128]{1,0:T(8,128)S(1)}) custom-call(s32[4]{0:T(128)S(1)} %pad_add_fusion.refs_0_, bf16[2,2,3,128,128]{4,3,2,1,0:T(8,128)(2,1)S(1)} %get-tuple-element.57.refs_1_.refs_2_, bf16[2,2,2,3,128,128]{5,4,3,2,1,0:T(8,128)(2,1)S(1)} %get-tuple-element.58.refs_2_, f32[2]{0:T(128)S(1)} %bitcast.41, ...), custom_call_target="tpu_custom_call" | custom-call | flops 2516582400 | bytes 39321600 | tf_op jit(solution)/shard_map/head_terms/pallas_call | solution.py:289
  143.5 1.4 sort_pieces.2
  144.9 1.4 add_blocks.3
  146.3 0.8 copy-done.5
  148.0 0.6 constant_dynamic-slice_fusion
  148.6 0.8 collective-permute-start.32
  149.5 2.6 %collective-permute-start.33 = (bf16[2,3,128,128]{3,2,1,0:T(8,128)(2,1)}, bf16[2,3,128,128]{3,2,1,0:T(8,128)(2,1)S(1)}, u32[]{:S(2)}, u32[]{:S(2)}) collective-permute-start(bf16[2,3,128,128]{3,2,1,0:T(8,128)(2,1)} %copy-done.7), channel_id=1, source_target_pairs={{0,6},{1,7},{2,0},{3,1},{4,2},{5,3},{6,4},{7,5},{8,14},{9,15},{10,... | collective-permute-start | bytes 589832 | tf_op jit(solution)/shard_map/ppermute | solution.py:251
  152.1 1.6 copy-done.3
  153.7 1.0 copy-done.6
  154.7 9.9 %head_terms.4 = (f32[4000,2048]{1,0:T(8,128)}, f32[8,128]{1,0:T(8,128)S(1)}) custom-call(s32[4]{0:T(128)S(1)} %pad_add_fusion.refs_0_, bf16[2,3,128,128]{3,2,1,0:T(8,128)(2,1)S(1)} %get-tuple-element.62.refs_1_.refs_3_, bf16[2,2,3,128,128]{4,3,2,1,0:T(8,128)(2,1)S(1)} %copy-done.6, f32[2]{0:T(128)S(1)} %bitcast.42, ...), custom_call_target="tpu_custom_call", output_to_operand_aliasing={{0}: (7, {})} | custom-call | flops 1258291200 | bytes 19660800 | tf_op jit(solution)/shard_map/head_terms/pallas_call | solution.py:289
  164.6 1.1 sort_pieces.3
  165.8 0.6 collective-permute-start.34
  166.4 1.5 collective-permute-start.35
  167.9 2.8 %collective-permute-start.36 = (bf16[2,3,128,128]{3,2,1,0:T(8,128)(2,1)S(1)}, bf16[2,3,128,128]{3,2,1,0:T(8,128)(2,1)S(1)}, u32[]{:S(2)}, u32[]{:S(2)}) collective-permute-start(bf16[2,3,128,128]{3,2,1,0:T(8,128)(2,1)S(1)} %get-tuple-element.77), channel_id=1, source_target_pairs={{0,6},{1,7},{2,0},{3,1},{4,2},{5,3},{6,4},{7,5},{8,14},{9,15},{10,... | collective-permute-start | bytes 589832 | tf_op jit(solution)/shard_map/ppermute | solution.py:251
  170.8 17.5 %head_terms.5 = (f32[4000,2048]{1,0:T(8,128)}, f32[8,128]{1,0:T(8,128)S(1)}) custom-call(s32[4]{0:T(128)S(1)} %pad_add_fusion.refs_0_, bf16[2,3,128,128]{3,2,1,0:T(8,128)(2,1)S(1)} %get-tuple-element.68.refs_1_.refs_7_, f32[2]{0:T(128)S(1)} %bitcast.43, bf16[4,768,512]{2,1,0:T(8,128)(2,1)S(1)} %copy-done.1, ...), custom_call_target="tpu_custom_call", output_to_operand_aliasing={{0}: (6, {})} | custom-call | flops 2516582400 | bytes 39321600 | tf_op jit(solution)/shard_map/head_terms/pallas_call | solution.py:289
  188.3 2.2 %scale_hidden.1 = bf16[3,128,512]{2,1,0:T(8,128)(2,1)} custom-call(s32[4]{0:T(128)S(1)} %pad_add_fusion.refs_0_, f32[8,128]{1,0:T(8,128)S(1)} %get-tuple-element.71.refs_1_, f32[1]{0:T(128)} %bitcast.20.refs_2_, bf16[2,3,128,128]{3,2,1,0:T(8,128)(2,1)S(1)} %get-tuple-element.62.refs_1_.refs_3_, bf16[2,3,128,128]{3,2,1,0:T(8,128)(2,1)S(1)} %collective-permute-done.31.refs_4_, ...), custom_call_target="tpu_custom_call" | custom-call | tf_op jit(solution)/shard_map/scale_hidden/pallas_call | solution.py:289
  (75 shorter events, 9.0 us)
Async XLA Ops:
  1.7 6.9 %collective-permute-start.1 = (bf16[3,128,128]{2,1,0:T(8,128)(2,1)S(1)}, bf16[3,128,128]{2,1,0:T(8,128)(2,1)S(1)}, u32[]{:S(2)}, u32[]{:S(2)}) collective-permute-start(bf16[3,128,128]{2,1,0:T(8,128)(2,1)S(1)} %get-tuple-element.84.refs_1_), channel_id=1, source_target_pairs={{0,2},{1,3},{2,6},{3,7},{6,4},{7,5},{4,0},{5,1},{8,10},{9,11},{10,... | collective-permute-start | bytes 294920 | tf_op jit(solution)/shard_map/ppermute | solution.py:247
  9.1 7.1 %collective-permute-start.6 = (bf16[3,128,128]{2,1,0:T(8,128)(2,1)S(1)}, bf16[3,128,128]{2,1,0:T(8,128)(2,1)S(1)}, u32[]{:S(2)}, u32[]{:S(2)}) collective-permute-start(bf16[3,128,128]{2,1,0:T(8,128)(2,1)S(1)} %feature_chunk.3.refs_2_), channel_id=1, source_target_pairs={{0,2},{1,3},{2,6},{3,7},{6,4},{7,5},{4,0},{5,1},{8,10},{9,11},{10,... | collective-permute-start | bytes 294920 | tf_op jit(solution)/shard_map/ppermute | solution.py:247
  10.2 13.8 %collective-permute-start.3 = (bf16[3,128,128]{2,1,0:T(8,128)(2,1)S(1)}, bf16[3,128,128]{2,1,0:T(8,128)(2,1)S(1)}, u32[]{:S(2)}, u32[]{:S(2)}) collective-permute-start(bf16[3,128,128]{2,1,0:T(8,128)(2,1)S(1)} %get-tuple-element.84.refs_1_), channel_id=1, source_target_pairs={{0,4},{1,5},{2,0},{3,1},{6,2},{7,3},{4,6},{5,7},{8,12},{9,13},{10,... | collective-permute-start | bytes 294920 | tf_op jit(solution)/shard_map/ppermute | solution.py:247
  12.1 11.9 %collective-permute-start.2 = (bf16[3,128,128]{2,1,0:T(8,128)(2,1)S(1)}, bf16[3,128,128]{2,1,0:T(8,128)(2,1)S(1)}, u32[]{:S(2)}, u32[]{:S(2)}) collective-permute-start(bf16[3,128,128]{2,1,0:T(8,128)(2,1)S(1)} %get-tuple-element.84.refs_1_), channel_id=1, source_target_pairs={{0,6},{1,7},{2,4},{3,5},{6,0},{7,1},{4,2},{5,3},{8,14},{9,15},{10,... | collective-permute-start | bytes 294920 | tf_op jit(solution)/shard_map/ppermute | solution.py:247
  16.8 9.2 %collective-permute-start.10 = (bf16[3,128,128]{2,1,0:T(8,128)(2,1)S(1)}, bf16[3,128,128]{2,1,0:T(8,128)(2,1)S(1)}, u32[]{:S(2)}, u32[]{:S(2)}) collective-permute-start(bf16[3,128,128]{2,1,0:T(8,128)(2,1)S(1)} %feature_chunk.4.refs_2_), channel_id=1, source_target_pairs={{0,2},{1,3},{2,6},{3,7},{6,4},{7,5},{4,0},{5,1},{8,10},{9,11},{10,... | collective-permute-start | bytes 294920 | tf_op jit(solution)/shard_map/ppermute | solution.py:247
  20.3 6.9 %collective-permute-start.7 = (bf16[3,128,128]{2,1,0:T(8,128)(2,1)S(1)}, bf16[3,128,128]{2,1,0:T(8,128)(2,1)S(1)}, u32[]{:S(2)}, u32[]{:S(2)}) collective-permute-start(bf16[3,128,128]{2,1,0:T(8,128)(2,1)S(1)} %collective-permute-done.6.refs_3_.refs_1_), channel_id=1, source_target_pairs={{0,2},{1,3},{2,6},{3,7},{6,4},{7,5},{4,0},{5,1},{8,10},{9,11},{10,... | collective-permute-start | bytes 294920 | tf_op jit(solution)/shard_map/ppermute | solution.py:247
  24.7 11.5 %collective-permute-start.4 = (bf16[2,3,128,128]{3,2,1,0:T(8,128)(2,1)S(1)}, bf16[2,3,128,128]{3,2,1,0:T(8,128)(2,1)S(1)}, u32[]{:S(2)}, u32[]{:S(2)}) collective-permute-start(bf16[2,3,128,128]{3,2,1,0:T(8,128)(2,1)S(1)} %get-tuple-element.41), channel_id=1, source_target_pairs={{0,8},{8,0},{1,9},{9,1},{2,10},{10,2},{3,11},{11,3},{4,12},{12,4},... | collective-permute-start | bytes 589832 | tf_op jit(solution)/shard_map/ppermute | solution.py:355
  26.0 13.7 %collective-permute-start.11 = (bf16[3,128,128]{2,1,0:T(8,128)(2,1)S(1)}, bf16[3,128,128]{2,1,0:T(8,128)(2,1)S(1)}, u32[]{:S(2)}, u32[]{:S(2)}) collective-permute-start(bf16[3,128,128]{2,1,0:T(8,128)(2,1)S(1)} %collective-permute-done.10.refs_3_.refs_1_), channel_id=1, source_target_pairs={{0,2},{1,3},{2,6},{3,7},{6,4},{7,5},{4,0},{5,1},{8,10},{9,11},{10,... | collective-permute-start | bytes 294920 | tf_op jit(solution)/shard_map/ppermute | solution.py:247
  27.2 11.2 %collective-permute-start.8 = (bf16[3,128,128]{2,1,0:T(8,128)(2,1)S(1)}, bf16[3,128,128]{2,1,0:T(8,128)(2,1)S(1)}, u32[]{:S(2)}, u32[]{:S(2)}) collective-permute-start(bf16[3,128,128]{2,1,0:T(8,128)(2,1)S(1)} %collective-permute-done.7.refs_4_), channel_id=1, source_target_pairs={{0,2},{1,3},{2,6},{3,7},{6,4},{7,5},{4,0},{5,1},{8,10},{9,11},{10,... | collective-permute-start | bytes 294920 | tf_op jit(solution)/shard_map/ppermute | solution.py:247
  31.4 16.0 %collective-permute-start = (s32[3,1]{0,1:T(1,128)S(1)}, s32[3,1]{0,1:T(1,128)S(1)}, u32[]{:S(2)}, u32[]{:S(2)}) collective-permute-start(s32[3,1]{0,1:T(1,128)S(1)} %bitcast.77), channel_id=1, source_target_pairs={{0,8},{8,0},{1,9},{9,1},{2,10},{10,2},{3,11},{11,3},{4,12},{12,4},... | collective-permute-start | bytes 44 | tf_op jit(solution)/shard_map/ppermute | solution.py:284
  34.0 5.7 %collective-permute-start.14 = (bf16[3,128,128]{2,1,0:T(8,128)(2,1)S(1)}, bf16[3,128,128]{2,1,0:T(8,128)(2,1)S(1)}, u32[]{:S(2)}, u32[]{:S(2)}) collective-permute-start(bf16[3,128,128]{2,1,0:T(8,128)(2,1)S(1)} %feature_chunk.5.refs_2_), channel_id=1, source_target_pairs={{0,2},{1,3},{2,6},{3,7},{6,4},{7,5},{4,0},{5,1},{8,10},{9,11},{10,... | collective-permute-start | bytes 294920 | tf_op jit(solution)/shard_map/ppermute | solution.py:247
  36.8 11.5 %collective-permute-start.5 = (bf16[2,2,3,128,128]{4,3,2,1,0:T(8,128)(2,1)S(1)}, bf16[2,2,3,128,128]{4,3,2,1,0:T(8,128)(2,1)S(1)}, u32[]{:S(2)}, u32[]{:S(2)}) collective-permute-start(bf16[2,2,3,128,128]{4,3,2,1,0:T(8,128)(2,1)S(1)} %join_tokens.4.refs_1_.refs_2_), channel_id=1, source_target_pairs={{0,1},{1,0},{2,3},{3,2},{4,5},{5,4},{6,7},{7,6},{8,9},{9,8},{10,11... | collective-permute-start | bytes 1179656 | tf_op jit(solution)/shard_map/ppermute | solution.py:237
  39.0 5.7 %collective-permute-start.9 = (bf16[2,3,128,128]{3,2,1,0:T(8,128)(2,1)S(1)}, bf16[2,3,128,128]{3,2,1,0:T(8,128)(2,1)S(1)}, u32[]{:S(2)}, u32[]{:S(2)}) collective-permute-start(bf16[2,3,128,128]{3,2,1,0:T(8,128)(2,1)S(1)} %get-tuple-element.43), channel_id=1, source_target_pairs={{0,8},{8,0},{1,9},{9,1},{2,10},{10,2},{3,11},{11,3},{4,12},{12,4},... | collective-permute-start | bytes 589832 | tf_op jit(solution)/shard_map/ppermute | solution.py:355
  39.6 5.7 %collective-permute-start.12 = (bf16[3,128,128]{2,1,0:T(8,128)(2,1)S(1)}, bf16[3,128,128]{2,1,0:T(8,128)(2,1)S(1)}, u32[]{:S(2)}, u32[]{:S(2)}) collective-permute-start(bf16[3,128,128]{2,1,0:T(8,128)(2,1)S(1)} %collective-permute-done.11.refs_4_), channel_id=1, source_target_pairs={{0,2},{1,3},{2,6},{3,7},{6,4},{7,5},{4,0},{5,1},{8,10},{9,11},{10,... | collective-permute-start | bytes 294920 | tf_op jit(solution)/shard_map/ppermute | solution.py:247
  39.7 7.7 %collective-permute-start.15 = (bf16[3,128,128]{2,1,0:T(8,128)(2,1)S(1)}, bf16[3,128,128]{2,1,0:T(8,128)(2,1)S(1)}, u32[]{:S(2)}, u32[]{:S(2)}) collective-permute-start(bf16[3,128,128]{2,1,0:T(8,128)(2,1)S(1)} %collective-permute-done.14.refs_3_), channel_id=1, source_target_pairs={{0,2},{1,3},{2,6},{3,7},{6,4},{7,5},{4,0},{5,1},{8,10},{9,11},{10,... | collective-permute-start | bytes 294920 | tf_op jit(solution)/shard_map/ppermute | solution.py:247
  46.0 5.7 %collective-permute-start.13 = (bf16[2,3,128,128]{3,2,1,0:T(8,128)(2,1)S(1)}, bf16[2,3,128,128]{3,2,1,0:T(8,128)(2,1)S(1)}, u32[]{:S(2)}, u32[]{:S(2)}) collective-permute-start(bf16[2,3,128,128]{3,2,1,0:T(8,128)(2,1)S(1)} %get-tuple-element.45), channel_id=1, source_target_pairs={{0,8},{8,0},{1,9},{9,1},{2,10},{10,2},{3,11},{11,3},{4,12},{12,4},... | collective-permute-start | bytes 589832 | tf_op jit(solution)/shard_map/ppermute | solution.py:355
  47.4 5.9 %collective-permute-start.16 = (bf16[3,128,128]{2,1,0:T(8,128)(2,1)S(1)}, bf16[3,128,128]{2,1,0:T(8,128)(2,1)S(1)}, u32[]{:S(2)}, u32[]{:S(2)}) collective-permute-start(bf16[3,128,128]{2,1,0:T(8,128)(2,1)S(1)} %collective-permute-done.15.refs_4_), channel_id=1, source_target_pairs={{0,2},{1,3},{2,6},{3,7},{6,4},{7,5},{4,0},{5,1},{8,10},{9,11},{10,... | collective-permute-start | bytes 294920 | tf_op jit(solution)/shard_map/ppermute | solution.py:247
  47.5 13.2 %collective-permute-start.18 = (bf16[2,2,3,128,128]{4,3,2,1,0:T(8,128)(2,1)S(1)}, bf16[2,2,3,128,128]{4,3,2,1,0:T(8,128)(2,1)S(1)}, u32[]{:S(2)}, u32[]{:S(2)}) collective-permute-start(bf16[2,2,3,128,128]{4,3,2,1,0:T(8,128)(2,1)S(1)} %join_tokens.5.refs_1_.refs_3_), channel_id=1, source_target_pairs={{0,1},{1,0},{2,3},{3,2},{4,5},{5,4},{6,7},{7,6},{8,9},{9,8},{10,11... | collective-permute-start | bytes 1179656 | tf_op jit(solution)/shard_map/ppermute | solution.py:237
  52.4 13.3 %collective-permute-start.17 = (bf16[2,2,3,128,128]{4,3,2,1,0:T(8,128)(2,1)S(1)}, bf16[2,2,3,128,128]{4,3,2,1,0:T(8,128)(2,1)S(1)}, u32[]{:S(2)}, u32[]{:S(2)}) collective-permute-start(bf16[2,2,3,128,128]{4,3,2,1,0:T(8,128)(2,1)S(1)} %join_tokens.6.refs_1_), channel_id=1, source_target_pairs={{0,1},{1,0},{2,3},{3,2},{4,5},{5,4},{6,7},{7,6},{8,9},{9,8},{10,11... | collective-permute-start | bytes 1179656 | tf_op jit(solution)/shard_map/ppermute | solution.py:237
  54.2 6.6 %collective-permute-start.19 = (bf16[2,3,128,128]{3,2,1,0:T(8,128)(2,1)S(1)}, bf16[2,3,128,128]{3,2,1,0:T(8,128)(2,1)S(1)}, u32[]{:S(2)}, u32[]{:S(2)}) collective-permute-start(bf16[2,3,128,128]{3,2,1,0:T(8,128)(2,1)S(1)} %get-tuple-element.52), channel_id=1, source_target_pairs={{0,8},{8,0},{1,9},{9,1},{2,10},{10,2},{3,11},{11,3},{4,12},{12,4},... | collective-permute-start | bytes 589832 | tf_op jit(solution)/shard_map/ppermute | solution.py:355
  61.3 15.3 %collective-permute-start.20 = (bf16[2,2,3,128,128]{4,3,2,1,0:T(8,128)(2,1)S(1)}, bf16[2,2,3,128,128]{4,3,2,1,0:T(8,128)(2,1)S(1)}, u32[]{:S(2)}, u32[]{:S(2)}) collective-permute-start(bf16[2,2,3,128,128]{4,3,2,1,0:T(8,128)(2,1)S(1)} %join_tokens.7.refs_1_), channel_id=1, source_target_pairs={{0,1},{1,0},{2,3},{3,2},{4,5},{5,4},{6,7},{7,6},{8,9},{9,8},{10,11... | collective-permute-start | bytes 1179656 | tf_op jit(solution)/shard_map/ppermute | solution.py:237
  82.1 20.0 %copy-start = (bf16[4,768,512]{2,1,0:T(8,128)(2,1)}, bf16[4,768,512]{2,1,0:T(8,128)(2,1)S(1)}, u32[]{:S(2)}) copy-start(bf16[4,768,512]{2,1,0:T(8,128)(2,1)S(1)} %get-tuple-element.59.refs_4_.refs_3_) | copy-start | bytes 9437188
  82.1 42.9 %collective-permute-start.27 = (bf16[4,768,512]{2,1,0:T(8,128)(2,1)S(1)}, bf16[4,768,512]{2,1,0:T(8,128)(2,1)}, u32[]{:S(2)}, u32[]{:S(2)}) collective-permute-start(bf16[4,768,512]{2,1,0:T(8,128)(2,1)S(1)} %get-tuple-element.59.refs_4_.refs_3_), channel_id=1, source_target_pairs={{0,16},{16,0},{1,17},{17,1},{2,18},{18,2},{3,19},{19,3},{4,20},{20... | collective-permute-start | bytes 9437192 | tf_op jit(solution)/shard_map/ppermute | solution.py:254
  82.3 4.6 %collective-permute-start.21 = (f32[2,3,2000]{2,1,0:T(4,128)S(1)}, f32[2,3,2000]{2,1,0:T(4,128)S(1)}, u32[]{:S(2)}, u32[]{:S(2)}) collective-permute-start(f32[2,3,2000]{2,1,0:T(4,128)S(1)} %add_add_fusion), channel_id=1, source_target_pairs={{0,8},{8,0},{1,9},{9,1},{2,10},{10,2},{3,11},{11,3},{4,12},{12,4},... | collective-permute-start | bytes 144008 | tf_op jit(solution)/shard_map/ppermute | solution.py:374
  88.9 13.8 %collective-permute-start.23 = (f32[1]{0:T(128)}, f32[1]{0:T(128)}, u32[]{:S(2)}, u32[]{:S(2)}) collective-permute-start(f32[1]{0:T(128)} %bitcast.11), channel_id=1, source_target_pairs={{0,1},{1,0},{2,3},{3,2},{4,5},{5,4},{6,7},{7,6},{8,9},{9,8},{10,11... | collective-permute-start | bytes 20 | tf_op jit(solution)/shard_map/ppermute | solution.py:388
  102.2 20.5 %collective-permute-start.22 = (bf16[2,2,2,3,128,128]{5,4,3,2,1,0:T(8,128)(2,1)S(1)}, bf16[2,2,2,3,128,128]{5,4,3,2,1,0:T(8,128)(2,1)S(1)}, u32[]{:S(2)}, u32[]{:S(2)}) collective-permute-start(bf16[2,2,2,3,128,128]{5,4,3,2,1,0:T(8,128)(2,1)S(1)} %get-tuple-element.56), channel_id=1, source_target_pairs={{0,1},{1,0},{2,3},{3,2},{4,5},{5,4},{6,7},{7,6},{8,9},{9,8},{10,11... | collective-permute-start | bytes 2359304 | tf_op jit(solution)/shard_map/ppermute | solution.py:237
  103.5 12.1 %collective-permute-start.24 = (f32[2,7,2000]{2,1,0:T(8,128)S(1)}, f32[2,7,2000]{2,1,0:T(8,128)S(1)}, u32[]{:S(2)}, u32[]{:S(2)}) collective-permute-start(f32[2,7,2000]{2,1,0:T(8,128)S(1)} %pad_maximum_fusion.refs_1_), channel_id=1, source_target_pairs={{0,16},{16,0},{1,17},{17,1},{2,18},{18,2},{3,19},{19,3},{4,20},{20... | collective-permute-start | bytes 336008 | tf_op jit(solution)/shard_map/ppermute | solution.py:254
  114.0 31.0 %collective-permute-start.29 = (bf16[2,2,2,3,128,128]{5,4,3,2,1,0:T(8,128)(2,1)S(1)}, bf16[2,2,2,3,128,128]{5,4,3,2,1,0:T(8,128)(2,1)S(1)}, u32[]{:S(2)}, u32[]{:S(2)}) collective-permute-start(bf16[2,2,2,3,128,128]{5,4,3,2,1,0:T(8,128)(2,1)S(1)} %get-tuple-element.63), channel_id=1, source_target_pairs={{0,1},{1,0},{2,3},{3,2},{4,5},{5,4},{6,7},{7,6},{8,9},{9,8},{10,11... | collective-permute-start | bytes 2359304 | tf_op jit(solution)/shard_map/ppermute | solution.py:237
  117.0 3.5 %collective-permute-start.25 = (f32[2,1]{0,1:T(1,128)S(1)}, f32[2,1]{0,1:T(1,128)S(1)}, u32[]{:S(2)}, u32[]{:S(2)}) collective-permute-start(f32[2,1]{0,1:T(1,128)S(1)} %constant_dynamic-slice_fusion.2), channel_id=1, source_target_pairs={{0,2},{1,3},{2,0},{3,1},{4,6},{5,7},{6,4},{7,5},{8,10},{9,11},{10,... | collective-permute-start | bytes 32 | tf_op jit(solution)/shard_map/ppermute | solution.py:388
  118.2 25.3 %copy-start.2 = (f32[4000,12]{1,0:T(8,128)}, f32[4000,12]{1,0:T(8,128)S(1)}, u32[]{:S(2)}) copy-start(f32[4000,12]{1,0:T(8,128)S(1)} %turn_gradients.1.refs_6_.refs_5_) | copy-start | bytes 576004
  120.6 4.4 %collective-permute-start.26 = (f32[2,1]{0,1:T(1,128)S(1)}, f32[2,1]{0,1:T(1,128)S(1)}, u32[]{:S(2)}, u32[]{:S(2)}) collective-permute-start(f32[2,1]{0,1:T(1,128)S(1)} %fusion.14), channel_id=1, source_target_pairs={{0,4},{1,5},{2,6},{3,7},{4,0},{5,1},{6,2},{7,3},{8,12},{9,13},{10,... | collective-permute-start | bytes 32 | tf_op jit(solution)/shard_map/ppermute | solution.py:388
  123.5 20.1 %collective-permute-start.28 = (bf16[2,2,3,128,128]{4,3,2,1,0:T(8,128)(2,1)S(1)}, bf16[2,2,3,128,128]{4,3,2,1,0:T(8,128)(2,1)S(1)}, u32[]{:S(2)}, u32[]{:S(2)}) collective-permute-start(bf16[2,2,3,128,128]{4,3,2,1,0:T(8,128)(2,1)S(1)} %get-tuple-element.61), channel_id=1, source_target_pairs={{0,8},{8,0},{1,9},{9,1},{2,10},{10,2},{3,11},{11,3},{4,12},{12,4},... | collective-permute-start | bytes 1179656 | tf_op jit(solution)/shard_map/ppermute | solution.py:485
  125.1 27.0 %copy-start.1 = (bf16[4,768,512]{2,1,0:T(8,128)(2,1)S(1)}, bf16[4,768,512]{2,1,0:T(8,128)(2,1)}, u32[]{:S(2)}) copy-start(bf16[4,768,512]{2,1,0:T(8,128)(2,1)} %copy-done) | copy-start | bytes 9437188
  144.9 2.7 %copy-start.7 = (bf16[2,3,128,128]{3,2,1,0:T(8,128)(2,1)}, bf16[2,3,128,128]{3,2,1,0:T(8,128)(2,1)S(1)}, u32[]{:S(2)}) copy-start(bf16[2,3,128,128]{3,2,1,0:T(8,128)(2,1)S(1)} %get-tuple-element.74) | copy-start | bytes 589828
  144.9 2.7 %copy-start.8 = (bf16[2,3,128,128]{3,2,1,0:T(8,128)(2,1)}, bf16[2,3,128,128]{3,2,1,0:T(8,128)(2,1)S(1)}, u32[]{:S(2)}) copy-start(bf16[2,3,128,128]{3,2,1,0:T(8,128)(2,1)S(1)} %get-tuple-element.73) | copy-start | bytes 589828
  146.3 0.8 copy-start.5
  147.1 17.5 %collective-permute-start.30 = (bf16[2,2,3,128,128]{4,3,2,1,0:T(8,128)(2,1)}, bf16[2,2,3,128,128]{4,3,2,1,0:T(8,128)(2,1)}, u32[]{:S(2)}, u32[]{:S(2)}) collective-permute-start(bf16[2,2,3,128,128]{4,3,2,1,0:T(8,128)(2,1)} %get-tuple-element.67), channel_id=1, source_target_pairs={{0,8},{8,0},{1,9},{9,1},{2,10},{10,2},{3,11},{11,3},{4,12},{12,4},... | collective-permute-start | bytes 1179656 | tf_op jit(solution)/shard_map/ppermute | solution.py:485
  147.7 20.3 %collective-permute-start.31 = (bf16[2,3,128,128]{3,2,1,0:T(8,128)(2,1)}, bf16[2,3,128,128]{3,2,1,0:T(8,128)(2,1)S(1)}, u32[]{:S(2)}, u32[]{:S(2)}) collective-permute-start(bf16[2,3,128,128]{3,2,1,0:T(8,128)(2,1)} %get-tuple-element.72), channel_id=1, source_target_pairs={{0,2},{1,3},{2,4},{3,5},{4,6},{5,7},{6,0},{7,1},{8,10},{9,11},{10,... | collective-permute-start | bytes 589832 | tf_op jit(solution)/shard_map/ppermute | solution.py:251
  148.6 39.6 %collective-permute-start.32 = (bf16[2,3,128,128]{3,2,1,0:T(8,128)(2,1)}, bf16[2,3,128,128]{3,2,1,0:T(8,128)(2,1)S(1)}, u32[]{:S(2)}, u32[]{:S(2)}) collective-permute-start(bf16[2,3,128,128]{3,2,1,0:T(8,128)(2,1)} %copy-done.8), channel_id=1, source_target_pairs={{0,4},{1,5},{2,6},{3,7},{4,0},{5,1},{6,2},{7,3},{8,12},{9,13},{10,... | collective-permute-start | bytes 589832 | tf_op jit(solution)/shard_map/ppermute | solution.py:251
  149.5 38.8 %collective-permute-start.33 = (bf16[2,3,128,128]{3,2,1,0:T(8,128)(2,1)}, bf16[2,3,128,128]{3,2,1,0:T(8,128)(2,1)S(1)}, u32[]{:S(2)}, u32[]{:S(2)}) collective-permute-start(bf16[2,3,128,128]{3,2,1,0:T(8,128)(2,1)} %copy-done.7), channel_id=1, source_target_pairs={{0,6},{1,7},{2,0},{3,1},{4,2},{5,3},{6,4},{7,5},{8,14},{9,15},{10,... | collective-permute-start | bytes 589832 | tf_op jit(solution)/shard_map/ppermute | solution.py:251
  152.1 1.6 copy-start.3
  153.7 1.0 copy-start.6
  154.7 16.1 %copy-start.4 = (f32[4000,12]{1,0:T(8,128)S(1)}, f32[4000,12]{1,0:T(8,128)}, u32[]{:S(2)}) copy-start(f32[4000,12]{1,0:T(8,128)} %copy-done.2) | copy-start | bytes 576004
  165.8 22.5 %collective-permute-start.34 = (bf16[2,3,128,128]{3,2,1,0:T(8,128)(2,1)S(1)}, bf16[2,3,128,128]{3,2,1,0:T(8,128)(2,1)S(1)}, u32[]{:S(2)}, u32[]{:S(2)}) collective-permute-start(bf16[2,3,128,128]{3,2,1,0:T(8,128)(2,1)S(1)} %get-tuple-element.75), channel_id=1, source_target_pairs={{0,2},{1,3},{2,4},{3,5},{4,6},{5,7},{6,0},{7,1},{8,10},{9,11},{10,... | collective-permute-start | bytes 589832 | tf_op jit(solution)/shard_map/ppermute | solution.py:251
  166.4 21.9 %collective-permute-start.35 = (bf16[2,3,128,128]{3,2,1,0:T(8,128)(2,1)S(1)}, bf16[2,3,128,128]{3,2,1,0:T(8,128)(2,1)S(1)}, u32[]{:S(2)}, u32[]{:S(2)}) collective-permute-start(bf16[2,3,128,128]{3,2,1,0:T(8,128)(2,1)S(1)} %get-tuple-element.76), channel_id=1, source_target_pairs={{0,4},{1,5},{2,6},{3,7},{4,0},{5,1},{6,2},{7,3},{8,12},{9,13},{10,... | collective-permute-start | bytes 589832 | tf_op jit(solution)/shard_map/ppermute | solution.py:251
  167.9 20.4 %collective-permute-start.36 = (bf16[2,3,128,128]{3,2,1,0:T(8,128)(2,1)S(1)}, bf16[2,3,128,128]{3,2,1,0:T(8,128)(2,1)S(1)}, u32[]{:S(2)}, u32[]{:S(2)}) collective-permute-start(bf16[2,3,128,128]{3,2,1,0:T(8,128)(2,1)S(1)} %get-tuple-element.77), channel_id=1, source_target_pairs={{0,6},{1,7},{2,0},{3,1},{4,2},{5,3},{6,4},{7,5},{8,14},{9,15},{10,... | collective-permute-start | bytes 589832 | tf_op jit(solution)/shard_map/ppermute | solution.py:251

commit v3 on v2

--- a/solution.py
+++ b/solution.py
@@ -176,12 +176,12 @@
             c += 1
 
 
-def head_kernel(groups, docs, *refs):
+def head_kernel(groups, docs, width, split, *refs):
     index_ref, margin_ref = refs[:2]
     rows = refs[2:2 + groups]
     columns_ref = refs[2 + groups]
-    out_ref, token_ref, spread_ref = refs[-3:]
-    chunks, tokens, width = rows[0].shape
+    out_ref, token_ref, spread_ref = refs[-3 - split], refs[-2], refs[-1]
+    chunks, tokens, lanes = rows[0].shape
     length = tokens // docs
     count = groups * docs
 
@@ -201,12 +201,24 @@
             total = None
             for g in range(groups):
                 ref = rows[(g - first) % groups]
-                features = jnp.concatenate([ref[c] for c in range(chunks)], axis=1)
+                features = jnp.concatenate(
+                    [ref[c, :, lane:lane + width] for lane in range(0, lanes, width) for c in range(chunks)], axis=1
+                )
                 term = jnp.dot(
                     spread_ref[:, g * tokens:(g + 1) * tokens], features, preferred_element_type=jnp.float32
                 )
                 total = term if total is None else total + term
-            out_ref[...] = total
+            if split:
+                sent_ref = refs[-3]
+                sent_ref[...] = total.astype(jnp.bfloat16)
+                out_ref[...] = sent_ref[...].astype(jnp.float32)
+            else:
+                out_ref[...] = total
+
+
+def widen_kernel(index_ref, piece_ref, previous_ref, out_ref, token_ref):
+    token_ref[...] = jnp.zeros_like(token_ref)
+    out_ref[...] = piece_ref[...].astype(jnp.float32)
 
 
 def on_device(axes, hidden_states, head_weight, owner_pos, token_ids, teacher_margin):
@@ -284,15 +296,18 @@
         lengths = lengths + lax.ppermute(own_lengths, "seq", shift_perm(slots, s))
     validity = (owner_blocks < lengths[None]).astype(jnp.float32)
 
-    def run(kernel, name, operands, specs, shapes, out_specs=None, waits=(), flops=0, aliases={}, scratch=(), grid=()):
+    def run(kernel, name, operands, specs, shapes, out_specs=None, waits=(), flops=0, aliases={}, scratch=(), grid=(), prefetch=0):
         waits = [value for value in waits if value is not None]
         return pl.pallas_call(
             waiting(kernel, len(waits)),
-            grid=grid,
-            in_specs=[index_spec] + [any_spec] * len(waits) + specs,
-            out_specs=out_specs or [vmem_spec] * len(shapes),
+            grid_spec=pltpu.PrefetchScalarGridSpec(
+                num_scalar_prefetch=prefetch,
+                grid=grid,
+                in_specs=[index_spec] * (1 - prefetch) + [any_spec] * len(waits) + specs,
+                out_specs=out_specs or [vmem_spec] * len(shapes),
+                scratch_shapes=list(scratch),
+            ),
             out_shape=shapes,
-            scratch_shapes=list(scratch),
             input_output_aliases={1 + len(waits) + i: o for i, o in aliases.items()},
             compiler_params=params,
             cost_estimate=cost(flops, flops // 64),
@@ -334,11 +349,17 @@
         logit_parts.append(chunk_logits)
 
     first_step = None
+    picked = []
     for c in range(chunks):
         own = sliced[c]
         if c > 0:
             (own,) = run(
-                copy_kernel, "feature_chunk", [own], [vmem_spec], [bf16(docs, part, width)], waits=[first_step]
+                copy_kernel,
+                "feature_chunk",
+                [own],
+                [vmem_spec],
+                [bf16(docs, part, width)],
+                waits=[first_step, picked[c - 2] if c > 1 else None],
             )
         held = [own]
         for back in range(1, outer):
@@ -352,6 +373,7 @@
             [moved_shape] * slots,
             waits=[gathered_chunks[c - 1] if c > 0 else None],
         )
+        picked.append(mine)
         arrived = [lax.ppermute(sends[s - 1], "seq", shift_perm(slots, -s)) for s in range(1, slots)]
         if c == last and c > 1:
             add_logits(0, [mine])
@@ -417,36 +439,69 @@
 
     head_terms = divisor(terms, 800)
     ranges = terms // head_terms
-    next_range = 0
+    owned = (ranges - 1) // groups if groups > 1 else 0
     grad_head = token = None
-
-    def run_head(count, *waits):
-        nonlocal grad_head, token, next_range
+    shares = []
+
+    def run_head(start, count, split, *waits):
+        nonlocal grad_head, token
         if count == 0:
             return
         previous = [] if grad_head is None else [grad_head]
-        start = next_range
-        term_spec = pl.BlockSpec((head_terms, 2 * groups * docs), lambda r, d: (start + r, 0))
-        grad_head, token = run(
-            functools.partial(head_kernel, groups, docs),
+        row = lambda r, index_ref: start + r + (index_ref[1] * owned if split else 0)
+        grad_head, *sent, token = run(
+            functools.partial(head_kernel, groups, docs, width, split),
             "head_terms",
             [margin_all, *features_all, head_columns, *previous],
             [index_spec]
-            + [pl.BlockSpec((chunks, tokens, width), lambda r, d: (0, 0, d))] * groups
-            + [term_spec]
+            + [pl.BlockSpec((chunks, tokens, width), lambda r, d, index_ref: (0, 0, d))] * groups
+            + [pl.BlockSpec((head_terms, 2 * groups * docs), lambda r, d, index_ref: (row(r, index_ref), 0))]
             + [any_spec] * len(previous),
-            [jax.ShapeDtypeStruct((terms, depth), jnp.float32), jax.ShapeDtypeStruct((8, LANES), jnp.float32)],
-            out_specs=[
-                pl.BlockSpec((head_terms, block_width), lambda r, d: (start + r, d)),
-                pl.BlockSpec((8, LANES), lambda r, d: (0, 0)),
-            ],
+            [jax.ShapeDtypeStruct((terms, depth), jnp.float32)]
+            + [bf16(count * head_terms, depth)] * split
+            + [jax.ShapeDtypeStruct((8, LANES), jnp.float32)],
+            out_specs=[pl.BlockSpec((head_terms, block_width), lambda r, d, index_ref: (row(r, index_ref), d))]
+            + [pl.BlockSpec((head_terms, block_width), lambda r, d, index_ref: (r, d))] * split
+            + [pl.BlockSpec((8, LANES), lambda r, d, index_ref: (0, 0))],
             waits=waits,
-            flops=count * 2 * groups * tokens * head_terms * depth // 4,
+            flops=count * 2 * groups * tokens * head_terms * depth * (1 if split else 1024) // 4,
             aliases={2 + groups: 0} if previous else {},
             scratch=[pltpu.VMEM((head_terms, groups * tokens), jnp.bfloat16)],
             grid=(count, strips),
-        )
-        next_range += count
+            prefetch=1,
+        )
+        if split:
+            shares.append((start, other_groups(sent[0])[1:]))
+
+    def widen_shares():
+        nonlocal grad_head, token
+        for start, arrived in shares:
+            for g, piece in enumerate(arrived, 1):
+
+                def row(r, index_ref, start=start, g=g):
+                    return start + r + lax.rem(index_ref[1] + g, groups) * owned
+
+                grad_head, token = run(
+                    widen_kernel,
+                    "widen_share",
+                    [piece, grad_head],
+                    [pl.BlockSpec((head_terms // 2, depth), lambda r, index_ref: (r, 0)), any_spec],
+                    [
+                        jax.ShapeDtypeStruct((terms, depth), jnp.float32),
+                        jax.ShapeDtypeStruct((8, LANES), jnp.float32),
+                    ],
+                    out_specs=[
+                        pl.BlockSpec(
+                            (head_terms // 2, depth),
+                            functools.partial(lambda row, r, index_ref: (2 * row(0, index_ref) + r, 0), row),
+                        ),
+                        pl.BlockSpec((8, LANES), lambda r, index_ref: (0, 0)),
+                    ],
+                    flops=piece.size,
+                    aliases={1: 0},
+                    grid=(2 * piece.shape[0] // head_terms,),
+                    prefetch=1,
+                )
 
     half = -(-chunks // 2)
     chunk_groups = [members for members in (range(half), range(half, chunks)) if members]
@@ -468,7 +523,6 @@
         )
         pairs.append([sums[0]] + [across_y(sums[q], q) for q in range(1, inner)])
 
-    share = ranges // 5
     mine_all = []
     arrived_all = []
 
@@ -495,14 +549,17 @@
         )
         arrived_all.append([pieces[0]] + [across_z(pieces[ahead], ahead) for ahead in range(1, outer)])
 
+    early = -(-owned // 2)
     add_blocks(pairs[0])
-    run_head(2 * share, mine_all[0][0], pairs[-1][0])
+    run_head(0, early, True, mine_all[0][0], pairs[-1][0])
     sort_pieces(mine_all[0], token)
     if len(pairs) > 1:
         add_blocks(pairs[1], arrived_all[0][0])
-        run_head(share, arrived_all[0][0], mine_all[1][0])
+    run_head(early, owned - early, True, arrived_all[0][0], mine_all[-1][0])
+    if len(pairs) > 1:
         sort_pieces(mine_all[1], token)
-    run_head(ranges - next_range, arrived_all[-1][0])
+    run_head(owned * groups, ranges - owned * groups, False, arrived_all[-1][0], *arrived_all[0][1:])
+    widen_shares()
     (grad_hidden,) = run(
         functools.partial(finish_kernel, [len(members) for members in chunk_groups], outer),
         "scale_hidden",

time: 191 us -> 196 us (1.026)
  waiting for transfers between devices: 21.7 us -> 35.2 us
  starting transfers between devices: 51.6 us -> 43.4 us
    ppermute x12, waiting for transfers between devices: 4.15 us -> 24.3 us  [around_ring(): return lax.ppermute(value, 'vocab', perm)]
    ppermute x12, starting transfers between devices: 24.9 us -> 13.5 us  [around_ring(): return lax.ppermute(value, 'vocab', perm)]
    ppermute x4, waiting for transfers between devices: 7.46 us -> 1.92 us  [on_device(): lax.ppermute(sends[s - 1], 'seq', shift_perm(slots, -s))]
    ppermute x3, starting transfers between devices: 3.73 us -> 6.28 us  [add_distance(): lax.ppermute(value, 'vocab', [(i, i ^ distance) for i in range(blocks)])]
    pallas_call x26 -> x28, Pallas kernels: 103 us -> 102 us  [run(): pl.pallas_call(waiting(kernel, len(waits)), grid_spec=pltpu.PrefetchScala...]
  transfers between devices with their start and end apart: 37 -> 39, of which waited for: 10 -> 14; matrix products, arithmetic and copies ran while one was open for 3% -> 3% of each run, Pallas kernels for 49% -> 47%
where the time goes in v3:
time: 196 us; the launch traced here: 195 us
  Pallas kernels  102 us (52%)
  starting transfers between devices  43.4 us (22%)
  waiting for transfers between devices  35.2 us (18%)
  local copies, waits for them, and re-layouts  6.63 us (3%)
  other arithmetic  3.71 us (2%)
  between operations  3.58 us (2%)
    pallas_call x28, Pallas kernels, run(): pl.pallas_call(waiting(kernel, len(waits)), grid_spec=pltpu.PrefetchScala...  102 us
    ppermute x12, waiting for transfers between devices, around_ring(): return lax.ppermute(value, 'vocab', perm)  24.3 us
    ppermute x12, starting transfers between devices, around_ring(): return lax.ppermute(value, 'vocab', perm)  13.5 us
    ppermute x6, starting transfers between devices, across_z(): return lax.ppermute(value, 'vocab', perm)  9.72 us
    ppermute x3, starting transfers between devices, add_distance(): lax.ppermute(value, 'vocab', [(i, i ^ distance) for i in range(blocks)])  6.28 us
    ppermute x6, starting transfers between devices, across_y(): return lax.ppermute(value, 'vocab', perm)  5.52 us
  transfers between devices with their start and end apart: 39, of which 14 were waited for; matrix products, arithmetic and copies ran while one was open for 3% of the time, Pallas kernels for 47%

profile of v3, /device:TPU:0, one launch (start us, length us, event | category | flops | bytes accessed | tf_op | source)
XLA Modules:
  0.0 194.8 jit_solution(11805243463608225754)
XLA Ops:
  0.6 1.1 fusion.12
  1.7 4.1 %collective-permute-start.3 = (bf16[3,128,128]{2,1,0:T(8,128)(2,1)S(1)}, bf16[3,128,128]{2,1,0:T(8,128)(2,1)S(1)}, u32[]{:S(2)}, u32[]{:S(2)}) collective-permute-start(bf16[3,128,128]{2,1,0:T(8,128)(2,1)S(1)} %get-tuple-element.92.refs_1_), channel_id=1, source_target_pairs={{0,4},{1,5},{2,0},{3,1},{6,2},{7,3},{4,6},{5,7},{8,12},{9,13},{10,... | collective-permute-start | bytes 294920 | tf_op jit(solution)/shard_map/ppermute | solution.py:259
  5.8 1.3 collective-permute-start.2
  7.1 0.8 collective-permute-start.1
  8.0 8.0 %collective-permute-done.1.refs_2_.refs_1_ = bf16[3,128,128]{2,1,0:T(8,128)(2,1)S(1)} collective-permute-done((bf16[3,128,128]{2,1,0:T(8,128)(2,1)S(1)}, bf16[3,128,128]{2,1,0:T(8,128)(2,1)S(1)}, u32[]{:S(2)}, u32[]{:S(2)}) %collective-permute-start.1) | collective-permute-done | bytes 98336 | tf_op jit(solution)/shard_map/ppermute | solution.py:259
  16.6 0.7 pick_halves.4
  17.3 4.9 %collective-permute-done.6.refs_3_.refs_1_ = bf16[3,128,128]{2,1,0:T(8,128)(2,1)S(1)} collective-permute-done((bf16[3,128,128]{2,1,0:T(8,128)(2,1)S(1)}, bf16[3,128,128]{2,1,0:T(8,128)(2,1)S(1)}, u32[]{:S(2)}, u32[]{:S(2)}) %collective-permute-start.6) | collective-permute-done | bytes 98336 | tf_op jit(solution)/shard_map/ppermute | solution.py:259
  22.8 3.0 %collective-permute-start.7 = (bf16[3,128,128]{2,1,0:T(8,128)(2,1)S(1)}, bf16[3,128,128]{2,1,0:T(8,128)(2,1)S(1)}, u32[]{:S(2)}, u32[]{:S(2)}) collective-permute-start(bf16[3,128,128]{2,1,0:T(8,128)(2,1)S(1)} %collective-permute-done.6.refs_3_.refs_1_), channel_id=1, source_target_pairs={{0,2},{1,3},{2,6},{3,7},{6,4},{7,5},{4,0},{5,1},{8,10},{9,11},{10,... | collective-permute-start | bytes 294920 | tf_op jit(solution)/shard_map/ppermute | solution.py:259
  25.8 1.5 collective-permute-start.4
  27.3 1.3 collective-permute-done.10.refs_3_.refs_1_
  28.6 1.1 collective-permute-done.7.refs_4_
  29.7 2.0 %collective-permute-start.8 = (bf16[3,128,128]{2,1,0:T(8,128)(2,1)S(1)}, bf16[3,128,128]{2,1,0:T(8,128)(2,1)S(1)}, u32[]{:S(2)}, u32[]{:S(2)}) collective-permute-start(bf16[3,128,128]{2,1,0:T(8,128)(2,1)S(1)} %collective-permute-done.7.refs_4_), channel_id=1, source_target_pairs={{0,2},{1,3},{2,6},{3,7},{6,4},{7,5},{4,0},{5,1},{8,10},{9,11},{10,... | collective-permute-start | bytes 294920 | tf_op jit(solution)/shard_map/ppermute | solution.py:259
  31.7 0.8 convert_reduce_fusion
  32.5 1.5 collective-permute-start
  34.0 0.9 reshape.71
  35.6 1.6 collective-permute-start.5
  37.1 0.7 pick_halves.5
  38.4 1.1 collective-permute-start.14
  40.0 1.0 collective-permute-start.12
  41.1 3.9 %collective-permute-done.14.refs_3_ = bf16[3,128,128]{2,1,0:T(8,128)(2,1)S(1)} collective-permute-done((bf16[3,128,128]{2,1,0:T(8,128)(2,1)S(1)}, bf16[3,128,128]{2,1,0:T(8,128)(2,1)S(1)}, u32[]{:S(2)}, u32[]{:S(2)}) %collective-permute-start.14) | collective-permute-done | bytes 98336 | tf_op jit(solution)/shard_map/ppermute | solution.py:259
  46.0 0.7 pick_halves.6
  46.7 1.0 collective-permute-start.13
  48.3 2.4 %collective-permute-done.15.refs_4_ = bf16[3,128,128]{2,1,0:T(8,128)(2,1)S(1)} collective-permute-done((bf16[3,128,128]{2,1,0:T(8,128)(2,1)S(1)}, bf16[3,128,128]{2,1,0:T(8,128)(2,1)S(1)}, u32[]{:S(2)}, u32[]{:S(2)}) %collective-permute-start.15) | collective-permute-done | bytes 98336 | tf_op jit(solution)/shard_map/ppermute | solution.py:259
  50.7 1.8 collective-permute-done.13.refs_3_
  53.7 2.5 %collective-permute-done.16.refs_5_ = bf16[3,128,128]{2,1,0:T(8,128)(2,1)S(1)} collective-permute-done((bf16[3,128,128]{2,1,0:T(8,128)(2,1)S(1)}, bf16[3,128,128]{2,1,0:T(8,128)(2,1)S(1)}, u32[]{:S(2)}, u32[]{:S(2)}) %collective-permute-start.16) | collective-permute-done | bytes 98336 | tf_op jit(solution)/shard_map/ppermute | solution.py:259
  56.2 0.9 pick_halves.7
  57.7 5.5 %pooled_logits.4 = (f32[2,3,2000]{2,1,0:T(4,128)S(1)}, bf16[4,768,512]{2,1,0:T(8,128)(2,1)S(1)}) custom-call(s32[4]{0:T(128)S(1)} %pad_add_fusion.refs_0_, bf16[2,3,128,128]{3,2,1,0:T(8,128)(2,1)S(1)} %get-tuple-element.50.refs_1_.refs_3_, bf16[2,2,3,128,128]{4,3,2,1,0:T(8,128)(2,1)S(1)} %join_tokens.4.refs_1_.refs_2_, ...), custom_call_target="tpu_custom_call" | custom-call | flops 3145728000 | bytes 49152000 | tf_op jit(solution)/shard_map/pooled_logits/pallas_call | solution.py:301
  63.7 0.7 collective-permute-start.20
  64.4 1.9 collective-permute-done.17.refs_2_
  66.4 5.5 %pooled_logits.5 = (f32[2,3,2000]{2,1,0:T(4,128)S(1)}, bf16[4,768,512]{2,1,0:T(8,128)(2,1)S(1)}) custom-call(s32[4]{0:T(128)S(1)} %pad_add_fusion.refs_0_, f32[2,3,2000]{2,1,0:T(4,128)S(1)} %get-tuple-element.88.refs_1_, bf16[2,2,3,128,128]{4,3,2,1,0:T(8,128)(2,1)S(1)} %collective-permute-done.17.refs_2_, ...), custom_call_target="tpu_custom_call", output_to_operand_aliasing={{1}: (10, {})} | custom-call | flops 3145728000 | bytes 49152000 | tf_op jit(solution)/shard_map/pooled_logits/pallas_call | solution.py:301
  71.8 5.5 %pooled_logits.6 = (f32[2,3,2000]{2,1,0:T(4,128)S(1)}, bf16[4,768,512]{2,1,0:T(8,128)(2,1)S(1)}) custom-call(s32[4]{0:T(128)S(1)} %pad_add_fusion.refs_0_, bf16[2,2,3,128,128]{4,3,2,1,0:T(8,128)(2,1)S(1)} %join_tokens.6.refs_1_, bf16[2,2,3,128,128]{4,3,2,1,0:T(8,128)(2,1)S(1)} %collective-permute-done.17.refs_2_, ...), custom_call_target="tpu_custom_call", output_to_operand_aliasing={{1}: (8, {})} | custom-call | flops 3145728000 | bytes 49152000 | tf_op jit(solution)/shard_map/pooled_logits/pallas_call | solution.py:301
  77.3 5.5 %pooled_logits.7 = (f32[2,3,2000]{2,1,0:T(4,128)S(1)}, bf16[4,768,512]{2,1,0:T(8,128)(2,1)S(1)}) custom-call(s32[4]{0:T(128)S(1)} %pad_add_fusion.refs_0_, bf16[2,2,3,128,128]{4,3,2,1,0:T(8,128)(2,1)S(1)} %join_tokens.7.refs_1_, bf16[2,2,3,128,128]{4,3,2,1,0:T(8,128)(2,1)S(1)} %collective-permute-done.20.refs_2_, ...), custom_call_target="tpu_custom_call", output_to_operand_aliasing={{1}: (8, {})} | custom-call | flops 3145728000 | bytes 49152000 | tf_op jit(solution)/shard_map/pooled_logits/pallas_call | solution.py:301
  83.8 3.7 %collective-permute-done.21 = f32[2,3,2000]{2,1,0:T(4,128)S(1)} collective-permute-done((f32[2,3,2000]{2,1,0:T(4,128)S(1)}, f32[2,3,2000]{2,1,0:T(4,128)S(1)}, u32[]{:S(2)}, u32[]{:S(2)}) %collective-permute-start.21) | collective-permute-done | bytes 48032 | tf_op jit(solution)/shard_map/ppermute | solution.py:396
  89.6 1.4 collective-permute-start.23
  91.2 10.2 %hidden_terms.2 = (bf16[2,2,2,3,128,128]{5,4,3,2,1,0:T(8,128)(2,1)S(1)}, bf16[2,2,2,3,128,128]{5,4,3,2,1,0:T(8,128)(2,1)S(1)}) custom-call(s32[4]{0:T(128)S(1)} %pad_add_fusion.refs_0_, bf16[4000,2048]{1,0:T(8,128)(2,1)} %bitcast.60, bf16[4000,2048]{1,0:T(8,128)(2,1)} %bitcast.61, bf16[4000,2048]{1,0:T(8,128)(2,1)} %bitcast.62, bf16[4000,2048]{1,0:T(8,128)(2,1)} %bitcast.63, ...), custom_call_target="tpu_custom_call" | custom-call | flops 1572864000 | bytes 24576000 | tf_op jit(solution)/shard_map/hidden_terms/pallas_call | solution.py:301
  101.4 2.1 %collective-permute-start.22 = (bf16[2,2,2,3,128,128]{5,4,3,2,1,0:T(8,128)(2,1)S(1)}, bf16[2,2,2,3,128,128]{5,4,3,2,1,0:T(8,128)(2,1)S(1)}, u32[]{:S(2)}, u32[]{:S(2)}) collective-permute-start(bf16[2,2,2,3,128,128]{5,4,3,2,1,0:T(8,128)(2,1)S(1)} %get-tuple-element.60), channel_id=1, source_target_pairs={{0,1},{1,0},{2,3},{3,2},{4,5},{5,4},{6,7},{7,6},{8,9},{9,8},{10,11... | collective-permute-start | bytes 2359304 | tf_op jit(solution)/shard_map/ppermute | solution.py:249
  104.3 10.4 %hidden_terms.3 = (bf16[2,2,2,3,128,128]{5,4,3,2,1,0:T(8,128)(2,1)S(1)}, bf16[2,2,2,3,128,128]{5,4,3,2,1,0:T(8,128)(2,1)S(1)}) custom-call(s32[4]{0:T(128)S(1)} %pad_add_fusion.refs_0_, f32[2,7,2000]{2,1,0:T(8,128)S(1)} %pad_maximum_fusion.refs_1_, bf16[4000,2048]{1,0:T(8,128)(2,1)} %bitcast.68, bf16[4000,2048]{1,0:T(8,128)(2,1)} %bitcast.69, ...), custom_call_target="tpu_custom_call" | custom-call | flops 1572864000 | bytes 24576000 | tf_op jit(solution)/shard_map/hidden_terms/pallas_call | solution.py:301
  115.4 0.7 pad_maximum_fusion.1
  116.2 2.4 %collective-permute-start.25 = (f32[2,1]{0,1:T(1,128)S(1)}, f32[2,1]{0,1:T(1,128)S(1)}, u32[]{:S(2)}, u32[]{:S(2)}) collective-permute-start(f32[2,1]{0,1:T(1,128)S(1)} %constant_dynamic-slice_fusion.2), channel_id=1, source_target_pairs={{0,2},{1,3},{2,0},{3,1},{4,6},{5,7},{6,4},{7,5},{8,10},{9,11},{10,... | collective-permute-start | bytes 32 | tf_op jit(solution)/shard_map/ppermute | solution.py:410
  118.6 1.3 turn_gradients.1.refs_6_.refs_8_
  119.8 0.7 pad_maximum_fusion.2
  120.5 1.4 collective-permute-done.22.refs_2_
  121.9 0.7 add_blocks.2
  122.6 1.0 collective-permute-start.28
  123.7 2.5 %collective-permute-start.26 = (f32[2,1]{0,1:T(1,128)S(1)}, f32[2,1]{0,1:T(1,128)S(1)}, u32[]{:S(2)}, u32[]{:S(2)}) collective-permute-start(f32[2,1]{0,1:T(1,128)S(1)} %fusion.14), channel_id=1, source_target_pairs={{0,4},{1,5},{2,6},{3,7},{4,0},{5,1},{6,2},{7,3},{8,12},{9,13},{10,... | collective-permute-start | bytes 32 | tf_op jit(solution)/shard_map/ppermute | solution.py:410
  126.2 1.9 collective-permute-done.26
  128.2 11.7 %head_terms.3 = (f32[4000,2048]{1,0:T(8,128)}, bf16[800,2048]{1,0:T(8,128)(2,1)}, f32[8,128]{1,0:T(8,128)S(1)}) custom-call(s32[4]{0:T(128)S(1)} %pad_add_fusion.refs_0_, bf16[2,2,3,128,128]{4,3,2,1,0:T(8,128)(2,1)S(1)} %get-tuple-element.61.refs_1_.refs_2_, bf16[2,2,2,3,128,128]{5,4,3,2,1,0:T(8,128)(2,1)S(1)} %get-tuple-element.62.refs_2_, f32[2]{0:T(128)S(1)} %bitcast.41, ...), custom_call_target="tpu_custom_call" | custom-call | flops 1258291200 | bytes 19660800 | tf_op jit(solution)/shard_map/head_terms/pallas_call | solution.py:301
  140.0 1.5 sort_pieces.2
  141.5 1.4 add_blocks.3
  142.8 0.7 copy-done.5
  143.6 1.3 collective-permute-start.32
  144.9 2.1 %collective-permute-start.33 = (bf16[2,3,128,128]{3,2,1,0:T(8,128)(2,1)}, bf16[2,3,128,128]{3,2,1,0:T(8,128)(2,1)S(1)}, u32[]{:S(2)}, u32[]{:S(2)}) collective-permute-start(bf16[2,3,128,128]{3,2,1,0:T(8,128)(2,1)} %get-tuple-element.75), channel_id=1, source_target_pairs={{0,2},{1,3},{2,4},{3,5},{4,6},{5,7},{6,0},{7,1},{8,10},{9,11},{10,... | collective-permute-start | bytes 589832 | tf_op jit(solution)/shard_map/ppermute | solution.py:263
  147.1 0.8 collective-permute-start.34
  147.8 2.9 %collective-permute-start.35 = (bf16[2,3,128,128]{3,2,1,0:T(8,128)(2,1)}, bf16[2,3,128,128]{3,2,1,0:T(8,128)(2,1)}, u32[]{:S(2)}, u32[]{:S(2)}) collective-permute-start(bf16[2,3,128,128]{3,2,1,0:T(8,128)(2,1)} %get-tuple-element.77), channel_id=1, source_target_pairs={{0,6},{1,7},{2,0},{3,1},{4,2},{5,3},{6,4},{7,5},{8,14},{9,15},{10,... | collective-permute-start | bytes 589832 | tf_op jit(solution)/shard_map/ppermute | solution.py:263
  151.4 1.6 copy-done.3
  153.0 1.0 copy-done.6
  153.9 11.0 %head_terms.4 = (f32[4000,2048]{1,0:T(8,128)}, bf16[800,2048]{1,0:T(8,128)(2,1)}, f32[8,128]{1,0:T(8,128)S(1)}) custom-call(s32[4]{0:T(128)S(1)} %pad_add_fusion.refs_0_, bf16[2,3,128,128]{3,2,1,0:T(8,128)(2,1)S(1)} %get-tuple-element.66.refs_1_.refs_3_, bf16[2,2,3,128,128]{4,3,2,1,0:T(8,128)(2,1)S(1)} %copy-done.6, ...), custom_call_target="tpu_custom_call", output_to_operand_aliasing={{0}: (7, {})} | custom-call | flops 1258291200 | bytes 19660800 | tf_op jit(solution)/shard_map/head_terms/pallas_call | solution.py:301
  165.5 1.9 %sort_pieces.3 = (bf16[2,3,128,128]{3,2,1,0:T(8,128)(2,1)S(1)}, bf16[2,3,128,128]{3,2,1,0:T(8,128)(2,1)}, bf16[2,3,128,128]{3,2,1,0:T(8,128)(2,1)}, bf16[2,3,128,128]{3,2,1,0:T(8,128)(2,1)}) custom-call(s32[4]{0:T(128)S(1)} %pad_add_fusion.refs_0_, f32[8,128]{1,0:T(8,128)S(1)} %get-tuple-element.72.refs_1_, bf16[2,2,3,128,128]{4,3,2,1,0:T(8,128)(2,1)S(1)} %copy-done.6, ...), custom_call_target="tpu_custom_call" | custom-call | tf_op jit(solution)/shard_map/sort_pieces/pallas_call | solution.py:301
  167.5 1.2 collective-permute-start.37
  168.7 2.6 %collective-permute-start.38 = (bf16[2,3,128,128]{3,2,1,0:T(8,128)(2,1)}, bf16[2,3,128,128]{3,2,1,0:T(8,128)(2,1)}, u32[]{:S(2)}, u32[]{:S(2)}) collective-permute-start(bf16[2,3,128,128]{3,2,1,0:T(8,128)(2,1)} %get-tuple-element.85), channel_id=1, source_target_pairs={{0,6},{1,7},{2,0},{3,1},{4,2},{5,3},{6,4},{7,5},{8,14},{9,15},{10,... | collective-permute-start | bytes 589832 | tf_op jit(solution)/shard_map/ppermute | solution.py:263
  171.3 10.6 %head_terms.5 = (f32[4000,2048]{1,0:T(8,128)}, f32[8,128]{1,0:T(8,128)}) custom-call(s32[4]{0:T(128)S(1)} %pad_add_fusion.refs_0_, bf16[2,3,128,128]{3,2,1,0:T(8,128)(2,1)S(1)} %get-tuple-element.74.refs_1_.refs_7_, bf16[2,3,128,128]{3,2,1,0:T(8,128)(2,1)S(1)} %collective-permute-done.33.refs_2_.refs_4_, ...), custom_call_target="tpu_custom_call", output_to_operand_aliasing={{0}: (9, {})} | custom-call | flops 1288490188800 | bytes 20132659200 | tf_op jit(solution)/shard_map/head_terms/pallas_call | solution.py:301
  182.0 5.0 %widen_share.2 = (f32[4000,2048]{1,0:T(8,128)}, f32[8,128]{1,0:T(8,128)}) custom-call(s32[4]{0:T(128)S(1)} %pad_add_fusion.refs_0_, bf16[800,2048]{1,0:T(8,128)(2,1)} %collective-permute-done.31.refs_1_, f32[4000,2048]{1,0:T(8,128)} %get-tuple-element.79.refs_2_), custom_call_target="tpu_custom_call", output_to_operand_aliasing={{0}: (2, {})} | custom-call | flops 1638400 | bytes 25600 | tf_op jit(solution)/shard_map/widen_share/pallas_call | solution.py:301
  187.0 5.0 %widen_share.3 = (f32[4000,2048]{1,0:T(8,128)}, f32[8,128]{1,0:T(8,128)S(1)}) custom-call(s32[4]{0:T(128)S(1)} %pad_add_fusion.refs_0_, bf16[800,2048]{1,0:T(8,128)(2,1)} %collective-permute-done.30.refs_1_, f32[4000,2048]{1,0:T(8,128)} %get-tuple-element.80.refs_2_), custom_call_target="tpu_custom_call", output_to_operand_aliasing={{0}: (2, {})} | custom-call | flops 1638400 | bytes 25600 | tf_op jit(solution)/shard_map/widen_share/pallas_call | solution.py:301
  192.0 2.9 %scale_hidden.1 = bf16[3,128,512]{2,1,0:T(8,128)(2,1)} custom-call(s32[4]{0:T(128)S(1)} %pad_add_fusion.refs_0_, f32[8,128]{1,0:T(8,128)S(1)} %get-tuple-element.82.refs_1_, f32[1]{0:T(128)} %bitcast.20.refs_2_, bf16[2,3,128,128]{3,2,1,0:T(8,128)(2,1)S(1)} %get-tuple-element.66.refs_1_.refs_3_, ...), custom_call_target="tpu_custom_call" | custom-call | tf_op jit(solution)/shard_map/scale_hidden/pallas_call | solution.py:301
  (77 shorter events, 10.5 us)
Async XLA Ops:
  1.7 14.9 %collective-permute-start.3 = (bf16[3,128,128]{2,1,0:T(8,128)(2,1)S(1)}, bf16[3,128,128]{2,1,0:T(8,128)(2,1)S(1)}, u32[]{:S(2)}, u32[]{:S(2)}) collective-permute-start(bf16[3,128,128]{2,1,0:T(8,128)(2,1)S(1)} %get-tuple-element.92.refs_1_), channel_id=1, source_target_pairs={{0,4},{1,5},{2,0},{3,1},{6,2},{7,3},{4,6},{5,7},{8,12},{9,13},{10,... | collective-permute-start | bytes 294920 | tf_op jit(solution)/shard_map/ppermute | solution.py:259
  5.8 10.8 %collective-permute-start.2 = (bf16[3,128,128]{2,1,0:T(8,128)(2,1)S(1)}, bf16[3,128,128]{2,1,0:T(8,128)(2,1)S(1)}, u32[]{:S(2)}, u32[]{:S(2)}) collective-permute-start(bf16[3,128,128]{2,1,0:T(8,128)(2,1)S(1)} %get-tuple-element.92.refs_1_), channel_id=1, source_target_pairs={{0,6},{1,7},{2,4},{3,5},{6,0},{7,1},{4,2},{5,3},{8,14},{9,15},{10,... | collective-permute-start | bytes 294920 | tf_op jit(solution)/shard_map/ppermute | solution.py:259
  7.1 8.8 %collective-permute-start.1 = (bf16[3,128,128]{2,1,0:T(8,128)(2,1)S(1)}, bf16[3,128,128]{2,1,0:T(8,128)(2,1)S(1)}, u32[]{:S(2)}, u32[]{:S(2)}) collective-permute-start(bf16[3,128,128]{2,1,0:T(8,128)(2,1)S(1)} %get-tuple-element.92.refs_1_), channel_id=1, source_target_pairs={{0,2},{1,3},{2,6},{3,7},{6,4},{7,5},{4,0},{5,1},{8,10},{9,11},{10,... | collective-permute-start | bytes 294920 | tf_op jit(solution)/shard_map/ppermute | solution.py:259
  16.5 5.7 %collective-permute-start.6 = (bf16[3,128,128]{2,1,0:T(8,128)(2,1)S(1)}, bf16[3,128,128]{2,1,0:T(8,128)(2,1)S(1)}, u32[]{:S(2)}, u32[]{:S(2)}) collective-permute-start(bf16[3,128,128]{2,1,0:T(8,128)(2,1)S(1)} %feature_chunk.3.refs_2_), channel_id=1, source_target_pairs={{0,2},{1,3},{2,6},{3,7},{6,4},{7,5},{4,0},{5,1},{8,10},{9,11},{10,... | collective-permute-start | bytes 294920 | tf_op jit(solution)/shard_map/ppermute | solution.py:259
  22.7 5.9 %collective-permute-start.10 = (bf16[3,128,128]{2,1,0:T(8,128)(2,1)S(1)}, bf16[3,128,128]{2,1,0:T(8,128)(2,1)S(1)}, u32[]{:S(2)}, u32[]{:S(2)}) collective-permute-start(bf16[3,128,128]{2,1,0:T(8,128)(2,1)S(1)} %feature_chunk.4.refs_2_), channel_id=1, source_target_pairs={{0,2},{1,3},{2,6},{3,7},{6,4},{7,5},{4,0},{5,1},{8,10},{9,11},{10,... | collective-permute-start | bytes 294920 | tf_op jit(solution)/shard_map/ppermute | solution.py:259
  22.8 6.8 %collective-permute-start.7 = (bf16[3,128,128]{2,1,0:T(8,128)(2,1)S(1)}, bf16[3,128,128]{2,1,0:T(8,128)(2,1)S(1)}, u32[]{:S(2)}, u32[]{:S(2)}) collective-permute-start(bf16[3,128,128]{2,1,0:T(8,128)(2,1)S(1)} %collective-permute-done.6.refs_3_.refs_1_), channel_id=1, source_target_pairs={{0,2},{1,3},{2,6},{3,7},{6,4},{7,5},{4,0},{5,1},{8,10},{9,11},{10,... | collective-permute-start | bytes 294920 | tf_op jit(solution)/shard_map/ppermute | solution.py:259
  25.8 9.1 %collective-permute-start.4 = (bf16[2,3,128,128]{3,2,1,0:T(8,128)(2,1)S(1)}, bf16[2,3,128,128]{3,2,1,0:T(8,128)(2,1)S(1)}, u32[]{:S(2)}, u32[]{:S(2)}) collective-permute-start(bf16[2,3,128,128]{3,2,1,0:T(8,128)(2,1)S(1)} %get-tuple-element.45), channel_id=1, source_target_pairs={{0,8},{8,0},{1,9},{9,1},{2,10},{10,2},{3,11},{11,3},{4,12},{12,4},... | collective-permute-start | bytes 589832 | tf_op jit(solution)/shard_map/ppermute | solution.py:377
  28.6 11.4 %collective-permute-start.11 = (bf16[3,128,128]{2,1,0:T(8,128)(2,1)S(1)}, bf16[3,128,128]{2,1,0:T(8,128)(2,1)S(1)}, u32[]{:S(2)}, u32[]{:S(2)}) collective-permute-start(bf16[3,128,128]{2,1,0:T(8,128)(2,1)S(1)} %collective-permute-done.10.refs_3_.refs_1_), channel_id=1, source_target_pairs={{0,2},{1,3},{2,6},{3,7},{6,4},{7,5},{4,0},{5,1},{8,10},{9,11},{10,... | collective-permute-start | bytes 294920 | tf_op jit(solution)/shard_map/ppermute | solution.py:259
  29.7 7.5 %collective-permute-start.8 = (bf16[3,128,128]{2,1,0:T(8,128)(2,1)S(1)}, bf16[3,128,128]{2,1,0:T(8,128)(2,1)S(1)}, u32[]{:S(2)}, u32[]{:S(2)}) collective-permute-start(bf16[3,128,128]{2,1,0:T(8,128)(2,1)S(1)} %collective-permute-done.7.refs_4_), channel_id=1, source_target_pairs={{0,2},{1,3},{2,6},{3,7},{6,4},{7,5},{4,0},{5,1},{8,10},{9,11},{10,... | collective-permute-start | bytes 294920 | tf_op jit(solution)/shard_map/ppermute | solution.py:259
  32.5 15.3 %collective-permute-start = (s32[3,1]{0,1:T(1,128)S(1)}, s32[3,1]{0,1:T(1,128)S(1)}, u32[]{:S(2)}, u32[]{:S(2)}) collective-permute-start(s32[3,1]{0,1:T(1,128)S(1)} %bitcast.77), channel_id=1, source_target_pairs={{0,8},{8,0},{1,9},{9,1},{2,10},{10,2},{3,11},{11,3},{4,12},{12,4},... | collective-permute-start | bytes 44 | tf_op jit(solution)/shard_map/ppermute | solution.py:296
  35.6 15.2 %collective-permute-start.5 = (bf16[2,2,3,128,128]{4,3,2,1,0:T(8,128)(2,1)S(1)}, bf16[2,2,3,128,128]{4,3,2,1,0:T(8,128)(2,1)S(1)}, u32[]{:S(2)}, u32[]{:S(2)}) collective-permute-start(bf16[2,2,3,128,128]{4,3,2,1,0:T(8,128)(2,1)S(1)} %join_tokens.4.refs_1_.refs_2_), channel_id=1, source_target_pairs={{0,1},{1,0},{2,3},{3,2},{4,5},{5,4},{6,7},{7,6},{8,9},{9,8},{10,11... | collective-permute-start | bytes 1179656 | tf_op jit(solution)/shard_map/ppermute | solution.py:249
  38.4 6.6 %collective-permute-start.14 = (bf16[3,128,128]{2,1,0:T(8,128)(2,1)S(1)}, bf16[3,128,128]{2,1,0:T(8,128)(2,1)S(1)}, u32[]{:S(2)}, u32[]{:S(2)}) collective-permute-start(bf16[3,128,128]{2,1,0:T(8,128)(2,1)S(1)} %feature_chunk.5.refs_2_), channel_id=1, source_target_pairs={{0,2},{1,3},{2,6},{3,7},{6,4},{7,5},{4,0},{5,1},{8,10},{9,11},{10,... | collective-permute-start | bytes 294920 | tf_op jit(solution)/shard_map/ppermute | solution.py:259
  39.5 5.7 %collective-permute-start.9 = (bf16[2,3,128,128]{3,2,1,0:T(8,128)(2,1)S(1)}, bf16[2,3,128,128]{3,2,1,0:T(8,128)(2,1)S(1)}, u32[]{:S(2)}, u32[]{:S(2)}) collective-permute-start(bf16[2,3,128,128]{3,2,1,0:T(8,128)(2,1)S(1)} %get-tuple-element.47), channel_id=1, source_target_pairs={{0,8},{8,0},{1,9},{9,1},{2,10},{10,2},{3,11},{11,3},{4,12},{12,4},... | collective-permute-start | bytes 589832 | tf_op jit(solution)/shard_map/ppermute | solution.py:377
  40.0 6.0 %collective-permute-start.12 = (bf16[3,128,128]{2,1,0:T(8,128)(2,1)S(1)}, bf16[3,128,128]{2,1,0:T(8,128)(2,1)S(1)}, u32[]{:S(2)}, u32[]{:S(2)}) collective-permute-start(bf16[3,128,128]{2,1,0:T(8,128)(2,1)S(1)} %collective-permute-done.11.refs_4_), channel_id=1, source_target_pairs={{0,2},{1,3},{2,6},{3,7},{6,4},{7,5},{4,0},{5,1},{8,10},{9,11},{10,... | collective-permute-start | bytes 294920 | tf_op jit(solution)/shard_map/ppermute | solution.py:259
  45.0 5.7 %collective-permute-start.15 = (bf16[3,128,128]{2,1,0:T(8,128)(2,1)S(1)}, bf16[3,128,128]{2,1,0:T(8,128)(2,1)S(1)}, u32[]{:S(2)}, u32[]{:S(2)}) collective-permute-start(bf16[3,128,128]{2,1,0:T(8,128)(2,1)S(1)} %collective-permute-done.14.refs_3_), channel_id=1, source_target_pairs={{0,2},{1,3},{2,6},{3,7},{6,4},{7,5},{4,0},{5,1},{8,10},{9,11},{10,... | collective-permute-start | bytes 294920 | tf_op jit(solution)/shard_map/ppermute | solution.py:259
  46.7 5.7 %collective-permute-start.13 = (bf16[2,3,128,128]{3,2,1,0:T(8,128)(2,1)S(1)}, bf16[2,3,128,128]{3,2,1,0:T(8,128)(2,1)S(1)}, u32[]{:S(2)}, u32[]{:S(2)}) collective-permute-start(bf16[2,3,128,128]{3,2,1,0:T(8,128)(2,1)S(1)} %get-tuple-element.49), channel_id=1, source_target_pairs={{0,8},{8,0},{1,9},{9,1},{2,10},{10,2},{3,11},{11,3},{4,12},{12,4},... | collective-permute-start | bytes 589832 | tf_op jit(solution)/shard_map/ppermute | solution.py:377
  47.8 15.4 %collective-permute-start.18 = (bf16[2,2,3,128,128]{4,3,2,1,0:T(8,128)(2,1)S(1)}, bf16[2,2,3,128,128]{4,3,2,1,0:T(8,128)(2,1)S(1)}, u32[]{:S(2)}, u32[]{:S(2)}) collective-permute-start(bf16[2,2,3,128,128]{4,3,2,1,0:T(8,128)(2,1)S(1)} %join_tokens.5.refs_1_.refs_3_), channel_id=1, source_target_pairs={{0,1},{1,0},{2,3},{3,2},{4,5},{5,4},{6,7},{7,6},{8,9},{9,8},{10,11... | collective-permute-start | bytes 1179656 | tf_op jit(solution)/shard_map/ppermute | solution.py:249
  50.7 5.5 %collective-permute-start.16 = (bf16[3,128,128]{2,1,0:T(8,128)(2,1)S(1)}, bf16[3,128,128]{2,1,0:T(8,128)(2,1)S(1)}, u32[]{:S(2)}, u32[]{:S(2)}) collective-permute-start(bf16[3,128,128]{2,1,0:T(8,128)(2,1)S(1)} %collective-permute-done.15.refs_4_), channel_id=1, source_target_pairs={{0,2},{1,3},{2,6},{3,7},{6,4},{7,5},{4,0},{5,1},{8,10},{9,11},{10,... | collective-permute-start | bytes 294920 | tf_op jit(solution)/shard_map/ppermute | solution.py:259
  53.0 13.3 %collective-permute-start.17 = (bf16[2,2,3,128,128]{4,3,2,1,0:T(8,128)(2,1)S(1)}, bf16[2,2,3,128,128]{4,3,2,1,0:T(8,128)(2,1)S(1)}, u32[]{:S(2)}, u32[]{:S(2)}) collective-permute-start(bf16[2,2,3,128,128]{4,3,2,1,0:T(8,128)(2,1)S(1)} %join_tokens.6.refs_1_), channel_id=1, source_target_pairs={{0,1},{1,0},{2,3},{3,2},{4,5},{5,4},{6,7},{7,6},{8,9},{9,8},{10,11... | collective-permute-start | bytes 1179656 | tf_op jit(solution)/shard_map/ppermute | solution.py:249
  57.1 6.1 %collective-permute-start.19 = (bf16[2,3,128,128]{3,2,1,0:T(8,128)(2,1)S(1)}, bf16[2,3,128,128]{3,2,1,0:T(8,128)(2,1)S(1)}, u32[]{:S(2)}, u32[]{:S(2)}) collective-permute-start(bf16[2,3,128,128]{3,2,1,0:T(8,128)(2,1)S(1)} %get-tuple-element.56), channel_id=1, source_target_pairs={{0,8},{8,0},{1,9},{9,1},{2,10},{10,2},{3,11},{11,3},{4,12},{12,4},... | collective-permute-start | bytes 589832 | tf_op jit(solution)/shard_map/ppermute | solution.py:377
  63.7 13.6 %collective-permute-start.20 = (bf16[2,2,3,128,128]{4,3,2,1,0:T(8,128)(2,1)S(1)}, bf16[2,2,3,128,128]{4,3,2,1,0:T(8,128)(2,1)S(1)}, u32[]{:S(2)}, u32[]{:S(2)}) collective-permute-start(bf16[2,2,3,128,128]{4,3,2,1,0:T(8,128)(2,1)S(1)} %join_tokens.7.refs_1_), channel_id=1, source_target_pairs={{0,1},{1,0},{2,3},{3,2},{4,5},{5,4},{6,7},{7,6},{8,9},{9,8},{10,11... | collective-permute-start | bytes 1179656 | tf_op jit(solution)/shard_map/ppermute | solution.py:249
  82.8 18.5 %copy-start = (bf16[4,768,512]{2,1,0:T(8,128)(2,1)}, bf16[4,768,512]{2,1,0:T(8,128)(2,1)S(1)}, u32[]{:S(2)}) copy-start(bf16[4,768,512]{2,1,0:T(8,128)(2,1)S(1)} %get-tuple-element.63.refs_4_.refs_6_) | copy-start | bytes 9437188
  82.8 45.4 %collective-permute-start.27 = (bf16[4,768,512]{2,1,0:T(8,128)(2,1)S(1)}, bf16[4,768,512]{2,1,0:T(8,128)(2,1)}, u32[]{:S(2)}, u32[]{:S(2)}) collective-permute-start(bf16[4,768,512]{2,1,0:T(8,128)(2,1)S(1)} %get-tuple-element.63.refs_4_.refs_6_), channel_id=1, source_target_pairs={{0,16},{16,0},{1,17},{17,1},{2,18},{18,2},{3,19},{19,3},{4,20},{20... | collective-permute-start | bytes 9437192 | tf_op jit(solution)/shard_map/ppermute | solution.py:266
  83.0 4.6 %collective-permute-start.21 = (f32[2,3,2000]{2,1,0:T(4,128)S(1)}, f32[2,3,2000]{2,1,0:T(4,128)S(1)}, u32[]{:S(2)}, u32[]{:S(2)}) collective-permute-start(f32[2,3,2000]{2,1,0:T(4,128)S(1)} %add_add_fusion), channel_id=1, source_target_pairs={{0,8},{8,0},{1,9},{9,1},{2,10},{10,2},{3,11},{11,3},{4,12},{12,4},... | collective-permute-start | bytes 144008 | tf_op jit(solution)/shard_map/ppermute | solution.py:396
  89.6 13.8 %collective-permute-start.23 = (f32[1]{0:T(128)}, f32[1]{0:T(128)}, u32[]{:S(2)}, u32[]{:S(2)}) collective-permute-start(f32[1]{0:T(128)} %bitcast.11), channel_id=1, source_target_pairs={{0,1},{1,0},{2,3},{3,2},{4,5},{5,4},{6,7},{7,6},{8,9},{9,8},{10,11... | collective-permute-start | bytes 20 | tf_op jit(solution)/shard_map/ppermute | solution.py:410
  101.4 20.5 %collective-permute-start.22 = (bf16[2,2,2,3,128,128]{5,4,3,2,1,0:T(8,128)(2,1)S(1)}, bf16[2,2,2,3,128,128]{5,4,3,2,1,0:T(8,128)(2,1)S(1)}, u32[]{:S(2)}, u32[]{:S(2)}) collective-permute-start(bf16[2,2,2,3,128,128]{5,4,3,2,1,0:T(8,128)(2,1)S(1)} %get-tuple-element.60), channel_id=1, source_target_pairs={{0,1},{1,0},{2,3},{3,2},{4,5},{5,4},{6,7},{7,6},{8,9},{9,8},{10,11... | collective-permute-start | bytes 2359304 | tf_op jit(solution)/shard_map/ppermute | solution.py:249
  104.2 10.6 %collective-permute-start.24 = (f32[2,7,2000]{2,1,0:T(8,128)S(1)}, f32[2,7,2000]{2,1,0:T(8,128)S(1)}, u32[]{:S(2)}, u32[]{:S(2)}) collective-permute-start(f32[2,7,2000]{2,1,0:T(8,128)S(1)} %pad_maximum_fusion.refs_1_), channel_id=1, source_target_pairs={{0,16},{16,0},{1,17},{17,1},{2,18},{18,2},{3,19},{19,3},{4,20},{20... | collective-permute-start | bytes 336008 | tf_op jit(solution)/shard_map/ppermute | solution.py:266
  114.7 26.7 %collective-permute-start.29 = (bf16[2,2,2,3,128,128]{5,4,3,2,1,0:T(8,128)(2,1)S(1)}, bf16[2,2,2,3,128,128]{5,4,3,2,1,0:T(8,128)(2,1)S(1)}, u32[]{:S(2)}, u32[]{:S(2)}) collective-permute-start(bf16[2,2,2,3,128,128]{5,4,3,2,1,0:T(8,128)(2,1)S(1)} %get-tuple-element.67), channel_id=1, source_target_pairs={{0,1},{1,0},{2,3},{3,2},{4,5},{5,4},{6,7},{7,6},{8,9},{9,8},{10,11... | collective-permute-start | bytes 2359304 | tf_op jit(solution)/shard_map/ppermute | solution.py:249
  116.2 7.5 %collective-permute-start.25 = (f32[2,1]{0,1:T(1,128)S(1)}, f32[2,1]{0,1:T(1,128)S(1)}, u32[]{:S(2)}, u32[]{:S(2)}) collective-permute-start(f32[2,1]{0,1:T(1,128)S(1)} %constant_dynamic-slice_fusion.2), channel_id=1, source_target_pairs={{0,2},{1,3},{2,0},{3,1},{4,6},{5,7},{6,4},{7,5},{8,10},{9,11},{10,... | collective-permute-start | bytes 32 | tf_op jit(solution)/shard_map/ppermute | solution.py:410
  119.8 20.1 %copy-start.2 = (f32[4000,12]{1,0:T(8,128)}, f32[4000,12]{1,0:T(8,128)S(1)}, u32[]{:S(2)}) copy-start(f32[4000,12]{1,0:T(8,128)S(1)} %turn_gradients.1.refs_6_.refs_8_) | copy-start | bytes 576004
  122.6 17.3 %collective-permute-start.28 = (bf16[2,2,3,128,128]{4,3,2,1,0:T(8,128)(2,1)S(1)}, bf16[2,2,3,128,128]{4,3,2,1,0:T(8,128)(2,1)S(1)}, u32[]{:S(2)}, u32[]{:S(2)}) collective-permute-start(bf16[2,2,3,128,128]{4,3,2,1,0:T(8,128)(2,1)S(1)} %get-tuple-element.65), channel_id=1, source_target_pairs={{0,8},{8,0},{1,9},{9,1},{2,10},{10,2},{3,11},{11,3},{4,12},{12,4},... | collective-permute-start | bytes 1179656 | tf_op jit(solution)/shard_map/ppermute | solution.py:539
  123.7 4.4 %collective-permute-start.26 = (f32[2,1]{0,1:T(1,128)S(1)}, f32[2,1]{0,1:T(1,128)S(1)}, u32[]{:S(2)}, u32[]{:S(2)}) collective-permute-start(f32[2,1]{0,1:T(1,128)S(1)} %fusion.14), channel_id=1, source_target_pairs={{0,4},{1,5},{2,6},{3,7},{4,0},{5,1},{6,2},{7,3},{8,12},{9,13},{10,... | collective-permute-start | bytes 32 | tf_op jit(solution)/shard_map/ppermute | solution.py:410
  128.2 23.1 %copy-start.1 = (bf16[4,768,512]{2,1,0:T(8,128)(2,1)S(1)}, bf16[4,768,512]{2,1,0:T(8,128)(2,1)}, u32[]{:S(2)}) copy-start(bf16[4,768,512]{2,1,0:T(8,128)(2,1)} %copy-done) | copy-start | bytes 9437188
  142.8 0.7 copy-start.5
  143.6 21.4 %collective-permute-start.32 = (bf16[2,2,3,128,128]{4,3,2,1,0:T(8,128)(2,1)}, bf16[2,2,3,128,128]{4,3,2,1,0:T(8,128)(2,1)}, u32[]{:S(2)}, u32[]{:S(2)}) collective-permute-start(bf16[2,2,3,128,128]{4,3,2,1,0:T(8,128)(2,1)} %get-tuple-element.73), channel_id=1, source_target_pairs={{0,8},{8,0},{1,9},{9,1},{2,10},{10,2},{3,11},{11,3},{4,12},{12,4},... | collective-permute-start | bytes 1179656 | tf_op jit(solution)/shard_map/ppermute | solution.py:539
  144.9 22.5 %collective-permute-start.33 = (bf16[2,3,128,128]{3,2,1,0:T(8,128)(2,1)}, bf16[2,3,128,128]{3,2,1,0:T(8,128)(2,1)S(1)}, u32[]{:S(2)}, u32[]{:S(2)}) collective-permute-start(bf16[2,3,128,128]{3,2,1,0:T(8,128)(2,1)} %get-tuple-element.75), channel_id=1, source_target_pairs={{0,2},{1,3},{2,4},{3,5},{4,6},{5,7},{6,0},{7,1},{8,10},{9,11},{10,... | collective-permute-start | bytes 589832 | tf_op jit(solution)/shard_map/ppermute | solution.py:263
  147.1 20.4 %collective-permute-start.34 = (bf16[2,3,128,128]{3,2,1,0:T(8,128)(2,1)}, bf16[2,3,128,128]{3,2,1,0:T(8,128)(2,1)}, u32[]{:S(2)}, u32[]{:S(2)}) collective-permute-start(bf16[2,3,128,128]{3,2,1,0:T(8,128)(2,1)} %get-tuple-element.76), channel_id=1, source_target_pairs={{0,4},{1,5},{2,6},{3,7},{4,0},{5,1},{6,2},{7,3},{8,12},{9,13},{10,... | collective-permute-start | bytes 589832 | tf_op jit(solution)/shard_map/ppermute | solution.py:263
  147.8 20.9 %collective-permute-start.35 = (bf16[2,3,128,128]{3,2,1,0:T(8,128)(2,1)}, bf16[2,3,128,128]{3,2,1,0:T(8,128)(2,1)}, u32[]{:S(2)}, u32[]{:S(2)}) collective-permute-start(bf16[2,3,128,128]{3,2,1,0:T(8,128)(2,1)} %get-tuple-element.77), channel_id=1, source_target_pairs={{0,6},{1,7},{2,0},{3,1},{4,2},{5,3},{6,4},{7,5},{8,14},{9,15},{10,... | collective-permute-start | bytes 589832 | tf_op jit(solution)/shard_map/ppermute | solution.py:263
  151.4 1.6 copy-start.3
  153.0 1.0 copy-start.6
  153.9 17.4 %copy-start.4 = (f32[4000,12]{1,0:T(8,128)S(1)}, f32[4000,12]{1,0:T(8,128)}, u32[]{:S(2)}) copy-start(f32[4000,12]{1,0:T(8,128)} %copy-done.2) | copy-start | bytes 576004
  165.0 22.0 %collective-permute-start.30 = (bf16[800,2048]{1,0:T(8,128)(2,1)}, bf16[800,2048]{1,0:T(8,128)(2,1)}, u32[]{:S(2)}, u32[]{:S(2)}) collective-permute-start(bf16[800,2048]{1,0:T(8,128)(2,1)} %get-tuple-element.70), channel_id=1, source_target_pairs={{0,16},{16,0},{1,17},{17,1},{2,18},{18,2},{3,19},{19,3},{4,20},{20... | collective-permute-start | bytes 9830408 | tf_op jit(solution)/shard_map/ppermute | solution.py:266
  165.0 17.0 %collective-permute-start.31 = (bf16[800,2048]{1,0:T(8,128)(2,1)}, bf16[800,2048]{1,0:T(8,128)(2,1)}, u32[]{:S(2)}, u32[]{:S(2)}) collective-permute-start(bf16[800,2048]{1,0:T(8,128)(2,1)} %get-tuple-element.71), channel_id=1, source_target_pairs={{0,16},{16,0},{1,17},{17,1},{2,18},{18,2},{3,19},{19,3},{4,20},{20... | collective-permute-start | bytes 9830408 | tf_op jit(solution)/shard_map/ppermute | solution.py:266
  167.4 24.5 %collective-permute-start.36 = (bf16[2,3,128,128]{3,2,1,0:T(8,128)(2,1)}, bf16[2,3,128,128]{3,2,1,0:T(8,128)(2,1)}, u32[]{:S(2)}, u32[]{:S(2)}) collective-permute-start(bf16[2,3,128,128]{3,2,1,0:T(8,128)(2,1)} %get-tuple-element.83), channel_id=1, source_target_pairs={{0,2},{1,3},{2,4},{3,5},{4,6},{5,7},{6,0},{7,1},{8,10},{9,11},{10,... | collective-permute-start | bytes 589832 | tf_op jit(solution)/shard_map/ppermute | solution.py:263
  167.5 24.5 %collective-permute-start.37 = (bf16[2,3,128,128]{3,2,1,0:T(8,128)(2,1)}, bf16[2,3,128,128]{3,2,1,0:T(8,128)(2,1)}, u32[]{:S(2)}, u32[]{:S(2)}) collective-permute-start(bf16[2,3,128,128]{3,2,1,0:T(8,128)(2,1)} %get-tuple-element.84), channel_id=1, source_target_pairs={{0,4},{1,5},{2,6},{3,7},{4,0},{5,1},{6,2},{7,3},{8,12},{9,13},{10,... | collective-permute-start | bytes 589832 | tf_op jit(solution)/shard_map/ppermute | solution.py:263
  168.7 23.3 %collective-permute-start.38 = (bf16[2,3,128,128]{3,2,1,0:T(8,128)(2,1)}, bf16[2,3,128,128]{3,2,1,0:T(8,128)(2,1)}, u32[]{:S(2)}, u32[]{:S(2)}) collective-permute-start(bf16[2,3,128,128]{3,2,1,0:T(8,128)(2,1)} %get-tuple-element.85), channel_id=1, source_target_pairs={{0,6},{1,7},{2,0},{3,1},{4,2},{5,3},{6,4},{7,5},{8,14},{9,15},{10,... | collective-permute-start | bytes 589832 | tf_op jit(solution)/shard_map/ppermute | solution.py:263

commit v4 on v2

--- a/solution.py
+++ b/solution.py
@@ -9,6 +9,7 @@
 
 LANES = 128
 VMEM_BYTES = 48 * 1024 * 1024
+HEAD_VMEM_BYTES = 58 * 1024 * 1024
 
 
 def shift_perm(count, shift):
@@ -17,6 +18,15 @@
 
 def waiting(kernel, count):
     return lambda *refs: kernel(refs[0], *refs[1 + count:])
+
+
+def marking(kernel, scratch):
+    def marked(*refs):
+        at = len(refs) - 1 - scratch
+        refs[at][...] = jnp.zeros_like(refs[at])
+        kernel(*refs[:at], *refs[at + 1:])
+
+    return marked
 
 
 def divisor(terms, limit):
@@ -271,30 +281,33 @@
     index_spec = pl.BlockSpec(memory_space=pltpu.SMEM)
     vmem_spec = pl.BlockSpec(memory_space=pltpu.VMEM)
     any_spec = pl.BlockSpec(memory_space=pl.ANY)
-    params = pltpu.CompilerParams(vmem_limit_bytes=VMEM_BYTES)
 
     def cost(flops, transferred):
         return pl.CostEstimate(flops=int(flops), bytes_accessed=int(transferred), transcendentals=0)
 
     owner_blocks = blocked(owner_pos)
     places = lax.rem(owner_blocks + (length - seq * part), length)
-    own_lengths = jnp.sum((token_ids != 0).astype(jnp.int32), axis=1, keepdims=True)
-    lengths = own_lengths
-    for s in range(1, slots):
-        lengths = lengths + lax.ppermute(own_lengths, "seq", shift_perm(slots, s))
-    validity = (owner_blocks < lengths[None]).astype(jnp.float32)
-
-    def run(kernel, name, operands, specs, shapes, out_specs=None, waits=(), flops=0, aliases={}, scratch=(), grid=()):
+    own_lengths = jnp.sum((token_ids != 0).astype(jnp.float32), axis=1)
+
+    def run(
+        kernel, name, operands, specs, shapes, out_specs=None, waits=(), flops=0, aliases={}, scratch=(), grid=(),
+        mark=False, limit=VMEM_BYTES,
+    ):
         waits = [value for value in waits if value is not None]
+        out_specs = list(out_specs or [vmem_spec] * len(shapes))
+        if mark:
+            kernel = marking(kernel, len(scratch))
+            shapes = list(shapes) + [jax.ShapeDtypeStruct((8, LANES), jnp.float32)]
+            out_specs.append(pl.BlockSpec((8, LANES), lambda *_: (0, 0)) if grid else vmem_spec)
         return pl.pallas_call(
             waiting(kernel, len(waits)),
             grid=grid,
             in_specs=[index_spec] + [any_spec] * len(waits) + specs,
-            out_specs=out_specs or [vmem_spec] * len(shapes),
+            out_specs=out_specs,
             out_shape=shapes,
             scratch_shapes=list(scratch),
             input_output_aliases={1 + len(waits) + i: o for i, o in aliases.items()},
-            compiler_params=params,
+            compiler_params=pltpu.CompilerParams(vmem_limit_bytes=limit),
             cost_estimate=cost(flops, flops // 64),
             name=name,
         )(index, *waits, *operands)
@@ -350,7 +363,7 @@
             held,
             [vmem_spec] * outer,
             [moved_shape] * slots,
-            waits=[gathered_chunks[c - 1] if c > 0 else None],
+            waits=[gathered_chunks[c - 1] if c > 0 else None, others[c - 2] if c > 1 else None],
         )
         arrived = [lax.ppermute(sends[s - 1], "seq", shift_perm(slots, -s)) for s in range(1, slots)]
         if c == last and c > 1:
@@ -366,12 +379,17 @@
         gathered_chunks.append(gathered)
         others.append(across_y(gathered, -1) if inner > 1 else None)
     for c in range(len(logit_parts), chunks):
-        add_logits(c, [validity, others[-2]] if c == 1 else [])
-
-    logit_part = functools.reduce(jnp.add, logit_parts)
-    logits = logit_part
+        add_logits(c, [others[-2]] if c == 1 else [])
+
+    logits = functools.reduce(jnp.add, logit_parts)
+    lengths = own_lengths
+    length_row = jnp.broadcast_to(jnp.pad(own_lengths, (0, columns - docs)).reshape(1, 1, columns), (steps, 1, columns))
+    counted = jnp.concatenate([logits, length_row], axis=1)
     for s in range(1, slots):
-        logits = logits + lax.ppermute(logit_part, "seq", shift_perm(slots, s))
+        arrived = lax.ppermute(counted, "seq", shift_perm(slots, s))
+        logits = logits + arrived[:, :docs]
+        lengths = lengths + arrived[0, docs, :docs]
+    validity = (owner_blocks < lengths[None, :, None].astype(jnp.int32)).astype(jnp.float32)
     softened = jax.nn.softplus(logits)
     pooled = validity * jnp.log1p(softened)
     slopes = validity * jax.nn.sigmoid(logits) / (1.0 + softened)
@@ -445,16 +463,18 @@
             aliases={2 + groups: 0} if previous else {},
             scratch=[pltpu.VMEM((head_terms, groups * tokens), jnp.bfloat16)],
             grid=(count, strips),
+            limit=HEAD_VMEM_BYTES,
         )
         next_range += count
 
     half = -(-chunks // 2)
     chunk_groups = [members for members in (range(half), range(half, chunks)) if members]
     pairs = []
+    marks = []
     for members in chunk_groups:
         pair_shape = (len(members), *piece_shape)
         lanes = len(members) * strips * width
-        sums = run(
+        *sums, mark = run(
             functools.partial(hidden_kernel, docs, inner, len(members) * strips, pair_shape),
             "hidden_terms",
             [head_rows] * (len(members) * strips) + [places, unscaled],
@@ -462,10 +482,12 @@
             [bf16(*pair_shape)] * inner,
             out_specs=[pl.BlockSpec(pair_shape, lambda v: (0,) * 6)] * inner,
             waits=[packed] if pairs else [],
+            mark=True,
             flops=2 * tokens * lanes * terms // 4,
             scratch=[pltpu.VMEM((tokens, columns), jnp.bfloat16), pltpu.VMEM((tokens, lanes), jnp.float32)],
             grid=(steps,),
         )
+        marks.append(mark)
         pairs.append([sums[0]] + [across_y(sums[q], q) for q in range(1, inner)])
 
     share = ranges // 5
@@ -474,35 +496,39 @@
 
     def add_blocks(pair, *waits):
         count = pair[0].shape[0]
-        mine = run(
+        *mine, mark = run(
             functools.partial(combine_kernel, inner, slots),
             "add_blocks",
             pair,
             [vmem_spec] * inner,
             [bf16(count, near, docs, part, width)] * slots,
             waits=waits,
+            mark=True,
         )
         mine_all.append([mine[0]] + [lax.ppermute(mine[s], "seq", shift_perm(slots, s)) for s in range(1, slots)])
+        return mark
 
     def sort_pieces(mine, *waits):
-        pieces = run(
+        *pieces, mark = run(
             functools.partial(sort_kernel, slots, near, outer),
             "sort_pieces",
             mine,
             [vmem_spec] * slots,
             [bf16(mine[0].shape[0], docs, part, width)] * outer,
             waits=waits,
+            mark=True,
         )
         arrived_all.append([pieces[0]] + [across_z(pieces[ahead], ahead) for ahead in range(1, outer)])
-
-    add_blocks(pairs[0])
-    run_head(2 * share, mine_all[0][0], pairs[-1][0])
-    sort_pieces(mine_all[0], token)
+        return mark
+
+    added = add_blocks(pairs[0])
+    run_head(2 * share, added, marks[-1])
+    sorted_mark = sort_pieces(mine_all[0], token)
     if len(pairs) > 1:
-        add_blocks(pairs[1], arrived_all[0][0])
-        run_head(share, arrived_all[0][0], mine_all[1][0])
-        sort_pieces(mine_all[1], token)
-    run_head(ranges - next_range, arrived_all[-1][0])
+        added = add_blocks(pairs[1], sorted_mark)
+        run_head(share, sorted_mark, added)
+        sorted_mark = sort_pieces(mine_all[1], token)
+    run_head(ranges - next_range, sorted_mark)
     (grad_hidden,) = run(
         functools.partial(finish_kernel, [len(members) for members in chunk_groups], outer),
         "scale_hidden",

time: 191 us -> 200 us (1.047)
  waiting for transfers between devices: 21.7 us -> 29.2 us
  starting transfers between devices: 51.6 us -> 47.9 us
  Pallas kernels: 103 us -> 105 us
    ppermute x12, waiting for transfers between devices: 4.15 us -> 22.6 us  [around_ring(): return lax.ppermute(value, 'vocab', perm)]
    ppermute x12, starting transfers between devices: 24.9 us -> 15.9 us  [around_ring(): return lax.ppermute(value, 'vocab', perm)]
    ppermute x4, waiting for transfers between devices: 7.46 us -> 3.2 us  [on_device(): lax.ppermute(sends[s - 1], 'seq', shift_perm(slots, -s))]
    ppermute x6, waiting for transfers between devices: 4.34 us -> 0.36 us  [across_y(): return lax.ppermute(value, 'vocab', perm)]
    ppermute x3, waiting for transfers between devices: 2.56 us -> 0.01 us  [add_distance(): lax.ppermute(value, 'vocab', [(i, i ^ distance) for i in range(blocks)])]
    ppermute x3, starting transfers between devices: 3.73 us -> 6.26 us  [add_distance(): lax.ppermute(value, 'vocab', [(i, i ^ distance) for i in range(blocks)])]
    unnamed x18 -> x48, local copies, waits for them, and re-layouts: 3.37 us -> 5.86 us
  transfers between devices with their start and end apart: 37 -> 36, of which waited for: 10 -> 11; matrix products, arithmetic and copies ran while one was open for 3% -> 3% of each run, Pallas kernels for 49% -> 48%
where the time goes in v4:
time: 200 us; the launch traced here: 199 us
  Pallas kernels  105 us (52%)
  starting transfers between devices  47.9 us (24%)
  waiting for transfers between devices  29.2 us (15%)
  local copies, waits for them, and re-layouts  8.44 us (4%)
  other arithmetic  4.27 us (2%)
  between operations  3.78 us (2%)
    pallas_call x26, Pallas kernels, run(): pl.pallas_call(waiting(kernel, len(waits)), grid=grid, in_specs=[index_sp...  105 us
    ppermute x12, waiting for transfers between devices, around_ring(): return lax.ppermute(value, 'vocab', perm)  22.6 us
    ppermute x12, starting transfers between devices, around_ring(): return lax.ppermute(value, 'vocab', perm)  15.9 us
    ppermute x6, starting transfers between devices, across_z(): return lax.ppermute(value, 'vocab', perm)  8.82 us
    ppermute x6, starting transfers between devices, across_y(): return lax.ppermute(value, 'vocab', perm)  8.05 us
    ppermute x3, starting transfers between devices, add_distance(): lax.ppermute(value, 'vocab', [(i, i ^ distance) for i in range(blocks)])  6.26 us
    unnamed x48, local copies, waits for them, and re-layouts  5.86 us
    ppermute x4, starting transfers between devices, on_device(): lax.ppermute(sends[s - 1], 'seq', shift_perm(slots, -s))  5.75 us
  transfers between devices with their start and end apart: 36, of which 11 were waited for; matrix products, arithmetic and copies ran while one was open for 3% of the time, Pallas kernels for 48%

profile of v4, /device:TPU:0, one launch (start us, length us, event | category | flops | bytes accessed | tf_op | source)
XLA Modules:
  0.0 198.7 jit_solution(12177434700049905339)
XLA Ops:
  0.6 1.1 fusion.12
  1.7 4.1 %collective-permute-start.2 = (bf16[3,128,128]{2,1,0:T(8,128)(2,1)S(1)}, bf16[3,128,128]{2,1,0:T(8,128)(2,1)S(1)}, u32[]{:S(2)}, u32[]{:S(2)}) collective-permute-start(bf16[3,128,128]{2,1,0:T(8,128)(2,1)S(1)} %get-tuple-element.92.refs_1_), channel_id=1, source_target_pairs={{0,4},{1,5},{2,0},{3,1},{6,2},{7,3},{4,6},{5,7},{8,12},{9,13},{10,... | collective-permute-start | bytes 294920 | tf_op jit(solution)/shard_map/ppermute | solution.py:257
  5.8 1.3 collective-permute-start.1
  7.2 0.8 collective-permute-start
  8.1 1.0 collective-permute-done.2.refs_4_
  9.0 4.0 %collective-permute-done.1.refs_3_ = bf16[3,128,128]{2,1,0:T(8,128)(2,1)S(1)} collective-permute-done((bf16[3,128,128]{2,1,0:T(8,128)(2,1)S(1)}, bf16[3,128,128]{2,1,0:T(8,128)(2,1)S(1)}, u32[]{:S(2)}, u32[]{:S(2)}) %collective-permute-start.1) | collective-permute-done | bytes 98336 | tf_op jit(solution)/shard_map/ppermute | solution.py:257
  13.0 3.0 %collective-permute-done.refs_2_.refs_1_ = bf16[3,128,128]{2,1,0:T(8,128)(2,1)S(1)} collective-permute-done((bf16[3,128,128]{2,1,0:T(8,128)(2,1)S(1)}, bf16[3,128,128]{2,1,0:T(8,128)(2,1)S(1)}, u32[]{:S(2)}, u32[]{:S(2)}) %collective-permute-start) | collective-permute-done | bytes 98336 | tf_op jit(solution)/shard_map/ppermute | solution.py:257
  16.0 0.7 pick_halves.4
  16.7 1.6 collective-permute-start.3
  18.9 5.5 %collective-permute-done.5.refs_3_.refs_1_ = bf16[3,128,128]{2,1,0:T(8,128)(2,1)S(1)} collective-permute-done((bf16[3,128,128]{2,1,0:T(8,128)(2,1)S(1)}, bf16[3,128,128]{2,1,0:T(8,128)(2,1)S(1)}, u32[]{:S(2)}, u32[]{:S(2)}) %collective-permute-start.5) | collective-permute-done | bytes 98336 | tf_op jit(solution)/shard_map/ppermute | solution.py:257
  25.0 1.6 collective-permute-start.4
  26.5 3.3 %collective-permute-done.6.refs_4_ = bf16[3,128,128]{2,1,0:T(8,128)(2,1)S(1)} collective-permute-done((bf16[3,128,128]{2,1,0:T(8,128)(2,1)S(1)}, bf16[3,128,128]{2,1,0:T(8,128)(2,1)S(1)}, u32[]{:S(2)}, u32[]{:S(2)}) %collective-permute-start.6) | collective-permute-done | bytes 98336 | tf_op jit(solution)/shard_map/ppermute | solution.py:257
  30.4 3.1 %collective-permute-start.9 = (bf16[3,128,128]{2,1,0:T(8,128)(2,1)S(1)}, bf16[3,128,128]{2,1,0:T(8,128)(2,1)S(1)}, u32[]{:S(2)}, u32[]{:S(2)}) collective-permute-start(bf16[3,128,128]{2,1,0:T(8,128)(2,1)S(1)} %feature_chunk.4.refs_3_), channel_id=1, source_target_pairs={{0,2},{1,3},{2,6},{3,7},{6,4},{7,5},{4,0},{5,1},{8,10},{9,11},{10,... | collective-permute-start | bytes 294920 | tf_op jit(solution)/shard_map/ppermute | solution.py:257
  33.5 1.9 collective-permute-done.7.refs_5_
  35.4 0.7 pick_halves.5
  36.7 1.7 collective-permute-start.10
  39.0 1.4 collective-permute-start.14
  40.3 2.6 %collective-permute-done.10.refs_5_ = bf16[3,128,128]{2,1,0:T(8,128)(2,1)S(1)} collective-permute-done((bf16[3,128,128]{2,1,0:T(8,128)(2,1)S(1)}, bf16[3,128,128]{2,1,0:T(8,128)(2,1)S(1)}, u32[]{:S(2)}, u32[]{:S(2)}) %collective-permute-start.10) | collective-permute-done | bytes 98336 | tf_op jit(solution)/shard_map/ppermute | solution.py:257
  42.9 1.1 collective-permute-start.11
  44.2 1.3 collective-permute-done.14.refs_4_
  45.5 1.0 collective-permute-start.15
  47.1 1.6 collective-permute-start.13
  48.7 0.7 pick_halves.6
  49.3 1.5 collective-permute-start.12
  50.9 0.7 fusion.11
  51.6 1.4 collective-permute-start.16
  52.9 3.2 %collective-permute-done.12.refs_3_ = bf16[2,3,128,128]{3,2,1,0:T(8,128)(2,1)S(1)} collective-permute-done((bf16[2,3,128,128]{3,2,1,0:T(8,128)(2,1)S(1)}, bf16[2,3,128,128]{3,2,1,0:T(8,128)(2,1)S(1)}, u32[]{:S(2)}, u32[]{:S(2)}) %collective-permute-start.12) | collective-permute-done | bytes 196640 | tf_op jit(solution)/shard_map/ppermute | solution.py:368
  56.7 1.1 collective-permute-start.17
  58.3 0.9 pick_halves.7
  59.2 2.1 %collective-permute-start.18 = (bf16[2,3,128,128]{3,2,1,0:T(8,128)(2,1)S(1)}, bf16[2,3,128,128]{3,2,1,0:T(8,128)(2,1)S(1)}, u32[]{:S(2)}, u32[]{:S(2)}) collective-permute-start(bf16[2,3,128,128]{3,2,1,0:T(8,128)(2,1)S(1)} %get-tuple-element.57), channel_id=1, source_target_pairs={{0,8},{8,0},{1,9},{9,1},{2,10},{10,2},{3,11},{11,3},{4,12},{12,4},... | collective-permute-start | bytes 589832 | tf_op jit(solution)/shard_map/ppermute | solution.py:368
  61.3 1.0 copy-done.3
  62.2 5.5 %pooled_logits.4 = (f32[2,3,2000]{2,1,0:T(4,128)S(1)}, bf16[4,768,512]{2,1,0:T(8,128)(2,1)S(1)}) custom-call(s32[4]{0:T(128)S(1)} %pad_add_fusion.refs_0_, bf16[2,3,128,128]{3,2,1,0:T(8,128)(2,1)S(1)} %get-tuple-element.51.refs_1_.refs_3_, bf16[2,2,3,128,128]{4,3,2,1,0:T(8,128)(2,1)S(1)} %join_tokens.4.refs_1_.refs_2_, ...), custom_call_target="tpu_custom_call" | custom-call | flops 3145728000 | bytes 49152000 | tf_op jit(solution)/shard_map/pooled_logits/pallas_call | solution.py:302
  68.3 1.6 collective-permute-start.19
  69.9 5.5 %pooled_logits.5 = (f32[2,3,2000]{2,1,0:T(4,128)S(1)}, bf16[4,768,512]{2,1,0:T(8,128)(2,1)S(1)}) custom-call(s32[4]{0:T(128)S(1)} %pad_add_fusion.refs_0_, bf16[2,2,3,128,128]{4,3,2,1,0:T(8,128)(2,1)S(1)} %collective-permute-done.17.refs_1_.refs_2_, bf16[2,2,3,128,128]{4,3,2,1,0:T(8,128)(2,1)S(1)} %join_tokens.5.refs_1_.refs_2_, ...), custom_call_target="tpu_custom_call", output_to_operand_aliasing={{1}: (9, {})} | custom-call | flops 3145728000 | bytes 49152000 | tf_op jit(solution)/shard_map/pooled_logits/pallas_call | solution.py:302
  75.4 5.5 %pooled_logits.6 = (f32[2,3,2000]{2,1,0:T(4,128)S(1)}, bf16[4,768,512]{2,1,0:T(8,128)(2,1)S(1)}) custom-call(s32[4]{0:T(128)S(1)} %pad_add_fusion.refs_0_, bf16[2,2,3,128,128]{4,3,2,1,0:T(8,128)(2,1)S(1)} %join_tokens.6.refs_1_, bf16[2,2,3,128,128]{4,3,2,1,0:T(8,128)(2,1)S(1)} %collective-permute-done.17.refs_1_.refs_2_, ...), custom_call_target="tpu_custom_call", output_to_operand_aliasing={{1}: (8, {})} | custom-call | flops 3145728000 | bytes 49152000 | tf_op jit(solution)/shard_map/pooled_logits/pallas_call | solution.py:302
  80.9 5.5 %pooled_logits.7 = (f32[2,3,2000]{2,1,0:T(4,128)S(1)}, bf16[4,768,512]{2,1,0:T(8,128)(2,1)S(1)}) custom-call(s32[4]{0:T(128)S(1)} %pad_add_fusion.refs_0_, bf16[2,2,3,128,128]{4,3,2,1,0:T(8,128)(2,1)S(1)} %join_tokens.7.refs_1_, bf16[2,2,3,128,128]{4,3,2,1,0:T(8,128)(2,1)S(1)} %collective-permute-done.19.refs_2_, ...), custom_call_target="tpu_custom_call", output_to_operand_aliasing={{1}: (8, {})} | custom-call | flops 3145728000 | bytes 49152000 | tf_op jit(solution)/shard_map/pooled_logits/pallas_call | solution.py:302
  86.6 0.9 collective-permute-start.20
  88.1 3.0 %collective-permute-done.20 = f32[2,4,2000]{2,1,0:T(4,128)S(1)} collective-permute-done((f32[2,4,2000]{2,1,0:T(4,128)S(1)}, f32[2,4,2000]{2,1,0:T(4,128)S(1)}, u32[]{:S(2)}, u32[]{:S(2)}) %collective-permute-start.20) | collective-permute-done | bytes 64032 | tf_op jit(solution)/shard_map/ppermute | solution.py:389
  91.3 0.7 multiply_reduce_fusion
  93.3 1.9 collective-permute-start.22
  95.4 0.8 copy-done.5
  96.2 10.8 %hidden_terms.2 = (bf16[2,2,2,3,128,128]{5,4,3,2,1,0:T(8,128)(2,1)S(1)}, bf16[2,2,2,3,128,128]{5,4,3,2,1,0:T(8,128)(2,1)S(1)}, f32[8,128]{1,0:T(8,128)}) custom-call(s32[4]{0:T(128)S(1)} %pad_add_fusion.refs_0_, bf16[4000,2048]{1,0:T(8,128)(2,1)} %bitcast.62, bf16[4000,2048]{1,0:T(8,128)(2,1)} %bitcast.63, bf16[4000,2048]{1,0:T(8,128)(2,1)} %bitcast.64, ...), custom_call_target="tpu_custom_call" | custom-call | flops 1572864000 | bytes 24576000 | tf_op jit(solution)/shard_map/hidden_terms/pallas_call | solution.py:302
  107.0 1.6 collective-permute-start.21
  109.5 11.3 %hidden_terms.3 = (bf16[2,2,2,3,128,128]{5,4,3,2,1,0:T(8,128)(2,1)S(1)}, bf16[2,2,2,3,128,128]{5,4,3,2,1,0:T(8,128)(2,1)}, f32[8,128]{1,0:T(8,128)S(1)}) custom-call(s32[4]{0:T(128)S(1)} %pad_add_fusion.refs_0_, f32[2,7,2000]{2,1,0:T(8,128)S(1)} %pad_maximum_fusion.refs_1_, bf16[4000,2048]{1,0:T(8,128)(2,1)} %bitcast.70, bf16[4000,2048]{1,0:T(8,128)(2,1)} %bitcast.71, ...), custom_call_target="tpu_custom_call" | custom-call | flops 1572864000 | bytes 24576000 | tf_op jit(solution)/shard_map/hidden_terms/pallas_call | solution.py:302
  122.0 0.7 pad_maximum_fusion.2
  122.8 1.2 collective-permute-start.24
  124.0 1.3 turn_gradients.1.refs_6_.refs_5_
  125.3 1.4 copy-done.1
  126.6 0.8 pad_maximum_fusion.3
  127.5 3.2 %collective-permute-start.25 = (f32[2,1]{0,1:T(1,128)S(1)}, f32[2,1]{0,1:T(1,128)S(1)}, u32[]{:S(2)}, u32[]{:S(2)}) collective-permute-start(f32[2,1]{0,1:T(1,128)S(1)} %fusion.14), channel_id=1, source_target_pairs={{0,4},{1,5},{2,6},{3,7},{4,0},{5,1},{6,2},{7,3},{8,12},{9,13},{10,... | collective-permute-start | bytes 32 | tf_op jit(solution)/shard_map/ppermute | solution.py:406
  130.7 1.4 add_blocks.2
  132.1 0.8 collective-permute-start.27
  133.5 18.5 %head_terms.3 = (f32[4000,2048]{1,0:T(8,128)}, f32[8,128]{1,0:T(8,128)}) custom-call(s32[4]{0:T(128)} %copy-done.6, f32[8,128]{1,0:T(8,128)} %copy-done.17, f32[8,128]{1,0:T(8,128)} %copy-done.16, f32[2]{0:T(128)} %bitcast.79, bf16[4,768,512]{2,1,0:T(8,128)(2,1)} %copy-done, bf16[4,768,512]{2,1,0:T(8,128)(2,1)} %collective-permute-done.26.refs_5_.refs_4_, ...), custom_call_target="tpu_custom_call" | custom-call | flops 2516582400 | bytes 39321600 | tf_op jit(solution)/shard_map/head_terms/pallas_call | solution.py:302
  152.1 0.7 copy-done.15
  152.7 0.7 sort_pieces.2
  153.4 0.7 add_blocks.3
  154.8 1.2 collective-permute-start.29
  156.7 1.9 collective-permute-start.31
  158.6 2.8 %collective-permute-start.32 = (bf16[2,3,128,128]{3,2,1,0:T(8,128)(2,1)S(1)}, bf16[2,3,128,128]{3,2,1,0:T(8,128)(2,1)S(1)}, u32[]{:S(2)}, u32[]{:S(2)}) collective-permute-start(bf16[2,3,128,128]{3,2,1,0:T(8,128)(2,1)S(1)} %get-tuple-element.83), channel_id=1, source_target_pairs={{0,6},{1,7},{2,0},{3,1},{4,2},{5,3},{6,4},{7,5},{8,14},{9,15},{10,... | collective-permute-start | bytes 589832 | tf_op jit(solution)/shard_map/ppermute | solution.py:261
  161.3 10.3 %head_terms.4 = (f32[4000,2048]{1,0:T(8,128)}, f32[8,128]{1,0:T(8,128)}) custom-call(s32[4]{0:T(128)} %copy-done.6, f32[8,128]{1,0:T(8,128)} %copy-done.10, f32[8,128]{1,0:T(8,128)} %copy-done.12, f32[2]{0:T(128)} %bitcast.80, bf16[4,768,512]{2,1,0:T(8,128)(2,1)} %copy-done, ...), custom_call_target="tpu_custom_call", output_to_operand_aliasing={{0}: (7, {})} | custom-call | flops 1258291200 | bytes 19660800 | tf_op jit(solution)/shard_map/head_terms/pallas_call | solution.py:302
  173.1 1.1 collective-permute-start.34
  174.2 2.8 %collective-permute-start.35 = (bf16[2,3,128,128]{3,2,1,0:T(8,128)(2,1)S(1)}, bf16[2,3,128,128]{3,2,1,0:T(8,128)(2,1)S(1)}, u32[]{:S(2)}, u32[]{:S(2)}) collective-permute-start(bf16[2,3,128,128]{3,2,1,0:T(8,128)(2,1)S(1)} %get-tuple-element.87), channel_id=1, source_target_pairs={{0,6},{1,7},{2,0},{3,1},{4,2},{5,3},{6,4},{7,5},{8,14},{9,15},{10,... | collective-permute-start | bytes 589832 | tf_op jit(solution)/shard_map/ppermute | solution.py:261
  177.1 18.8 %head_terms.5 = (f32[4000,2048]{1,0:T(8,128)}, f32[8,128]{1,0:T(8,128)}) custom-call(s32[4]{0:T(128)} %copy-done.6, f32[8,128]{1,0:T(8,128)} %copy-done.13, f32[2]{0:T(128)} %bitcast.81, bf16[4,768,512]{2,1,0:T(8,128)(2,1)} %copy-done, bf16[4,768,512]{2,1,0:T(8,128)(2,1)} %collective-permute-done.26.refs_5_.refs_4_, ...), custom_call_target="tpu_custom_call", output_to_operand_aliasing={{0}: (6, {})} | custom-call | flops 2516582400 | bytes 39321600 | tf_op jit(solution)/shard_map/head_terms/pallas_call | solution.py:302
  196.6 2.1 %scale_hidden.1 = bf16[3,128,512]{2,1,0:T(8,128)(2,1)} custom-call(s32[4]{0:T(128)S(1)} %copy-done.9, f32[8,128]{1,0:T(8,128)S(1)} %copy-done.11, f32[1]{0:T(128)} %bitcast.19.refs_2_, bf16[2,3,128,128]{3,2,1,0:T(8,128)(2,1)S(1)} %get-tuple-element.80.refs_3_, bf16[2,3,128,128]{3,2,1,0:T(8,128)(2,1)S(1)} %collective-permute-done.30.refs_4_, ...), custom_call_target="tpu_custom_call" | custom-call | tf_op jit(solution)/shard_map/scale_hidden/pallas_call | solution.py:302
  (105 shorter events, 11.4 us)
Async XLA Ops:
  0.6 43.4 %copy-start.21 = (s32[3,4000]{1,0:T(4,128)S(1)}, s32[3,4000]{1,0:T(4,128)}, u32[]{:S(2)}) copy-start(s32[3,4000]{1,0:T(4,128)} %param.7) | copy-start | bytes 144004
  1.7 7.3 %collective-permute-start.2 = (bf16[3,128,128]{2,1,0:T(8,128)(2,1)S(1)}, bf16[3,128,128]{2,1,0:T(8,128)(2,1)S(1)}, u32[]{:S(2)}, u32[]{:S(2)}) collective-permute-start(bf16[3,128,128]{2,1,0:T(8,128)(2,1)S(1)} %get-tuple-element.92.refs_1_), channel_id=1, source_target_pairs={{0,4},{1,5},{2,0},{3,1},{6,2},{7,3},{4,6},{5,7},{8,12},{9,13},{10,... | collective-permute-start | bytes 294920 | tf_op jit(solution)/shard_map/ppermute | solution.py:257
  5.8 7.2 %collective-permute-start.1 = (bf16[3,128,128]{2,1,0:T(8,128)(2,1)S(1)}, bf16[3,128,128]{2,1,0:T(8,128)(2,1)S(1)}, u32[]{:S(2)}, u32[]{:S(2)}) collective-permute-start(bf16[3,128,128]{2,1,0:T(8,128)(2,1)S(1)} %get-tuple-element.92.refs_1_), channel_id=1, source_target_pairs={{0,6},{1,7},{2,4},{3,5},{6,0},{7,1},{4,2},{5,3},{8,14},{9,15},{10,... | collective-permute-start | bytes 294920 | tf_op jit(solution)/shard_map/ppermute | solution.py:257
  7.2 8.8 %collective-permute-start = (bf16[3,128,128]{2,1,0:T(8,128)(2,1)S(1)}, bf16[3,128,128]{2,1,0:T(8,128)(2,1)S(1)}, u32[]{:S(2)}, u32[]{:S(2)}) collective-permute-start(bf16[3,128,128]{2,1,0:T(8,128)(2,1)S(1)} %get-tuple-element.92.refs_1_), channel_id=1, source_target_pairs={{0,2},{1,3},{2,6},{3,7},{6,4},{7,5},{4,0},{5,1},{8,10},{9,11},{10,... | collective-permute-start | bytes 294920 | tf_op jit(solution)/shard_map/ppermute | solution.py:257
  8.1 122.6 %copy-start.6 = (s32[4]{0:T(128)}, s32[4]{0:T(128)S(1)}, u32[]{:S(2)}) copy-start(s32[4]{0:T(128)S(1)} %pad_add_fusion.refs_0_) | copy-start | bytes 52
  8.1 49.8 %copy-start.23 = (s32[3,128]{1,0:T(4,128)S(1)}, s32[3,128]{1,0:T(4,128)}, u32[]{:S(2)}) copy-start(s32[3,128]{1,0:T(4,128)} %param.8) | copy-start | bytes 4612
  16.7 7.7 %collective-permute-start.3 = (bf16[2,3,128,128]{3,2,1,0:T(8,128)(2,1)S(1)}, bf16[2,3,128,128]{3,2,1,0:T(8,128)(2,1)S(1)}, u32[]{:S(2)}, u32[]{:S(2)}) collective-permute-start(bf16[2,3,128,128]{3,2,1,0:T(8,128)(2,1)S(1)} %get-tuple-element.46), channel_id=1, source_target_pairs={{0,8},{8,0},{1,9},{9,1},{2,10},{10,2},{3,11},{11,3},{4,12},{12,4},... | collective-permute-start | bytes 589832 | tf_op jit(solution)/shard_map/ppermute | solution.py:368
  18.8 5.6 %collective-permute-start.5 = (bf16[3,128,128]{2,1,0:T(8,128)(2,1)S(1)}, bf16[3,128,128]{2,1,0:T(8,128)(2,1)S(1)}, u32[]{:S(2)}, u32[]{:S(2)}) collective-permute-start(bf16[3,128,128]{2,1,0:T(8,128)(2,1)S(1)} %feature_chunk.3.refs_2_), channel_id=1, source_target_pairs={{0,2},{1,3},{2,6},{3,7},{6,4},{7,5},{4,0},{5,1},{8,10},{9,11},{10,... | collective-permute-start | bytes 294920 | tf_op jit(solution)/shard_map/ppermute | solution.py:257
  24.4 5.5 %collective-permute-start.6 = (bf16[3,128,128]{2,1,0:T(8,128)(2,1)S(1)}, bf16[3,128,128]{2,1,0:T(8,128)(2,1)S(1)}, u32[]{:S(2)}, u32[]{:S(2)}) collective-permute-start(bf16[3,128,128]{2,1,0:T(8,128)(2,1)S(1)} %collective-permute-done.5.refs_3_.refs_1_), channel_id=1, source_target_pairs={{0,2},{1,3},{2,6},{3,7},{6,4},{7,5},{4,0},{5,1},{8,10},{9,11},{10,... | collective-permute-start | bytes 294920 | tf_op jit(solution)/shard_map/ppermute | solution.py:257
  25.0 23.7 %collective-permute-start.4 = (bf16[2,2,3,128,128]{4,3,2,1,0:T(8,128)(2,1)S(1)}, bf16[2,2,3,128,128]{4,3,2,1,0:T(8,128)(2,1)S(1)}, u32[]{:S(2)}, u32[]{:S(2)}) collective-permute-start(bf16[2,2,3,128,128]{4,3,2,1,0:T(8,128)(2,1)S(1)} %join_tokens.4.refs_1_.refs_2_), channel_id=1, source_target_pairs={{0,1},{1,0},{2,3},{3,2},{4,5},{5,4},{6,7},{7,6},{8,9},{9,8},{10,11... | collective-permute-start | bytes 1179656 | tf_op jit(solution)/shard_map/ppermute | solution.py:247
  29.9 5.5 %collective-permute-start.7 = (bf16[3,128,128]{2,1,0:T(8,128)(2,1)S(1)}, bf16[3,128,128]{2,1,0:T(8,128)(2,1)S(1)}, u32[]{:S(2)}, u32[]{:S(2)}) collective-permute-start(bf16[3,128,128]{2,1,0:T(8,128)(2,1)S(1)} %collective-permute-done.6.refs_4_), channel_id=1, source_target_pairs={{0,2},{1,3},{2,6},{3,7},{6,4},{7,5},{4,0},{5,1},{8,10},{9,11},{10,... | collective-permute-start | bytes 294920 | tf_op jit(solution)/shard_map/ppermute | solution.py:257
  30.4 6.2 %collective-permute-start.9 = (bf16[3,128,128]{2,1,0:T(8,128)(2,1)S(1)}, bf16[3,128,128]{2,1,0:T(8,128)(2,1)S(1)}, u32[]{:S(2)}, u32[]{:S(2)}) collective-permute-start(bf16[3,128,128]{2,1,0:T(8,128)(2,1)S(1)} %feature_chunk.4.refs_3_), channel_id=1, source_target_pairs={{0,2},{1,3},{2,6},{3,7},{6,4},{7,5},{4,0},{5,1},{8,10},{9,11},{10,... | collective-permute-start | bytes 294920 | tf_op jit(solution)/shard_map/ppermute | solution.py:257
  36.1 10.4 %collective-permute-start.8 = (bf16[2,3,128,128]{3,2,1,0:T(8,128)(2,1)S(1)}, bf16[2,3,128,128]{3,2,1,0:T(8,128)(2,1)S(1)}, u32[]{:S(2)}, u32[]{:S(2)}) collective-permute-start(bf16[2,3,128,128]{3,2,1,0:T(8,128)(2,1)S(1)} %get-tuple-element.48), channel_id=1, source_target_pairs={{0,8},{8,0},{1,9},{9,1},{2,10},{10,2},{3,11},{11,3},{4,12},{12,4},... | collective-permute-start | bytes 589832 | tf_op jit(solution)/shard_map/ppermute | solution.py:368
  36.7 6.2 %collective-permute-start.10 = (bf16[3,128,128]{2,1,0:T(8,128)(2,1)S(1)}, bf16[3,128,128]{2,1,0:T(8,128)(2,1)S(1)}, u32[]{:S(2)}, u32[]{:S(2)}) collective-permute-start(bf16[3,128,128]{2,1,0:T(8,128)(2,1)S(1)} %collective-permute-done.9.refs_4_.refs_1_), channel_id=1, source_target_pairs={{0,2},{1,3},{2,6},{3,7},{6,4},{7,5},{4,0},{5,1},{8,10},{9,11},{10,... | collective-permute-start | bytes 294920 | tf_op jit(solution)/shard_map/ppermute | solution.py:257
  39.0 6.6 %collective-permute-start.14 = (bf16[3,128,128]{2,1,0:T(8,128)(2,1)S(1)}, bf16[3,128,128]{2,1,0:T(8,128)(2,1)S(1)}, u32[]{:S(2)}, u32[]{:S(2)}) collective-permute-start(bf16[3,128,128]{2,1,0:T(8,128)(2,1)S(1)} %feature_chunk.5.refs_3_), channel_id=1, source_target_pairs={{0,2},{1,3},{2,6},{3,7},{6,4},{7,5},{4,0},{5,1},{8,10},{9,11},{10,... | collective-permute-start | bytes 294920 | tf_op jit(solution)/shard_map/ppermute | solution.py:257
  42.9 5.7 %collective-permute-start.11 = (bf16[3,128,128]{2,1,0:T(8,128)(2,1)S(1)}, bf16[3,128,128]{2,1,0:T(8,128)(2,1)S(1)}, u32[]{:S(2)}, u32[]{:S(2)}) collective-permute-start(bf16[3,128,128]{2,1,0:T(8,128)(2,1)S(1)} %collective-permute-done.10.refs_5_), channel_id=1, source_target_pairs={{0,2},{1,3},{2,6},{3,7},{6,4},{7,5},{4,0},{5,1},{8,10},{9,11},{10,... | collective-permute-start | bytes 294920 | tf_op jit(solution)/shard_map/ppermute | solution.py:257
  44.2 17.1 %copy-start.18 = (s32[3,2,2000]{2,1,0:T(2,128)}, s32[3,2,2000]{2,1,0:T(2,128)S(1)}, u32[]{:S(2)}) copy-start(s32[3,2,2000]{2,1,0:T(2,128)S(1)} %reshape.83) | copy-start | bytes 144004
  45.5 6.0 %collective-permute-start.15 = (bf16[3,128,128]{2,1,0:T(8,128)(2,1)S(1)}, bf16[3,128,128]{2,1,0:T(8,128)(2,1)S(1)}, u32[]{:S(2)}, u32[]{:S(2)}) collective-permute-start(bf16[3,128,128]{2,1,0:T(8,128)(2,1)S(1)} %collective-permute-done.14.refs_4_), channel_id=1, source_target_pairs={{0,2},{1,3},{2,6},{3,7},{6,4},{7,5},{4,0},{5,1},{8,10},{9,11},{10,... | collective-permute-start | bytes 294920 | tf_op jit(solution)/shard_map/ppermute | solution.py:257
  47.1 11.2 %collective-permute-start.13 = (bf16[2,2,3,128,128]{4,3,2,1,0:T(8,128)(2,1)S(1)}, bf16[2,2,3,128,128]{4,3,2,1,0:T(8,128)(2,1)S(1)}, u32[]{:S(2)}, u32[]{:S(2)}) collective-permute-start(bf16[2,2,3,128,128]{4,3,2,1,0:T(8,128)(2,1)S(1)} %join_tokens.5.refs_1_.refs_2_), channel_id=1, source_target_pairs={{0,1},{1,0},{2,3},{3,2},{4,5},{5,4},{6,7},{7,6},{8,9},{9,8},{10,11... | collective-permute-start | bytes 1179656 | tf_op jit(solution)/shard_map/ppermute | solution.py:247
  48.7 12.6 %copy-start.2 = (bf16[2,2,3,128,128]{4,3,2,1,0:T(8,128)(2,1)}, bf16[2,2,3,128,128]{4,3,2,1,0:T(8,128)(2,1)S(1)}, u32[]{:S(2)}) copy-start(bf16[2,2,3,128,128]{4,3,2,1,0:T(8,128)(2,1)S(1)} %collective-permute-done.4.refs_2_.refs_1_.refs_3_) | copy-start | bytes 1179652
  49.3 6.8 %collective-permute-start.12 = (bf16[2,3,128,128]{3,2,1,0:T(8,128)(2,1)S(1)}, bf16[2,3,128,128]{3,2,1,0:T(8,128)(2,1)S(1)}, u32[]{:S(2)}, u32[]{:S(2)}) collective-permute-start(bf16[2,3,128,128]{3,2,1,0:T(8,128)(2,1)S(1)} %get-tuple-element.50), channel_id=1, source_target_pairs={{0,8},{8,0},{1,9},{9,1},{2,10},{10,2},{3,11},{11,3},{4,12},{12,4},... | collective-permute-start | bytes 589832 | tf_op jit(solution)/shard_map/ppermute | solution.py:368
  51.6 29.3 %copy-start.4 = (s32[2,3,2000]{2,1,0:T(4,128)}, s32[2,3,2000]{2,1,0:T(4,128)S(1)}, u32[]{:S(2)}) copy-start(s32[2,3,2000]{2,1,0:T(4,128)S(1)} %get-tuple-element.100.refs_8_.refs_7_.refs_9_.refs_10_) | copy-start | bytes 144004
  51.6 6.4 %collective-permute-start.16 = (bf16[3,128,128]{2,1,0:T(8,128)(2,1)S(1)}, bf16[3,128,128]{2,1,0:T(8,128)(2,1)S(1)}, u32[]{:S(2)}, u32[]{:S(2)}) collective-permute-start(bf16[3,128,128]{2,1,0:T(8,128)(2,1)S(1)} %collective-permute-done.15.refs_5_), channel_id=1, source_target_pairs={{0,2},{1,3},{2,6},{3,7},{6,4},{7,5},{4,0},{5,1},{8,10},{9,11},{10,... | collective-permute-start | bytes 294920 | tf_op jit(solution)/shard_map/ppermute | solution.py:257
  56.7 13.2 %collective-permute-start.17 = (bf16[2,2,3,128,128]{4,3,2,1,0:T(8,128)(2,1)S(1)}, bf16[2,2,3,128,128]{4,3,2,1,0:T(8,128)(2,1)S(1)}, u32[]{:S(2)}, u32[]{:S(2)}) collective-permute-start(bf16[2,2,3,128,128]{4,3,2,1,0:T(8,128)(2,1)S(1)} %join_tokens.6.refs_1_), channel_id=1, source_target_pairs={{0,1},{1,0},{2,3},{3,2},{4,5},{5,4},{6,7},{7,6},{8,9},{9,8},{10,11... | collective-permute-start | bytes 1179656 | tf_op jit(solution)/shard_map/ppermute | solution.py:247
  59.2 8.5 %collective-permute-start.18 = (bf16[2,3,128,128]{3,2,1,0:T(8,128)(2,1)S(1)}, bf16[2,3,128,128]{3,2,1,0:T(8,128)(2,1)S(1)}, u32[]{:S(2)}, u32[]{:S(2)}) collective-permute-start(bf16[2,3,128,128]{3,2,1,0:T(8,128)(2,1)S(1)} %get-tuple-element.57), channel_id=1, source_target_pairs={{0,8},{8,0},{1,9},{9,1},{2,10},{10,2},{3,11},{11,3},{4,12},{12,4},... | collective-permute-start | bytes 589832 | tf_op jit(solution)/shard_map/ppermute | solution.py:368
  61.2 1.0 copy-start.3
  68.3 12.6 %collective-permute-start.19 = (bf16[2,2,3,128,128]{4,3,2,1,0:T(8,128)(2,1)S(1)}, bf16[2,2,3,128,128]{4,3,2,1,0:T(8,128)(2,1)S(1)}, u32[]{:S(2)}, u32[]{:S(2)}) collective-permute-start(bf16[2,2,3,128,128]{4,3,2,1,0:T(8,128)(2,1)S(1)} %join_tokens.7.refs_1_), channel_id=1, source_target_pairs={{0,1},{1,0},{2,3},{3,2},{4,5},{5,4},{6,7},{7,6},{8,9},{9,8},{10,11... | collective-permute-start | bytes 1179656 | tf_op jit(solution)/shard_map/ppermute | solution.py:247
  80.9 10.3 %copy-start.19 = (s32[3,2,2000]{2,1,0:T(2,128)S(1)}, s32[3,2,2000]{2,1,0:T(2,128)}, u32[]{:S(2)}) copy-start(s32[3,2,2000]{2,1,0:T(2,128)} %copy-done.18) | copy-start | bytes 144004
  86.4 20.6 %copy-start = (bf16[4,768,512]{2,1,0:T(8,128)(2,1)}, bf16[4,768,512]{2,1,0:T(8,128)(2,1)S(1)}, u32[]{:S(2)}) copy-start(bf16[4,768,512]{2,1,0:T(8,128)(2,1)S(1)} %get-tuple-element.64.refs_4_.refs_3_) | copy-start | bytes 9437188
  86.4 47.1 %collective-permute-start.26 = (bf16[4,768,512]{2,1,0:T(8,128)(2,1)S(1)}, bf16[4,768,512]{2,1,0:T(8,128)(2,1)}, u32[]{:S(2)}, u32[]{:S(2)}) collective-permute-start(bf16[4,768,512]{2,1,0:T(8,128)(2,1)S(1)} %get-tuple-element.64.refs_4_.refs_3_), channel_id=1, source_target_pairs={{0,16},{16,0},{1,17},{17,1},{2,18},{18,2},{3,19},{19,3},{4,20},{20... | collective-permute-start | bytes 9437192 | tf_op jit(solution)/shard_map/ppermute | solution.py:264
  86.6 4.6 %collective-permute-start.20 = (f32[2,4,2000]{2,1,0:T(4,128)S(1)}, f32[2,4,2000]{2,1,0:T(4,128)S(1)}, u32[]{:S(2)}, u32[]{:S(2)}) collective-permute-start(f32[2,4,2000]{2,1,0:T(4,128)S(1)} %pad_maximum_fusion.1), channel_id=1, source_target_pairs={{0,8},{8,0},{1,9},{9,1},{2,10},{10,2},{3,11},{11,3},{4,12},{12,4},... | collective-permute-start | bytes 192008 | tf_op jit(solution)/shard_map/ppermute | solution.py:389
  93.3 15.3 %collective-permute-start.22 = (f32[1]{0:T(128)}, f32[1]{0:T(128)}, u32[]{:S(2)}, u32[]{:S(2)}) collective-permute-start(f32[1]{0:T(128)} %bitcast.10), channel_id=1, source_target_pairs={{0,1},{1,0},{2,3},{3,2},{4,5},{5,4},{6,7},{7,6},{8,9},{9,8},{10,11... | collective-permute-start | bytes 20 | tf_op jit(solution)/shard_map/ppermute | solution.py:406
  95.4 0.8 copy-start.5
  96.2 13.1 %copy-start.20 = (f32[2,3,2000]{2,1,0:T(4,128)S(1)}, f32[2,3,2000]{2,1,0:T(4,128)}, u32[]{:S(2)}) copy-start(f32[2,3,2000]{2,1,0:T(4,128)} %get-tuple-element.99) | copy-start | bytes 144004
  107.0 23.7 %collective-permute-start.21 = (bf16[2,2,2,3,128,128]{5,4,3,2,1,0:T(8,128)(2,1)S(1)}, bf16[2,2,2,3,128,128]{5,4,3,2,1,0:T(8,128)(2,1)S(1)}, u32[]{:S(2)}, u32[]{:S(2)}) collective-permute-start(bf16[2,2,2,3,128,128]{5,4,3,2,1,0:T(8,128)(2,1)S(1)} %get-tuple-element.61), channel_id=1, source_target_pairs={{0,1},{1,0},{2,3},{3,2},{4,5},{5,4},{6,7},{7,6},{8,9},{9,8},{10,11... | collective-permute-start | bytes 2359304 | tf_op jit(solution)/shard_map/ppermute | solution.py:247
  109.4 11.9 %collective-permute-start.23 = (f32[2,7,2000]{2,1,0:T(8,128)S(1)}, f32[2,7,2000]{2,1,0:T(8,128)S(1)}, u32[]{:S(2)}, u32[]{:S(2)}) collective-permute-start(f32[2,7,2000]{2,1,0:T(8,128)S(1)} %pad_maximum_fusion.refs_1_), channel_id=1, source_target_pairs={{0,16},{16,0},{1,17},{17,1},{2,18},{18,2},{3,19},{19,3},{4,20},{20... | collective-permute-start | bytes 336008 | tf_op jit(solution)/shard_map/ppermute | solution.py:264
  120.8 12.7 %copy-start.16 = (f32[8,128]{1,0:T(8,128)}, f32[8,128]{1,0:T(8,128)S(1)}, u32[]{:S(2)}) copy-start(f32[8,128]{1,0:T(8,128)S(1)} %get-tuple-element.63.refs_2_) | copy-start | bytes 12292
  120.8 32.7 %collective-permute-start.28 = (bf16[2,2,2,3,128,128]{5,4,3,2,1,0:T(8,128)(2,1)}, bf16[2,2,2,3,128,128]{5,4,3,2,1,0:T(8,128)(2,1)S(1)}, u32[]{:S(2)}, u32[]{:S(2)}) collective-permute-start(bf16[2,2,2,3,128,128]{5,4,3,2,1,0:T(8,128)(2,1)} %get-tuple-element.70), channel_id=1, source_target_pairs={{0,1},{1,0},{2,3},{3,2},{4,5},{5,4},{6,7},{7,6},{8,9},{9,8},{10,11... | collective-permute-start | bytes 2359304 | tf_op jit(solution)/shard_map/ppermute | solution.py:247
  122.8 4.6 %collective-permute-start.24 = (f32[2,1]{0,1:T(1,128)S(1)}, f32[2,1]{0,1:T(1,128)S(1)}, u32[]{:S(2)}, u32[]{:S(2)}) collective-permute-start(f32[2,1]{0,1:T(1,128)S(1)} %constant_dynamic-slice_fusion.2), channel_id=1, source_target_pairs={{0,2},{1,3},{2,0},{3,1},{4,6},{5,7},{6,4},{7,5},{8,10},{9,11},{10,... | collective-permute-start | bytes 32 | tf_op jit(solution)/shard_map/ppermute | solution.py:406
  125.3 1.4 copy-start.1
  127.5 5.4 %collective-permute-start.25 = (f32[2,1]{0,1:T(1,128)S(1)}, f32[2,1]{0,1:T(1,128)S(1)}, u32[]{:S(2)}, u32[]{:S(2)}) collective-permute-start(f32[2,1]{0,1:T(1,128)S(1)} %fusion.14), channel_id=1, source_target_pairs={{0,4},{1,5},{2,6},{3,7},{4,0},{5,1},{6,2},{7,3},{8,12},{9,13},{10,... | collective-permute-start | bytes 32 | tf_op jit(solution)/shard_map/ppermute | solution.py:406
  132.1 1.5 copy-start.17
  132.1 20.0 %collective-permute-start.27 = (bf16[2,2,3,128,128]{4,3,2,1,0:T(8,128)(2,1)}, bf16[2,2,3,128,128]{4,3,2,1,0:T(8,128)(2,1)S(1)}, u32[]{:S(2)}, u32[]{:S(2)}) collective-permute-start(bf16[2,2,3,128,128]{4,3,2,1,0:T(8,128)(2,1)} %get-tuple-element.67), channel_id=1, source_target_pairs={{0,8},{8,0},{1,9},{9,1},{2,10},{10,2},{3,11},{11,3},{4,12},{12,4},... | collective-permute-start | bytes 1179656 | tf_op jit(solution)/shard_map/ppermute | solution.py:508
  133.5 18.6 %copy-start.7 = (s32[4]{0:T(128)S(1)}, s32[4]{0:T(128)}, u32[]{:S(2)}) copy-start(s32[4]{0:T(128)} %copy-done.6) | copy-start | bytes 52
  133.5 22.6 %copy-start.22 = (f32[2,1]{0,1:T(1,128)S(1)}, f32[2,1]{0,1:T(1,128)}, u32[]{:S(2)}) copy-start(f32[2,1]{0,1:T(1,128)} %fusion.8) | copy-start | bytes 28
  152.1 0.7 copy-start.15
  153.4 7.9 %copy-start.10 = (f32[8,128]{1,0:T(8,128)}, f32[8,128]{1,0:T(8,128)S(1)}, u32[]{:S(2)}) copy-start(f32[8,128]{1,0:T(8,128)S(1)} %get-tuple-element.68.refs_1_) | copy-start | bytes 12292
  154.2 0.6 copy-start.12
  154.8 16.9 %collective-permute-start.29 = (bf16[2,2,3,128,128]{4,3,2,1,0:T(8,128)(2,1)S(1)}, bf16[2,2,3,128,128]{4,3,2,1,0:T(8,128)(2,1)S(1)}, u32[]{:S(2)}, u32[]{:S(2)}) collective-permute-start(bf16[2,2,3,128,128]{4,3,2,1,0:T(8,128)(2,1)S(1)} %get-tuple-element.75), channel_id=1, source_target_pairs={{0,8},{8,0},{1,9},{9,1},{2,10},{10,2},{3,11},{11,3},{4,12},{12,4},... | collective-permute-start | bytes 1179656 | tf_op jit(solution)/shard_map/ppermute | solution.py:508
  155.9 18.3 %collective-permute-start.30 = (bf16[2,3,128,128]{3,2,1,0:T(8,128)(2,1)S(1)}, bf16[2,3,128,128]{3,2,1,0:T(8,128)(2,1)S(1)}, u32[]{:S(2)}, u32[]{:S(2)}) collective-permute-start(bf16[2,3,128,128]{3,2,1,0:T(8,128)(2,1)S(1)} %get-tuple-element.81), channel_id=1, source_target_pairs={{0,2},{1,3},{2,4},{3,5},{4,6},{5,7},{6,0},{7,1},{8,10},{9,11},{10,... | collective-permute-start | bytes 589832 | tf_op jit(solution)/shard_map/ppermute | solution.py:261
  156.7 39.2 %collective-permute-start.31 = (bf16[2,3,128,128]{3,2,1,0:T(8,128)(2,1)S(1)}, bf16[2,3,128,128]{3,2,1,0:T(8,128)(2,1)S(1)}, u32[]{:S(2)}, u32[]{:S(2)}) collective-permute-start(bf16[2,3,128,128]{3,2,1,0:T(8,128)(2,1)S(1)} %get-tuple-element.82), channel_id=1, source_target_pairs={{0,4},{1,5},{2,6},{3,7},{4,0},{5,1},{6,2},{7,3},{8,12},{9,13},{10,... | collective-permute-start | bytes 589832 | tf_op jit(solution)/shard_map/ppermute | solution.py:261
  158.6 37.3 %collective-permute-start.32 = (bf16[2,3,128,128]{3,2,1,0:T(8,128)(2,1)S(1)}, bf16[2,3,128,128]{3,2,1,0:T(8,128)(2,1)S(1)}, u32[]{:S(2)}, u32[]{:S(2)}) collective-permute-start(bf16[2,3,128,128]{3,2,1,0:T(8,128)(2,1)S(1)} %get-tuple-element.83), channel_id=1, source_target_pairs={{0,6},{1,7},{2,0},{3,1},{4,2},{5,3},{6,4},{7,5},{8,14},{9,15},{10,... | collective-permute-start | bytes 589832 | tf_op jit(solution)/shard_map/ppermute | solution.py:261
  161.3 10.3 %copy-start.8 = (s32[4]{0:T(128)S(1)}, s32[4]{0:T(128)}, u32[]{:S(2)}) copy-start(s32[4]{0:T(128)} %copy-done.6) | copy-start | bytes 52
  171.7 0.7 copy-start.14
  173.0 4.1 %copy-start.13 = (f32[8,128]{1,0:T(8,128)}, f32[8,128]{1,0:T(8,128)S(1)}, u32[]{:S(2)}) copy-start(f32[8,128]{1,0:T(8,128)S(1)} %get-tuple-element.76.refs_1_) | copy-start | bytes 12292
  173.0 22.8 %collective-permute-start.33 = (bf16[2,3,128,128]{3,2,1,0:T(8,128)(2,1)S(1)}, bf16[2,3,128,128]{3,2,1,0:T(8,128)(2,1)S(1)}, u32[]{:S(2)}, u32[]{:S(2)}) collective-permute-start(bf16[2,3,128,128]{3,2,1,0:T(8,128)(2,1)S(1)} %get-tuple-element.85), channel_id=1, source_target_pairs={{0,2},{1,3},{2,4},{3,5},{4,6},{5,7},{6,0},{7,1},{8,10},{9,11},{10,... | collective-permute-start | bytes 589832 | tf_op jit(solution)/shard_map/ppermute | solution.py:261
  173.1 22.8 %collective-permute-start.34 = (bf16[2,3,128,128]{3,2,1,0:T(8,128)(2,1)S(1)}, bf16[2,3,128,128]{3,2,1,0:T(8,128)(2,1)S(1)}, u32[]{:S(2)}, u32[]{:S(2)}) collective-permute-start(bf16[2,3,128,128]{3,2,1,0:T(8,128)(2,1)S(1)} %get-tuple-element.86), channel_id=1, source_target_pairs={{0,4},{1,5},{2,6},{3,7},{4,0},{5,1},{6,2},{7,3},{8,12},{9,13},{10,... | collective-permute-start | bytes 589832 | tf_op jit(solution)/shard_map/ppermute | solution.py:261
  174.2 21.7 %collective-permute-start.35 = (bf16[2,3,128,128]{3,2,1,0:T(8,128)(2,1)S(1)}, bf16[2,3,128,128]{3,2,1,0:T(8,128)(2,1)S(1)}, u32[]{:S(2)}, u32[]{:S(2)}) collective-permute-start(bf16[2,3,128,128]{3,2,1,0:T(8,128)(2,1)S(1)} %get-tuple-element.87), channel_id=1, source_target_pairs={{0,6},{1,7},{2,0},{3,1},{4,2},{5,3},{6,4},{7,5},{8,14},{9,15},{10,... | collective-permute-start | bytes 589832 | tf_op jit(solution)/shard_map/ppermute | solution.py:261
  177.1 18.8 %copy-start.9 = (s32[4]{0:T(128)S(1)}, s32[4]{0:T(128)}, u32[]{:S(2)}) copy-start(s32[4]{0:T(128)} %copy-done.6) | copy-start | bytes 52
  195.9 0.7 copy-start.11

commit v5 on v2

--- a/solution.py
+++ b/solution.py
@@ -9,6 +9,7 @@
 
 LANES = 128
 VMEM_BYTES = 48 * 1024 * 1024
+HEAD_VMEM_BYTES = 58 * 1024 * 1024
 
 
 def shift_perm(count, shift):
@@ -271,7 +272,6 @@
     index_spec = pl.BlockSpec(memory_space=pltpu.SMEM)
     vmem_spec = pl.BlockSpec(memory_space=pltpu.VMEM)
     any_spec = pl.BlockSpec(memory_space=pl.ANY)
-    params = pltpu.CompilerParams(vmem_limit_bytes=VMEM_BYTES)
 
     def cost(flops, transferred):
         return pl.CostEstimate(flops=int(flops), bytes_accessed=int(transferred), transcendentals=0)
@@ -284,7 +284,7 @@
         lengths = lengths + lax.ppermute(own_lengths, "seq", shift_perm(slots, s))
     validity = (owner_blocks < lengths[None]).astype(jnp.float32)
 
-    def run(kernel, name, operands, specs, shapes, out_specs=None, waits=(), flops=0, aliases={}, scratch=(), grid=()):
+    def run(kernel, name, operands, specs, shapes, out_specs=None, waits=(), flops=0, aliases={}, scratch=(), grid=(), limit=VMEM_BYTES):
         waits = [value for value in waits if value is not None]
         return pl.pallas_call(
             waiting(kernel, len(waits)),
@@ -294,7 +294,7 @@
             out_shape=shapes,
             scratch_shapes=list(scratch),
             input_output_aliases={1 + len(waits) + i: o for i, o in aliases.items()},
-            compiler_params=params,
+            compiler_params=pltpu.CompilerParams(vmem_limit_bytes=limit),
             cost_estimate=cost(flops, flops // 64),
             name=name,
         )(index, *waits, *operands)
@@ -445,6 +445,7 @@
             aliases={2 + groups: 0} if previous else {},
             scratch=[pltpu.VMEM((head_terms, groups * tokens), jnp.bfloat16)],
             grid=(count, strips),
+            limit=HEAD_VMEM_BYTES,
         )
         next_range += count
 

time: 191 us -> 194 us (1.016)
  local copies, waits for them, and re-layouts: 6.67 us -> 9.81 us
  waiting for transfers between devices: 21.7 us -> 18.8 us
  Pallas kernels: 103 us -> 105 us
    unnamed x18 -> x40, local copies, waits for them, and re-layouts: 3.37 us -> 6.51 us
  transfers between devices with their start and end apart: 37 -> 37, of which waited for: 10 -> 9; matrix products, arithmetic and copies ran while one was open for 3% -> 3% of each run, Pallas kernels for 49% -> 50%
where the time goes in v5:
time: 194 us; the launch traced here: 193 us
  Pallas kernels  105 us (54%)
  starting transfers between devices  51.7 us (27%)
  waiting for transfers between devices  18.8 us (10%)
  local copies, waits for them, and re-layouts  9.81 us (5%)
  other arithmetic  4.23 us (2%)
  between operations  3.75 us (2%)
    pallas_call x26, Pallas kernels, run(): pl.pallas_call(waiting(kernel, len(waits)), grid=grid, in_specs=[index_sp...  105 us
    ppermute x12, starting transfers between devices, around_ring(): return lax.ppermute(value, 'vocab', perm)  24.9 us
    ppermute x6, starting transfers between devices, across_z(): return lax.ppermute(value, 'vocab', perm)  8.86 us
    ppermute x4, waiting for transfers between devices, on_device(): lax.ppermute(sends[s - 1], 'seq', shift_perm(slots, -s))  7.46 us
    ppermute x6, starting transfers between devices, across_y(): return lax.ppermute(value, 'vocab', perm)  6.73 us
    unnamed x40, local copies, waits for them, and re-layouts  6.51 us
    ppermute x4, starting transfers between devices, on_device(): lax.ppermute(sends[s - 1], 'seq', shift_perm(slots, -s))  4.3 us
    ppermute x12, waiting for transfers between devices, around_ring(): return lax.ppermute(value, 'vocab', perm)  4.14 us
  transfers between devices with their start and end apart: 37, of which 9 were waited for; matrix products, arithmetic and copies ran while one was open for 3% of the time, Pallas kernels for 50%

profile of v5, /device:TPU:0, one launch (start us, length us, event | category | flops | bytes accessed | tf_op | source)
XLA Modules:
  0.0 193.1 jit_solution(873233578657243890)
XLA Ops:
  0.6 1.1 fusion.12
  1.7 3.1 %collective-permute-start.1 = (bf16[3,128,128]{2,1,0:T(8,128)(2,1)S(1)}, bf16[3,128,128]{2,1,0:T(8,128)(2,1)S(1)}, u32[]{:S(2)}, u32[]{:S(2)}) collective-permute-start(bf16[3,128,128]{2,1,0:T(8,128)(2,1)S(1)} %get-tuple-element.84.refs_1_), channel_id=1, source_target_pairs={{0,2},{1,3},{2,6},{3,7},{6,4},{7,5},{4,0},{5,1},{8,10},{9,11},{10,... | collective-permute-start | bytes 294920 | tf_op jit(solution)/shard_map/ppermute | solution.py:248
  4.9 3.7 %collective-permute-done.1.refs_2_.refs_1_ = bf16[3,128,128]{2,1,0:T(8,128)(2,1)S(1)} collective-permute-done((bf16[3,128,128]{2,1,0:T(8,128)(2,1)S(1)}, bf16[3,128,128]{2,1,0:T(8,128)(2,1)S(1)}, u32[]{:S(2)}, u32[]{:S(2)}) %collective-permute-start.1) | collective-permute-done | bytes 98336 | tf_op jit(solution)/shard_map/ppermute | solution.py:248
  9.1 1.0 collective-permute-start.6
  10.2 1.9 collective-permute-start.3
  12.1 3.7 %collective-permute-start.2 = (bf16[3,128,128]{2,1,0:T(8,128)(2,1)S(1)}, bf16[3,128,128]{2,1,0:T(8,128)(2,1)S(1)}, u32[]{:S(2)}, u32[]{:S(2)}) collective-permute-start(bf16[3,128,128]{2,1,0:T(8,128)(2,1)S(1)} %get-tuple-element.84.refs_1_), channel_id=1, source_target_pairs={{0,6},{1,7},{2,4},{3,5},{6,0},{7,1},{4,2},{5,3},{8,14},{9,15},{10,... | collective-permute-start | bytes 294920 | tf_op jit(solution)/shard_map/ppermute | solution.py:248
  16.8 3.5 %collective-permute-start.10 = (bf16[3,128,128]{2,1,0:T(8,128)(2,1)S(1)}, bf16[3,128,128]{2,1,0:T(8,128)(2,1)S(1)}, u32[]{:S(2)}, u32[]{:S(2)}) collective-permute-start(bf16[3,128,128]{2,1,0:T(8,128)(2,1)S(1)} %feature_chunk.4.refs_2_), channel_id=1, source_target_pairs={{0,2},{1,3},{2,6},{3,7},{6,4},{7,5},{4,0},{5,1},{8,10},{9,11},{10,... | collective-permute-start | bytes 294920 | tf_op jit(solution)/shard_map/ppermute | solution.py:248
  20.3 3.7 %collective-permute-start.7 = (bf16[3,128,128]{2,1,0:T(8,128)(2,1)S(1)}, bf16[3,128,128]{2,1,0:T(8,128)(2,1)S(1)}, u32[]{:S(2)}, u32[]{:S(2)}) collective-permute-start(bf16[3,128,128]{2,1,0:T(8,128)(2,1)S(1)} %collective-permute-done.6.refs_3_.refs_1_), channel_id=1, source_target_pairs={{0,2},{1,3},{2,6},{3,7},{6,4},{7,5},{4,0},{5,1},{8,10},{9,11},{10,... | collective-permute-start | bytes 294920 | tf_op jit(solution)/shard_map/ppermute | solution.py:248
  24.0 0.7 pick_halves.4
  24.7 1.3 collective-permute-start.4
  26.0 1.2 collective-permute-start.11
  27.2 3.4 %collective-permute-start.8 = (bf16[3,128,128]{2,1,0:T(8,128)(2,1)S(1)}, bf16[3,128,128]{2,1,0:T(8,128)(2,1)S(1)}, u32[]{:S(2)}, u32[]{:S(2)}) collective-permute-start(bf16[3,128,128]{2,1,0:T(8,128)(2,1)S(1)} %collective-permute-done.7.refs_4_), channel_id=1, source_target_pairs={{0,2},{1,3},{2,6},{3,7},{6,4},{7,5},{4,0},{5,1},{8,10},{9,11},{10,... | collective-permute-start | bytes 294920 | tf_op jit(solution)/shard_map/ppermute | solution.py:248
  30.6 0.8 convert_reduce_fusion
  31.4 1.2 collective-permute-start
  32.5 0.9 reshape.71
  34.0 2.2 %collective-permute-start.14 = (bf16[3,128,128]{2,1,0:T(8,128)(2,1)S(1)}, bf16[3,128,128]{2,1,0:T(8,128)(2,1)S(1)}, u32[]{:S(2)}, u32[]{:S(2)}) collective-permute-start(bf16[3,128,128]{2,1,0:T(8,128)(2,1)S(1)} %feature_chunk.5.refs_2_), channel_id=1, source_target_pairs={{0,2},{1,3},{2,6},{3,7},{6,4},{7,5},{4,0},{5,1},{8,10},{9,11},{10,... | collective-permute-start | bytes 294920 | tf_op jit(solution)/shard_map/ppermute | solution.py:248
  36.8 1.6 collective-permute-start.5
  38.4 0.7 pick_halves.5
  39.7 1.1 collective-permute-start.15
  40.8 4.0 %collective-permute-done.9.refs_2_ = bf16[2,3,128,128]{3,2,1,0:T(8,128)(2,1)S(1)} collective-permute-done((bf16[2,3,128,128]{3,2,1,0:T(8,128)(2,1)S(1)}, bf16[2,3,128,128]{3,2,1,0:T(8,128)(2,1)S(1)}, u32[]{:S(2)}, u32[]{:S(2)}) %collective-permute-start.9) | collective-permute-done | bytes 196640 | tf_op jit(solution)/shard_map/ppermute | solution.py:355
  45.4 0.7 pick_halves.6
  46.0 1.4 collective-permute-start.13
  48.3 3.5 %collective-permute-done.13.refs_3_ = bf16[2,3,128,128]{3,2,1,0:T(8,128)(2,1)S(1)} collective-permute-done((bf16[2,3,128,128]{3,2,1,0:T(8,128)(2,1)S(1)}, bf16[2,3,128,128]{3,2,1,0:T(8,128)(2,1)S(1)}, u32[]{:S(2)}, u32[]{:S(2)}) %collective-permute-start.13) | collective-permute-done | bytes 196640 | tf_op jit(solution)/shard_map/ppermute | solution.py:355
  52.4 0.9 collective-permute-start.17
  53.3 0.9 pick_halves.7
  54.2 1.1 collective-permute-start.19
  55.3 5.5 %pooled_logits.4 = (f32[2,3,2000]{2,1,0:T(4,128)S(1)}, bf16[4,768,512]{2,1,0:T(8,128)(2,1)S(1)}) custom-call(s32[4]{0:T(128)S(1)} %pad_add_fusion.refs_0_, bf16[2,3,128,128]{3,2,1,0:T(8,128)(2,1)S(1)} %get-tuple-element.46.refs_1_.refs_3_, bf16[2,2,3,128,128]{4,3,2,1,0:T(8,128)(2,1)S(1)} %join_tokens.4.refs_1_.refs_2_, ...), custom_call_target="tpu_custom_call" | custom-call | flops 3145728000 | bytes 49152000 | tf_op jit(solution)/shard_map/pooled_logits/pallas_call | solution.py:289
  61.3 1.6 collective-permute-start.20
  62.9 2.8 %collective-permute-done.17.refs_2_ = bf16[2,2,3,128,128]{4,3,2,1,0:T(8,128)(2,1)S(1)} collective-permute-done((bf16[2,2,3,128,128]{4,3,2,1,0:T(8,128)(2,1)S(1)}, bf16[2,2,3,128,128]{4,3,2,1,0:T(8,128)(2,1)S(1)}, u32[]{:S(2)}, u32[]{:S(2)}) %collective-permute-start.17) | collective-permute-done | bytes 393248 | tf_op jit(solution)/shard_map/ppermute | solution.py:238
  65.7 5.5 %pooled_logits.5 = (f32[2,3,2000]{2,1,0:T(4,128)S(1)}, bf16[4,768,512]{2,1,0:T(8,128)(2,1)S(1)}) custom-call(s32[4]{0:T(128)S(1)} %pad_add_fusion.refs_0_, f32[2,3,2000]{2,1,0:T(4,128)S(1)} %get-tuple-element.80.refs_1_, bf16[2,2,3,128,128]{4,3,2,1,0:T(8,128)(2,1)S(1)} %collective-permute-done.17.refs_2_, ...), custom_call_target="tpu_custom_call", output_to_operand_aliasing={{1}: (10, {})} | custom-call | flops 3145728000 | bytes 49152000 | tf_op jit(solution)/shard_map/pooled_logits/pallas_call | solution.py:289
  71.1 5.5 %pooled_logits.6 = (f32[2,3,2000]{2,1,0:T(4,128)S(1)}, bf16[4,768,512]{2,1,0:T(8,128)(2,1)S(1)}) custom-call(s32[4]{0:T(128)S(1)} %pad_add_fusion.refs_0_, bf16[2,2,3,128,128]{4,3,2,1,0:T(8,128)(2,1)S(1)} %join_tokens.6.refs_1_, bf16[2,2,3,128,128]{4,3,2,1,0:T(8,128)(2,1)S(1)} %collective-permute-done.17.refs_2_, ...), custom_call_target="tpu_custom_call", output_to_operand_aliasing={{1}: (8, {})} | custom-call | flops 3145728000 | bytes 49152000 | tf_op jit(solution)/shard_map/pooled_logits/pallas_call | solution.py:289
  76.6 5.5 %pooled_logits.7 = (f32[2,3,2000]{2,1,0:T(4,128)S(1)}, bf16[4,768,512]{2,1,0:T(8,128)(2,1)S(1)}) custom-call(s32[4]{0:T(128)S(1)} %pad_add_fusion.refs_0_, bf16[2,2,3,128,128]{4,3,2,1,0:T(8,128)(2,1)S(1)} %join_tokens.7.refs_1_, bf16[2,2,3,128,128]{4,3,2,1,0:T(8,128)(2,1)S(1)} %collective-permute-done.20.refs_2_, ...), custom_call_target="tpu_custom_call", output_to_operand_aliasing={{1}: (8, {})} | custom-call | flops 3145728000 | bytes 49152000 | tf_op jit(solution)/shard_map/pooled_logits/pallas_call | solution.py:289
  83.6 3.2 %collective-permute-done.21 = f32[2,3,2000]{2,1,0:T(4,128)S(1)} collective-permute-done((f32[2,3,2000]{2,1,0:T(4,128)S(1)}, f32[2,3,2000]{2,1,0:T(4,128)S(1)}, u32[]{:S(2)}, u32[]{:S(2)}) %collective-permute-start.21) | collective-permute-done | bytes 48032 | tf_op jit(solution)/shard_map/ppermute | solution.py:374
  88.9 2.9 %collective-permute-start.23 = (f32[1]{0:T(128)}, f32[1]{0:T(128)}, u32[]{:S(2)}, u32[]{:S(2)}) collective-permute-start(f32[1]{0:T(128)} %bitcast.11), channel_id=1, source_target_pairs={{0,1},{1,0},{2,3},{3,2},{4,5},{5,4},{6,7},{7,6},{8,9},{9,8},{10,11... | collective-permute-start | bytes 20 | tf_op jit(solution)/shard_map/ppermute | solution.py:388
  92.0 10.2 %hidden_terms.2 = (bf16[2,2,2,3,128,128]{5,4,3,2,1,0:T(8,128)(2,1)S(1)}, bf16[2,2,2,3,128,128]{5,4,3,2,1,0:T(8,128)(2,1)S(1)}) custom-call(s32[4]{0:T(128)S(1)} %pad_add_fusion.refs_0_, bf16[4000,2048]{1,0:T(8,128)(2,1)} %bitcast.57, bf16[4000,2048]{1,0:T(8,128)(2,1)} %bitcast.58, bf16[4000,2048]{1,0:T(8,128)(2,1)} %bitcast.59, bf16[4000,2048]{1,0:T(8,128)(2,1)} %bitcast.60, ...), custom_call_target="tpu_custom_call" | custom-call | flops 1572864000 | bytes 24576000 | tf_op jit(solution)/shard_map/hidden_terms/pallas_call | solution.py:289
  103.6 11.3 %hidden_terms.3 = (bf16[2,2,2,3,128,128]{5,4,3,2,1,0:T(8,128)(2,1)S(1)}, bf16[2,2,2,3,128,128]{5,4,3,2,1,0:T(8,128)(2,1)}) custom-call(s32[4]{0:T(128)S(1)} %pad_add_fusion.refs_0_, f32[2,7,2000]{2,1,0:T(8,128)S(1)} %pad_maximum_fusion.refs_1_, bf16[4000,2048]{1,0:T(8,128)(2,1)} %bitcast.65, bf16[4000,2048]{1,0:T(8,128)(2,1)} %bitcast.66, ...), custom_call_target="tpu_custom_call" | custom-call | flops 1572864000 | bytes 24576000 | tf_op jit(solution)/shard_map/hidden_terms/pallas_call | solution.py:289
  114.9 0.9 copy-done.2
  115.8 1.5 collective-permute-start.29
  117.9 0.7 pad_maximum_fusion.1
  118.7 1.3 turn_gradients.1.refs_6_.refs_5_
  120.0 1.4 copy-done.1
  121.4 0.7 pad_maximum_fusion.2
  122.3 0.8 collective-permute-start.26
  123.2 1.4 add_blocks.2
  124.6 0.8 copy-done.8
  125.3 0.7 collective-permute-start.28
  126.0 0.8 collective-permute-done.26
  127.4 18.6 %head_terms.3 = (f32[4000,2048]{1,0:T(8,128)}, f32[8,128]{1,0:T(8,128)}) custom-call(s32[4]{0:T(128)} %copy-done.12, bf16[2,2,3,128,128]{4,3,2,1,0:T(8,128)(2,1)} %copy-done.8, bf16[2,2,2,3,128,128]{5,4,3,2,1,0:T(8,128)(2,1)} %copy-done.2, f32[2]{0:T(128)} %bitcast.74, bf16[4,768,512]{2,1,0:T(8,128)(2,1)} %copy-done, ...), custom_call_target="tpu_custom_call" | custom-call | flops 2516582400 | bytes 39321600 | tf_op jit(solution)/shard_map/head_terms/pallas_call | solution.py:289
  146.7 0.7 sort_pieces.2
  147.4 0.7 add_blocks.3
  148.1 0.7 copy-done.6
  149.4 1.8 collective-permute-start.31
  151.9 2.1 %collective-permute-start.32 = (bf16[2,3,128,128]{3,2,1,0:T(8,128)(2,1)S(1)}, bf16[2,3,128,128]{3,2,1,0:T(8,128)(2,1)S(1)}, u32[]{:S(2)}, u32[]{:S(2)}) collective-permute-start(bf16[2,3,128,128]{3,2,1,0:T(8,128)(2,1)S(1)} %get-tuple-element.73), channel_id=1, source_target_pairs={{0,4},{1,5},{2,6},{3,7},{4,0},{5,1},{6,2},{7,3},{8,12},{9,13},{10,... | collective-permute-start | bytes 589832 | tf_op jit(solution)/shard_map/ppermute | solution.py:252
  154.0 1.1 collective-permute-start.33
  155.1 10.4 %head_terms.4 = (f32[4000,2048]{1,0:T(8,128)}, f32[8,128]{1,0:T(8,128)}) custom-call(s32[4]{0:T(128)} %copy-done.12, bf16[2,3,128,128]{3,2,1,0:T(8,128)(2,1)} %copy-done.4, bf16[2,2,3,128,128]{4,3,2,1,0:T(8,128)(2,1)} %copy-done.6, f32[2]{0:T(128)} %bitcast.75, bf16[4,768,512]{2,1,0:T(8,128)(2,1)} %copy-done, ...), custom_call_target="tpu_custom_call", output_to_operand_aliasing={{0}: (7, {})} | custom-call | flops 1258291200 | bytes 19660800 | tf_op jit(solution)/shard_map/head_terms/pallas_call | solution.py:289
  165.5 0.7 copy-done.17
  166.1 0.7 sort_pieces.3
  166.8 0.7 copy-done.10
  167.5 0.9 collective-permute-start.34
  168.4 0.8 collective-permute-start.35
  169.2 2.1 %collective-permute-start.36 = (bf16[2,3,128,128]{3,2,1,0:T(8,128)(2,1)S(1)}, bf16[2,3,128,128]{3,2,1,0:T(8,128)(2,1)S(1)}, u32[]{:S(2)}, u32[]{:S(2)}) collective-permute-start(bf16[2,3,128,128]{3,2,1,0:T(8,128)(2,1)S(1)} %get-tuple-element.77), channel_id=1, source_target_pairs={{0,6},{1,7},{2,0},{3,1},{4,2},{5,3},{6,4},{7,5},{8,14},{9,15},{10,... | collective-permute-start | bytes 589832 | tf_op jit(solution)/shard_map/ppermute | solution.py:252
  171.3 18.8 %head_terms.5 = (f32[4000,2048]{1,0:T(8,128)}, f32[8,128]{1,0:T(8,128)}) custom-call(s32[4]{0:T(128)} %copy-done.12, bf16[2,3,128,128]{3,2,1,0:T(8,128)(2,1)} %copy-done.10, f32[2]{0:T(128)} %bitcast.76, bf16[4,768,512]{2,1,0:T(8,128)(2,1)} %copy-done, bf16[4,768,512]{2,1,0:T(8,128)(2,1)} %collective-permute-done.27.refs_5_.refs_4_, ...), custom_call_target="tpu_custom_call", output_to_operand_aliasing={{0}: (6, {})} | custom-call | flops 2516582400 | bytes 39321600 | tf_op jit(solution)/shard_map/head_terms/pallas_call | solution.py:289
  190.2 0.7 copy-done.16
  190.9 2.2 %scale_hidden.1 = bf16[3,128,512]{2,1,0:T(8,128)(2,1)} custom-call(s32[4]{0:T(128)S(1)} %copy-done.15, f32[8,128]{1,0:T(8,128)S(1)} %copy-done.16, f32[1]{0:T(128)} %bitcast.20.refs_2_, bf16[2,3,128,128]{3,2,1,0:T(8,128)(2,1)S(1)} %copy-done.5, bf16[2,3,128,128]{3,2,1,0:T(8,128)(2,1)S(1)} %collective-permute-done.31.refs_4_, ...), custom_call_target="tpu_custom_call" | custom-call | tf_op jit(solution)/shard_map/scale_hidden/pallas_call | solution.py:289
  (97 shorter events, 12.0 us)
Async XLA Ops:
  1.7 6.9 %collective-permute-start.1 = (bf16[3,128,128]{2,1,0:T(8,128)(2,1)S(1)}, bf16[3,128,128]{2,1,0:T(8,128)(2,1)S(1)}, u32[]{:S(2)}, u32[]{:S(2)}) collective-permute-start(bf16[3,128,128]{2,1,0:T(8,128)(2,1)S(1)} %get-tuple-element.84.refs_1_), channel_id=1, source_target_pairs={{0,2},{1,3},{2,6},{3,7},{6,4},{7,5},{4,0},{5,1},{8,10},{9,11},{10,... | collective-permute-start | bytes 294920 | tf_op jit(solution)/shard_map/ppermute | solution.py:248
  4.9 118.3 %copy-start.12 = (s32[4]{0:T(128)}, s32[4]{0:T(128)S(1)}, u32[]{:S(2)}) copy-start(s32[4]{0:T(128)S(1)} %pad_add_fusion.refs_0_) | copy-start | bytes 52
  9.1 7.1 %collective-permute-start.6 = (bf16[3,128,128]{2,1,0:T(8,128)(2,1)S(1)}, bf16[3,128,128]{2,1,0:T(8,128)(2,1)S(1)}, u32[]{:S(2)}, u32[]{:S(2)}) collective-permute-start(bf16[3,128,128]{2,1,0:T(8,128)(2,1)S(1)} %feature_chunk.3.refs_2_), channel_id=1, source_target_pairs={{0,2},{1,3},{2,6},{3,7},{6,4},{7,5},{4,0},{5,1},{8,10},{9,11},{10,... | collective-permute-start | bytes 294920 | tf_op jit(solution)/shard_map/ppermute | solution.py:248
  10.2 13.8 %collective-permute-start.3 = (bf16[3,128,128]{2,1,0:T(8,128)(2,1)S(1)}, bf16[3,128,128]{2,1,0:T(8,128)(2,1)S(1)}, u32[]{:S(2)}, u32[]{:S(2)}) collective-permute-start(bf16[3,128,128]{2,1,0:T(8,128)(2,1)S(1)} %get-tuple-element.84.refs_1_), channel_id=1, source_target_pairs={{0,4},{1,5},{2,0},{3,1},{6,2},{7,3},{4,6},{5,7},{8,12},{9,13},{10,... | collective-permute-start | bytes 294920 | tf_op jit(solution)/shard_map/ppermute | solution.py:248
  12.1 11.9 %collective-permute-start.2 = (bf16[3,128,128]{2,1,0:T(8,128)(2,1)S(1)}, bf16[3,128,128]{2,1,0:T(8,128)(2,1)S(1)}, u32[]{:S(2)}, u32[]{:S(2)}) collective-permute-start(bf16[3,128,128]{2,1,0:T(8,128)(2,1)S(1)} %get-tuple-element.84.refs_1_), channel_id=1, source_target_pairs={{0,6},{1,7},{2,4},{3,5},{6,0},{7,1},{4,2},{5,3},{8,14},{9,15},{10,... | collective-permute-start | bytes 294920 | tf_op jit(solution)/shard_map/ppermute | solution.py:248
  16.8 9.2 %collective-permute-start.10 = (bf16[3,128,128]{2,1,0:T(8,128)(2,1)S(1)}, bf16[3,128,128]{2,1,0:T(8,128)(2,1)S(1)}, u32[]{:S(2)}, u32[]{:S(2)}) collective-permute-start(bf16[3,128,128]{2,1,0:T(8,128)(2,1)S(1)} %feature_chunk.4.refs_2_), channel_id=1, source_target_pairs={{0,2},{1,3},{2,6},{3,7},{6,4},{7,5},{4,0},{5,1},{8,10},{9,11},{10,... | collective-permute-start | bytes 294920 | tf_op jit(solution)/shard_map/ppermute | solution.py:248
  20.3 6.9 %collective-permute-start.7 = (bf16[3,128,128]{2,1,0:T(8,128)(2,1)S(1)}, bf16[3,128,128]{2,1,0:T(8,128)(2,1)S(1)}, u32[]{:S(2)}, u32[]{:S(2)}) collective-permute-start(bf16[3,128,128]{2,1,0:T(8,128)(2,1)S(1)} %collective-permute-done.6.refs_3_.refs_1_), channel_id=1, source_target_pairs={{0,2},{1,3},{2,6},{3,7},{6,4},{7,5},{4,0},{5,1},{8,10},{9,11},{10,... | collective-permute-start | bytes 294920 | tf_op jit(solution)/shard_map/ppermute | solution.py:248
  24.7 11.5 %collective-permute-start.4 = (bf16[2,3,128,128]{3,2,1,0:T(8,128)(2,1)S(1)}, bf16[2,3,128,128]{3,2,1,0:T(8,128)(2,1)S(1)}, u32[]{:S(2)}, u32[]{:S(2)}) collective-permute-start(bf16[2,3,128,128]{3,2,1,0:T(8,128)(2,1)S(1)} %get-tuple-element.41), channel_id=1, source_target_pairs={{0,8},{8,0},{1,9},{9,1},{2,10},{10,2},{3,11},{11,3},{4,12},{12,4},... | collective-permute-start | bytes 589832 | tf_op jit(solution)/shard_map/ppermute | solution.py:355
  26.0 13.7 %collective-permute-start.11 = (bf16[3,128,128]{2,1,0:T(8,128)(2,1)S(1)}, bf16[3,128,128]{2,1,0:T(8,128)(2,1)S(1)}, u32[]{:S(2)}, u32[]{:S(2)}) collective-permute-start(bf16[3,128,128]{2,1,0:T(8,128)(2,1)S(1)} %collective-permute-done.10.refs_3_.refs_1_), channel_id=1, source_target_pairs={{0,2},{1,3},{2,6},{3,7},{6,4},{7,5},{4,0},{5,1},{8,10},{9,11},{10,... | collective-permute-start | bytes 294920 | tf_op jit(solution)/shard_map/ppermute | solution.py:248
  27.2 11.2 %collective-permute-start.8 = (bf16[3,128,128]{2,1,0:T(8,128)(2,1)S(1)}, bf16[3,128,128]{2,1,0:T(8,128)(2,1)S(1)}, u32[]{:S(2)}, u32[]{:S(2)}) collective-permute-start(bf16[3,128,128]{2,1,0:T(8,128)(2,1)S(1)} %collective-permute-done.7.refs_4_), channel_id=1, source_target_pairs={{0,2},{1,3},{2,6},{3,7},{6,4},{7,5},{4,0},{5,1},{8,10},{9,11},{10,... | collective-permute-start | bytes 294920 | tf_op jit(solution)/shard_map/ppermute | solution.py:248
  31.4 16.0 %collective-permute-start = (s32[3,1]{0,1:T(1,128)S(1)}, s32[3,1]{0,1:T(1,128)S(1)}, u32[]{:S(2)}, u32[]{:S(2)}) collective-permute-start(s32[3,1]{0,1:T(1,128)S(1)} %bitcast.77), channel_id=1, source_target_pairs={{0,8},{8,0},{1,9},{9,1},{2,10},{10,2},{3,11},{11,3},{4,12},{12,4},... | collective-permute-start | bytes 44 | tf_op jit(solution)/shard_map/ppermute | solution.py:284
  34.0 5.7 %collective-permute-start.14 = (bf16[3,128,128]{2,1,0:T(8,128)(2,1)S(1)}, bf16[3,128,128]{2,1,0:T(8,128)(2,1)S(1)}, u32[]{:S(2)}, u32[]{:S(2)}) collective-permute-start(bf16[3,128,128]{2,1,0:T(8,128)(2,1)S(1)} %feature_chunk.5.refs_2_), channel_id=1, source_target_pairs={{0,2},{1,3},{2,6},{3,7},{6,4},{7,5},{4,0},{5,1},{8,10},{9,11},{10,... | collective-permute-start | bytes 294920 | tf_op jit(solution)/shard_map/ppermute | solution.py:248
  36.8 11.5 %collective-permute-start.5 = (bf16[2,2,3,128,128]{4,3,2,1,0:T(8,128)(2,1)S(1)}, bf16[2,2,3,128,128]{4,3,2,1,0:T(8,128)(2,1)S(1)}, u32[]{:S(2)}, u32[]{:S(2)}) collective-permute-start(bf16[2,2,3,128,128]{4,3,2,1,0:T(8,128)(2,1)S(1)} %join_tokens.4.refs_1_.refs_2_), channel_id=1, source_target_pairs={{0,1},{1,0},{2,3},{3,2},{4,5},{5,4},{6,7},{7,6},{8,9},{9,8},{10,11... | collective-permute-start | bytes 1179656 | tf_op jit(solution)/shard_map/ppermute | solution.py:238
  39.0 5.7 %collective-permute-start.9 = (bf16[2,3,128,128]{3,2,1,0:T(8,128)(2,1)S(1)}, bf16[2,3,128,128]{3,2,1,0:T(8,128)(2,1)S(1)}, u32[]{:S(2)}, u32[]{:S(2)}) collective-permute-start(bf16[2,3,128,128]{3,2,1,0:T(8,128)(2,1)S(1)} %get-tuple-element.43), channel_id=1, source_target_pairs={{0,8},{8,0},{1,9},{9,1},{2,10},{10,2},{3,11},{11,3},{4,12},{12,4},... | collective-permute-start | bytes 589832 | tf_op jit(solution)/shard_map/ppermute | solution.py:355
  39.6 5.7 %collective-permute-start.12 = (bf16[3,128,128]{2,1,0:T(8,128)(2,1)S(1)}, bf16[3,128,128]{2,1,0:T(8,128)(2,1)S(1)}, u32[]{:S(2)}, u32[]{:S(2)}) collective-permute-start(bf16[3,128,128]{2,1,0:T(8,128)(2,1)S(1)} %collective-permute-done.11.refs_4_), channel_id=1, source_target_pairs={{0,2},{1,3},{2,6},{3,7},{6,4},{7,5},{4,0},{5,1},{8,10},{9,11},{10,... | collective-permute-start | bytes 294920 | tf_op jit(solution)/shard_map/ppermute | solution.py:248
  39.7 7.7 %collective-permute-start.15 = (bf16[3,128,128]{2,1,0:T(8,128)(2,1)S(1)}, bf16[3,128,128]{2,1,0:T(8,128)(2,1)S(1)}, u32[]{:S(2)}, u32[]{:S(2)}) collective-permute-start(bf16[3,128,128]{2,1,0:T(8,128)(2,1)S(1)} %collective-permute-done.14.refs_3_), channel_id=1, source_target_pairs={{0,2},{1,3},{2,6},{3,7},{6,4},{7,5},{4,0},{5,1},{8,10},{9,11},{10,... | collective-permute-start | bytes 294920 | tf_op jit(solution)/shard_map/ppermute | solution.py:248
  46.0 5.7 %collective-permute-start.13 = (bf16[2,3,128,128]{3,2,1,0:T(8,128)(2,1)S(1)}, bf16[2,3,128,128]{3,2,1,0:T(8,128)(2,1)S(1)}, u32[]{:S(2)}, u32[]{:S(2)}) collective-permute-start(bf16[2,3,128,128]{3,2,1,0:T(8,128)(2,1)S(1)} %get-tuple-element.45), channel_id=1, source_target_pairs={{0,8},{8,0},{1,9},{9,1},{2,10},{10,2},{3,11},{11,3},{4,12},{12,4},... | collective-permute-start | bytes 589832 | tf_op jit(solution)/shard_map/ppermute | solution.py:355
  47.4 5.9 %collective-permute-start.16 = (bf16[3,128,128]{2,1,0:T(8,128)(2,1)S(1)}, bf16[3,128,128]{2,1,0:T(8,128)(2,1)S(1)}, u32[]{:S(2)}, u32[]{:S(2)}) collective-permute-start(bf16[3,128,128]{2,1,0:T(8,128)(2,1)S(1)} %collective-permute-done.15.refs_4_), channel_id=1, source_target_pairs={{0,2},{1,3},{2,6},{3,7},{6,4},{7,5},{4,0},{5,1},{8,10},{9,11},{10,... | collective-permute-start | bytes 294920 | tf_op jit(solution)/shard_map/ppermute | solution.py:248
  47.5 13.2 %collective-permute-start.18 = (bf16[2,2,3,128,128]{4,3,2,1,0:T(8,128)(2,1)S(1)}, bf16[2,2,3,128,128]{4,3,2,1,0:T(8,128)(2,1)S(1)}, u32[]{:S(2)}, u32[]{:S(2)}) collective-permute-start(bf16[2,2,3,128,128]{4,3,2,1,0:T(8,128)(2,1)S(1)} %join_tokens.5.refs_1_.refs_3_), channel_id=1, source_target_pairs={{0,1},{1,0},{2,3},{3,2},{4,5},{5,4},{6,7},{7,6},{8,9},{9,8},{10,11... | collective-permute-start | bytes 1179656 | tf_op jit(solution)/shard_map/ppermute | solution.py:238
  52.4 13.3 %collective-permute-start.17 = (bf16[2,2,3,128,128]{4,3,2,1,0:T(8,128)(2,1)S(1)}, bf16[2,2,3,128,128]{4,3,2,1,0:T(8,128)(2,1)S(1)}, u32[]{:S(2)}, u32[]{:S(2)}) collective-permute-start(bf16[2,2,3,128,128]{4,3,2,1,0:T(8,128)(2,1)S(1)} %join_tokens.6.refs_1_), channel_id=1, source_target_pairs={{0,1},{1,0},{2,3},{3,2},{4,5},{5,4},{6,7},{7,6},{8,9},{9,8},{10,11... | collective-permute-start | bytes 1179656 | tf_op jit(solution)/shard_map/ppermute | solution.py:238
  54.2 6.6 %collective-permute-start.19 = (bf16[2,3,128,128]{3,2,1,0:T(8,128)(2,1)S(1)}, bf16[2,3,128,128]{3,2,1,0:T(8,128)(2,1)S(1)}, u32[]{:S(2)}, u32[]{:S(2)}) collective-permute-start(bf16[2,3,128,128]{3,2,1,0:T(8,128)(2,1)S(1)} %get-tuple-element.52), channel_id=1, source_target_pairs={{0,8},{8,0},{1,9},{9,1},{2,10},{10,2},{3,11},{11,3},{4,12},{12,4},... | collective-permute-start | bytes 589832 | tf_op jit(solution)/shard_map/ppermute | solution.py:355
  61.3 15.3 %collective-permute-start.20 = (bf16[2,2,3,128,128]{4,3,2,1,0:T(8,128)(2,1)S(1)}, bf16[2,2,3,128,128]{4,3,2,1,0:T(8,128)(2,1)S(1)}, u32[]{:S(2)}, u32[]{:S(2)}) collective-permute-start(bf16[2,2,3,128,128]{4,3,2,1,0:T(8,128)(2,1)S(1)} %join_tokens.7.refs_1_), channel_id=1, source_target_pairs={{0,1},{1,0},{2,3},{3,2},{4,5},{5,4},{6,7},{7,6},{8,9},{9,8},{10,11... | collective-permute-start | bytes 1179656 | tf_op jit(solution)/shard_map/ppermute | solution.py:238
  82.1 20.0 %copy-start = (bf16[4,768,512]{2,1,0:T(8,128)(2,1)}, bf16[4,768,512]{2,1,0:T(8,128)(2,1)S(1)}, u32[]{:S(2)}) copy-start(bf16[4,768,512]{2,1,0:T(8,128)(2,1)S(1)} %get-tuple-element.59.refs_4_.refs_3_) | copy-start | bytes 9437188
  82.1 45.2 %collective-permute-start.27 = (bf16[4,768,512]{2,1,0:T(8,128)(2,1)S(1)}, bf16[4,768,512]{2,1,0:T(8,128)(2,1)}, u32[]{:S(2)}, u32[]{:S(2)}) collective-permute-start(bf16[4,768,512]{2,1,0:T(8,128)(2,1)S(1)} %get-tuple-element.59.refs_4_.refs_3_), channel_id=1, source_target_pairs={{0,16},{16,0},{1,17},{17,1},{2,18},{18,2},{3,19},{19,3},{4,20},{20... | collective-permute-start | bytes 9437192 | tf_op jit(solution)/shard_map/ppermute | solution.py:255
  82.3 4.6 %collective-permute-start.21 = (f32[2,3,2000]{2,1,0:T(4,128)S(1)}, f32[2,3,2000]{2,1,0:T(4,128)S(1)}, u32[]{:S(2)}, u32[]{:S(2)}) collective-permute-start(f32[2,3,2000]{2,1,0:T(4,128)S(1)} %add_add_fusion), channel_id=1, source_target_pairs={{0,8},{8,0},{1,9},{9,1},{2,10},{10,2},{3,11},{11,3},{4,12},{12,4},... | collective-permute-start | bytes 144008 | tf_op jit(solution)/shard_map/ppermute | solution.py:374
  88.9 13.8 %collective-permute-start.23 = (f32[1]{0:T(128)}, f32[1]{0:T(128)}, u32[]{:S(2)}, u32[]{:S(2)}) collective-permute-start(f32[1]{0:T(128)} %bitcast.11), channel_id=1, source_target_pairs={{0,1},{1,0},{2,3},{3,2},{4,5},{5,4},{6,7},{7,6},{8,9},{9,8},{10,11... | collective-permute-start | bytes 20 | tf_op jit(solution)/shard_map/ppermute | solution.py:388
  102.2 21.0 %collective-permute-start.22 = (bf16[2,2,2,3,128,128]{5,4,3,2,1,0:T(8,128)(2,1)S(1)}, bf16[2,2,2,3,128,128]{5,4,3,2,1,0:T(8,128)(2,1)S(1)}, u32[]{:S(2)}, u32[]{:S(2)}) collective-permute-start(bf16[2,2,2,3,128,128]{5,4,3,2,1,0:T(8,128)(2,1)S(1)} %get-tuple-element.56), channel_id=1, source_target_pairs={{0,1},{1,0},{2,3},{3,2},{4,5},{5,4},{6,7},{7,6},{8,9},{9,8},{10,11... | collective-permute-start | bytes 2359304 | tf_op jit(solution)/shard_map/ppermute | solution.py:238
  103.5 13.8 %collective-permute-start.24 = (f32[2,7,2000]{2,1,0:T(8,128)S(1)}, f32[2,7,2000]{2,1,0:T(8,128)S(1)}, u32[]{:S(2)}, u32[]{:S(2)}) collective-permute-start(f32[2,7,2000]{2,1,0:T(8,128)S(1)} %pad_maximum_fusion.refs_1_), channel_id=1, source_target_pairs={{0,16},{16,0},{1,17},{17,1},{2,18},{18,2},{3,19},{19,3},{4,20},{20... | collective-permute-start | bytes 336008 | tf_op jit(solution)/shard_map/ppermute | solution.py:255
  114.9 0.9 copy-start.2
  115.8 31.6 %collective-permute-start.29 = (bf16[2,2,2,3,128,128]{5,4,3,2,1,0:T(8,128)(2,1)}, bf16[2,2,2,3,128,128]{5,4,3,2,1,0:T(8,128)(2,1)S(1)}, u32[]{:S(2)}, u32[]{:S(2)}) collective-permute-start(bf16[2,2,2,3,128,128]{5,4,3,2,1,0:T(8,128)(2,1)} %get-tuple-element.63), channel_id=1, source_target_pairs={{0,1},{1,0},{2,3},{3,2},{4,5},{5,4},{6,7},{7,6},{8,9},{9,8},{10,11... | collective-permute-start | bytes 2359304 | tf_op jit(solution)/shard_map/ppermute | solution.py:238
  118.7 3.5 %collective-permute-start.25 = (f32[2,1]{0,1:T(1,128)S(1)}, f32[2,1]{0,1:T(1,128)S(1)}, u32[]{:S(2)}, u32[]{:S(2)}) collective-permute-start(f32[2,1]{0,1:T(1,128)S(1)} %constant_dynamic-slice_fusion.2), channel_id=1, source_target_pairs={{0,2},{1,3},{2,0},{3,1},{4,6},{5,7},{6,4},{7,5},{8,10},{9,11},{10,... | collective-permute-start | bytes 32 | tf_op jit(solution)/shard_map/ppermute | solution.py:388
  120.0 1.4 copy-start.1
  122.3 4.4 %collective-permute-start.26 = (f32[2,1]{0,1:T(1,128)S(1)}, f32[2,1]{0,1:T(1,128)S(1)}, u32[]{:S(2)}, u32[]{:S(2)}) collective-permute-start(f32[2,1]{0,1:T(1,128)S(1)} %fusion.14), channel_id=1, source_target_pairs={{0,4},{1,5},{2,6},{3,7},{4,0},{5,1},{6,2},{7,3},{8,12},{9,13},{10,... | collective-permute-start | bytes 32 | tf_op jit(solution)/shard_map/ppermute | solution.py:388
  124.5 0.8 copy-start.8
  125.3 20.7 %collective-permute-start.28 = (bf16[2,2,3,128,128]{4,3,2,1,0:T(8,128)(2,1)}, bf16[2,2,3,128,128]{4,3,2,1,0:T(8,128)(2,1)S(1)}, u32[]{:S(2)}, u32[]{:S(2)}) collective-permute-start(bf16[2,2,3,128,128]{4,3,2,1,0:T(8,128)(2,1)} %get-tuple-element.61), channel_id=1, source_target_pairs={{0,8},{8,0},{1,9},{9,1},{2,10},{10,2},{3,11},{11,3},{4,12},{12,4},... | collective-permute-start | bytes 1179656 | tf_op jit(solution)/shard_map/ppermute | solution.py:486
  127.4 18.6 %copy-start.9 = (bf16[2,2,3,128,128]{4,3,2,1,0:T(8,128)(2,1)S(1)}, bf16[2,2,3,128,128]{4,3,2,1,0:T(8,128)(2,1)}, u32[]{:S(2)}) copy-start(bf16[2,2,3,128,128]{4,3,2,1,0:T(8,128)(2,1)} %copy-done.8) | copy-start | bytes 1179652
  127.4 18.6 %copy-start.13 = (s32[4]{0:T(128)S(1)}, s32[4]{0:T(128)}, u32[]{:S(2)}) copy-start(s32[4]{0:T(128)} %copy-done.12) | copy-start | bytes 52
  127.4 20.0 %copy-start.3 = (bf16[2,2,2,3,128,128]{5,4,3,2,1,0:T(8,128)(2,1)S(1)}, bf16[2,2,2,3,128,128]{5,4,3,2,1,0:T(8,128)(2,1)}, u32[]{:S(2)}) copy-start(bf16[2,2,2,3,128,128]{5,4,3,2,1,0:T(8,128)(2,1)} %copy-done.2) | copy-start | bytes 2359300
  127.4 23.9 %copy-start.19 = (f32[2,1]{0,1:T(1,128)S(1)}, f32[2,1]{0,1:T(1,128)}, u32[]{:S(2)}) copy-start(f32[2,1]{0,1:T(1,128)} %fusion.8) | copy-start | bytes 28
  146.0 0.7 copy-start.18
  147.4 7.7 %copy-start.4 = (bf16[2,3,128,128]{3,2,1,0:T(8,128)(2,1)}, bf16[2,3,128,128]{3,2,1,0:T(8,128)(2,1)S(1)}, u32[]{:S(2)}) copy-start(bf16[2,3,128,128]{3,2,1,0:T(8,128)(2,1)S(1)} %get-tuple-element.62.refs_1_.refs_3_) | copy-start | bytes 589828
  148.1 0.7 copy-start.6
  148.9 16.6 %collective-permute-start.30 = (bf16[2,2,3,128,128]{4,3,2,1,0:T(8,128)(2,1)S(1)}, bf16[2,2,3,128,128]{4,3,2,1,0:T(8,128)(2,1)S(1)}, u32[]{:S(2)}, u32[]{:S(2)}) collective-permute-start(bf16[2,2,3,128,128]{4,3,2,1,0:T(8,128)(2,1)S(1)} %get-tuple-element.67), channel_id=1, source_target_pairs={{0,8},{8,0},{1,9},{9,1},{2,10},{10,2},{3,11},{11,3},{4,12},{12,4},... | collective-permute-start | bytes 1179656 | tf_op jit(solution)/shard_map/ppermute | solution.py:486
  149.4 19.8 %collective-permute-start.31 = (bf16[2,3,128,128]{3,2,1,0:T(8,128)(2,1)S(1)}, bf16[2,3,128,128]{3,2,1,0:T(8,128)(2,1)S(1)}, u32[]{:S(2)}, u32[]{:S(2)}) collective-permute-start(bf16[2,3,128,128]{3,2,1,0:T(8,128)(2,1)S(1)} %get-tuple-element.72), channel_id=1, source_target_pairs={{0,2},{1,3},{2,4},{3,5},{4,6},{5,7},{6,0},{7,1},{8,10},{9,11},{10,... | collective-permute-start | bytes 589832 | tf_op jit(solution)/shard_map/ppermute | solution.py:252
  151.9 38.2 %collective-permute-start.32 = (bf16[2,3,128,128]{3,2,1,0:T(8,128)(2,1)S(1)}, bf16[2,3,128,128]{3,2,1,0:T(8,128)(2,1)S(1)}, u32[]{:S(2)}, u32[]{:S(2)}) collective-permute-start(bf16[2,3,128,128]{3,2,1,0:T(8,128)(2,1)S(1)} %get-tuple-element.73), channel_id=1, source_target_pairs={{0,4},{1,5},{2,6},{3,7},{4,0},{5,1},{6,2},{7,3},{8,12},{9,13},{10,... | collective-permute-start | bytes 589832 | tf_op jit(solution)/shard_map/ppermute | solution.py:252
  154.0 36.1 %collective-permute-start.33 = (bf16[2,3,128,128]{3,2,1,0:T(8,128)(2,1)S(1)}, bf16[2,3,128,128]{3,2,1,0:T(8,128)(2,1)S(1)}, u32[]{:S(2)}, u32[]{:S(2)}) collective-permute-start(bf16[2,3,128,128]{3,2,1,0:T(8,128)(2,1)S(1)} %get-tuple-element.74), channel_id=1, source_target_pairs={{0,6},{1,7},{2,0},{3,1},{4,2},{5,3},{6,4},{7,5},{8,14},{9,15},{10,... | collective-permute-start | bytes 589832 | tf_op jit(solution)/shard_map/ppermute | solution.py:252
  155.1 10.4 %copy-start.7 = (bf16[2,2,3,128,128]{4,3,2,1,0:T(8,128)(2,1)S(1)}, bf16[2,2,3,128,128]{4,3,2,1,0:T(8,128)(2,1)}, u32[]{:S(2)}) copy-start(bf16[2,2,3,128,128]{4,3,2,1,0:T(8,128)(2,1)} %copy-done.6) | copy-start | bytes 1179652
  155.1 10.4 %copy-start.14 = (s32[4]{0:T(128)S(1)}, s32[4]{0:T(128)}, u32[]{:S(2)}) copy-start(s32[4]{0:T(128)} %copy-done.12) | copy-start | bytes 52
  165.4 0.7 copy-start.17
  166.8 0.7 copy-start.10
  167.5 22.6 %collective-permute-start.34 = (bf16[2,3,128,128]{3,2,1,0:T(8,128)(2,1)S(1)}, bf16[2,3,128,128]{3,2,1,0:T(8,128)(2,1)S(1)}, u32[]{:S(2)}, u32[]{:S(2)}) collective-permute-start(bf16[2,3,128,128]{3,2,1,0:T(8,128)(2,1)S(1)} %get-tuple-element.75), channel_id=1, source_target_pairs={{0,2},{1,3},{2,4},{3,5},{4,6},{5,7},{6,0},{7,1},{8,10},{9,11},{10,... | collective-permute-start | bytes 589832 | tf_op jit(solution)/shard_map/ppermute | solution.py:252
  168.4 21.7 %collective-permute-start.35 = (bf16[2,3,128,128]{3,2,1,0:T(8,128)(2,1)S(1)}, bf16[2,3,128,128]{3,2,1,0:T(8,128)(2,1)S(1)}, u32[]{:S(2)}, u32[]{:S(2)}) collective-permute-start(bf16[2,3,128,128]{3,2,1,0:T(8,128)(2,1)S(1)} %get-tuple-element.76), channel_id=1, source_target_pairs={{0,4},{1,5},{2,6},{3,7},{4,0},{5,1},{6,2},{7,3},{8,12},{9,13},{10,... | collective-permute-start | bytes 589832 | tf_op jit(solution)/shard_map/ppermute | solution.py:252
  169.2 20.9 %collective-permute-start.36 = (bf16[2,3,128,128]{3,2,1,0:T(8,128)(2,1)S(1)}, bf16[2,3,128,128]{3,2,1,0:T(8,128)(2,1)S(1)}, u32[]{:S(2)}, u32[]{:S(2)}) collective-permute-start(bf16[2,3,128,128]{3,2,1,0:T(8,128)(2,1)S(1)} %get-tuple-element.77), channel_id=1, source_target_pairs={{0,6},{1,7},{2,0},{3,1},{4,2},{5,3},{6,4},{7,5},{8,14},{9,15},{10,... | collective-permute-start | bytes 589832 | tf_op jit(solution)/shard_map/ppermute | solution.py:252
  171.3 18.8 %copy-start.5 = (bf16[2,3,128,128]{3,2,1,0:T(8,128)(2,1)S(1)}, bf16[2,3,128,128]{3,2,1,0:T(8,128)(2,1)}, u32[]{:S(2)}) copy-start(bf16[2,3,128,128]{3,2,1,0:T(8,128)(2,1)} %copy-done.4) | copy-start | bytes 589828
  171.3 18.8 %copy-start.11 = (bf16[2,3,128,128]{3,2,1,0:T(8,128)(2,1)S(1)}, bf16[2,3,128,128]{3,2,1,0:T(8,128)(2,1)}, u32[]{:S(2)}) copy-start(bf16[2,3,128,128]{3,2,1,0:T(8,128)(2,1)} %copy-done.10) | copy-start | bytes 589828
  171.3 18.8 %copy-start.15 = (s32[4]{0:T(128)S(1)}, s32[4]{0:T(128)}, u32[]{:S(2)}) copy-start(s32[4]{0:T(128)} %copy-done.12) | copy-start | bytes 52
  190.2 0.7 copy-start.16
